TPU v7x, 256 devices: a whole 4x4x8 slice. The times are simulated.
256 devices in a mesh: section: 2 (over y_lo), azim: 32 (over x, z), axial: 4 (over y_hi, core).
Axes of the slice: x: 4, y: 4 (y_hi: 2, y_lo: 2; y = y_hi * 2 + y_lo), z: 8, core: 2. Of those that a mesh axis runs over, the one named last changes fastest.
Arguments:
- magnetic_vector_field: float32 [3, 32, 512, 512], P(None, 'azim', 'section', 'axial'), may hold values from -3 to 3
- imposed_current_density: float32 [3, 32, 512, 512], P(None, 'azim', 'section', 'axial'), may hold values from -6 to 6
- fixed_material_map: int32 [32, 512, 512], P('azim', 'section', 'axial'), may hold values from 0 to 7
- spinning_material_map: int32 [32, 128], replicated, may hold values from 0 to 7
- slab_slide_offsets: int32 [512], P('axial'), may hold values from 0 to 31, as said below
- inverse_permeability: float32 [8], replicated, may hold values from 0.1 to 1
- electric_conductance: float32 [8], replicated, may hold values from 0.05 to 0.5
- core_dissipation_coefficient: float32 [8], replicated, may hold values from 0.2 to 2
- inplane_thermal_conductance: float32 [8], replicated, may hold values from 1 to 4
- through_plane_conductance: float32 [8], replicated, may hold values from 0.1 to 0.5
- thermal_storage: float32 [8], replicated, may hold values from 0.05 to 0.3
- prior_thermal_state: float32 [32, 512, 512], P(None, ('section', 'azim'), 'axial'), may hold values from -6 to 6
- goal_sensitivity: float32 [32, 512, 512], P(None, ('section', 'azim'), 'axial'), may hold values from -16 to 16
Outputs:
- magnetic_misfit: float32 [3, 32, 512, 512], P(None, 'azim', 'section', 'axial')
- dual_magnetic_rhs: float32 [3, 32, 512, 512], P(None, 'azim', 'section', 'axial')
- thermal_state: float32 [32, 512, 512], P('azim', 'section', 'axial')
Inputs may be any that keep to these rules, and one draw needn't show every extreme that they name: `slab_slide_offsets`: the smallest and the largest offset each occur at some layer.
All inputs are finite; a program needn't handle non-finite values.
Results may differ from a plain program's by a relative error of at most 0.00002.
Values sent between devices are 32-bit elements; how exact they have to be, the bound alone decides.
No kernel may reach another device: no remote copies, remote signals or barrier semaphores. Data moves between devices by JAX's collectives and lax.ppermute only.
A program may use at most 64 MiB of HBM per device.

v0:
```python
import jax
import jax.numpy as jnp
from jax import lax
from jax.sharding import PartitionSpec as P

NREG = 8
SWEEPS = 4


def padded_2(block, sides, width, periodic):
    for axis, dim in sides:
        count = lax.axis_size(axis)
        forward = [(i, i + 1) for i in range(count - 1)]
        if periodic:
            forward.append((count - 1, 0))
        backward = [(target, source) for source, target in forward]
        low = lax.ppermute(
            lax.slice_in_dim(block, block.shape[dim] - width, None, axis=dim), axis, forward
        )
        high = lax.ppermute(lax.slice_in_dim(block, 0, width, axis=dim), axis, backward)
        block = jnp.concatenate([low, block, high], axis=dim)
    return block


def region_map(
    fixed_material_map,
    spinning_material_map,
    slab_slide_offsets,
    azim_cells,
    radial_cells,
    azim_total,
):
    shifted = jnp.mod(azim_cells[:, None] - slab_slide_offsets[None, :], azim_total)
    rotor_rows = jnp.transpose(spinning_material_map[shifted], (0, 2, 1))
    extra = fixed_material_map.shape[1] - rotor_rows.shape[1]
    rotor_rows = jnp.pad(rotor_rows, ((0, 0), (0, extra), (0, 0)))
    inside = (radial_cells < spinning_material_map.shape[1])[None, :, None]
    return jnp.where(inside, rotor_rows, fixed_material_map)


def lookup(regions, materials):
    results = [jnp.zeros(regions.shape, jnp.float32) for material in materials]
    for region in range(NREG):
        matches = regions == region
        results = [
            jnp.where(matches, material[region], result)
            for material, result in zip(materials, results)
        ]
    return results


def forward_diff(values, axis_dim):
    difference = jnp.diff(values, axis=axis_dim)
    window = [slice(0, -1), slice(0, -1), slice(0, -1)]
    window[axis_dim] = slice(None)
    return difference[tuple(window)]


def backward_diff(values, axis_dim):
    difference = -jnp.diff(values, axis=axis_dim)
    window = [slice(1, None), slice(1, None), slice(1, None)]
    window[axis_dim] = slice(None)
    return difference[tuple(window)]


def em_terms(padded):
    azim_part, radial_part, axial_part, reluct_pad = (padded[0], padded[1], padded[2], padded[3])
    flux_azim = forward_diff(axial_part, 1) - forward_diff(radial_part, 2)
    flux_radial = forward_diff(azim_part, 2) - forward_diff(axial_part, 0)
    flux_axial = forward_diff(radial_part, 0) - forward_diff(azim_part, 1)
    reluct_cell = reluct_pad[:-1, :-1, :-1]
    field_azim = reluct_cell * flux_azim
    field_radial = reluct_cell * flux_radial
    field_axial = reluct_cell * flux_axial
    curl_azim = backward_diff(field_radial, 2) - backward_diff(field_axial, 1)
    curl_radial = backward_diff(field_axial, 0) - backward_diff(field_azim, 2)
    curl_axial = backward_diff(field_azim, 1) - backward_diff(field_radial, 0)
    curl_term = jnp.stack([curl_azim, curl_radial, curl_axial])
    flux = jnp.stack([flux_azim, flux_radial, flux_axial])[:, 1:, 1:, 1:]
    return (curl_term, flux)


def relax(padded, local_thermal_storage, right_hand_sides):
    interior = padded[:, :, 1:-1, 1:-1]
    repeat_relaxation_passes = interior[:2]
    plane_cell = interior[2]
    axial_cell = interior[3]
    faces = [
        (
            jnp.roll(repeat_relaxation_passes, -1, axis=1),
            jnp.roll(plane_cell, -1, axis=0),
            plane_cell,
        ),
        (
            jnp.roll(repeat_relaxation_passes, 1, axis=1),
            jnp.roll(plane_cell, 1, axis=0),
            plane_cell,
        ),
        (padded[:2, :, 2:, 1:-1], padded[2, :, 2:, 1:-1], plane_cell),
        (padded[:2, :, :-2, 1:-1], padded[2, :, :-2, 1:-1], plane_cell),
        (padded[:2, :, 1:-1, 2:], padded[3, :, 1:-1, 2:], axial_cell),
        (padded[:2, :, 1:-1, :-2], padded[3, :, 1:-1, :-2], axial_cell),
    ]
    weight_sum = jnp.zeros(plane_cell.shape, jnp.float32)
    inflow = jnp.zeros(repeat_relaxation_passes.shape, jnp.float32)
    for neighbour, beside, own in faces:
        weight = 0.5 * (own + beside)
        weight_sum = weight_sum + weight
        inflow = inflow + weight * neighbour
    return (right_hand_sides + inflow) / (local_thermal_storage + weight_sum)


def azim_rims(stacked):
    return padded_2(stacked, (("azim", 1),), 1, True)


def depth_rims(stacked):
    return padded_2(stacked, (("section", 2), ("axial", 3)), 1, False)


def relay_out(stacked):
    return lax.all_to_all(stacked, "azim", split_axis=2, concat_axis=1, tiled=True)


def heat_rims(stacked):
    return padded_2(stacked, ((("section", "azim"), 2), ("axial", 3)), 1, False)


def body(
    magnetic_vector_field,
    imposed_current_density,
    fixed_material_map,
    spinning_material_map,
    slab_slide_offsets,
    inverse_permeability,
    electric_conductance,
    core_dissipation_coefficient,
    inplane_thermal_conductance,
    through_plane_conductance,
    thermal_storage,
    prior_thermal_state,
    goal_sensitivity,
):
    azim_count, radial_count, axial_count = fixed_material_map.shape
    azim_total = azim_count * lax.axis_size("azim")
    azim_cells = lax.axis_index("azim") * azim_count + jnp.arange(azim_count, dtype=jnp.int32)
    radial_cells = lax.axis_index("section") * radial_count + jnp.arange(
        radial_count, dtype=jnp.int32
    )
    regions = region_map(
        fixed_material_map,
        spinning_material_map,
        slab_slide_offsets,
        azim_cells,
        radial_cells,
        azim_total,
    )
    reluct_cell, eddy_cell, loss_cell = lookup(
        regions, (inverse_permeability, electric_conductance, core_dissipation_coefficient)
    )
    stacked = jnp.concatenate([magnetic_vector_field, reluct_cell[None]], axis=0)
    padded = depth_rims(azim_rims(stacked))
    curl_term, flux = em_terms(padded)
    magnetic_misfit = curl_term + eddy_cell * magnetic_vector_field - imposed_current_density
    thermal_rhs = loss_cell * jnp.sum(flux * flux, axis=0)
    plane_cell, axial_cell, local_thermal_storage = lookup(
        regions, (inplane_thermal_conductance, through_plane_conductance, thermal_storage)
    )
    relayed = relay_out(jnp.stack([thermal_rhs, plane_cell, axial_cell, local_thermal_storage]))
    thermal_exchange = relayed[0]
    plane_heat = relayed[1]
    axial_heat = relayed[2]
    storage_coefficient = relayed[3]
    right_hand_sides = jnp.stack(
        [storage_coefficient * prior_thermal_state + thermal_exchange, goal_sensitivity]
    )
    repeat_relaxation_passes = jnp.stack([prior_thermal_state, jnp.zeros_like(prior_thermal_state)])
    for iteration in range(SWEEPS):
        combined = jnp.concatenate(
            [repeat_relaxation_passes, plane_heat[None], axial_heat[None]], axis=0
        )
        repeat_relaxation_passes = relax(heat_rims(combined), storage_coefficient, right_hand_sides)
    output_tuple = lax.all_to_all(
        repeat_relaxation_passes, "azim", split_axis=1, concat_axis=2, tiled=True
    )
    thermal_state = output_tuple[0]
    dual_magnetic_rhs = 2.0 * loss_cell * output_tuple[1] * flux
    return (magnetic_misfit, dual_magnetic_rhs, thermal_state)


def solution(mesh):
    in_specs = (
        P(None, "azim", "section", "axial"),
        P(None, "azim", "section", "axial"),
        P("azim", "section", "axial"),
        P(),
        P("axial"),
        P(),
        P(),
        P(),
        P(),
        P(),
        P(),
        P(None, ("section", "azim"), "axial"),
        P(None, ("section", "azim"), "axial"),
    )
    out_specs = (
        P(None, "azim", "section", "axial"),
        P(None, "azim", "section", "axial"),
        P("azim", "section", "axial"),
    )
    return jax.shard_map(body, mesh=mesh, in_specs=in_specs, out_specs=out_specs, check_vma=False)
```

profile of v0, /device:TPU:1, one launch (start us, length us, event | category | flops | bytes accessed | tf_op | source)
XLA Modules:
  0.0 252.0 jit_solution(4269325337116339171)
XLA Ops:
  7.5 6.0 %select_bitcast_fusion.2 = (f32[1,1,256,128]{2,3,1,0:T(8,128)}, pred[1,256,128]{1,2,0:T(8,128)(4,1)S(1)}, pred[1,256,128]{1,2,0:T(8,128)(4,1)S(1)}, pred[1,256,1...) fusion(f32[]{:T(128)} %bitcast.49, f32[]{:T(128)} %bitcast.48, ...), kind=kLoop, calls=%fused_computation.244 | loop fusion | flops 557056 | bytes 590112 | tf_op jit(solution)/shard_map/stack | solution.py:169
  13.5 5.0 %select_bitcast_fusion.4 = f32[1,1,256,128]{2,3,1,0:T(8,128)S(1)} fusion(pred[1,256,128]{1,2,0:T(8,128)(4,1)S(1)} %get-tuple-element.19, pred[1,256,128]{1,2,0:T(8,128)(4,1)S(1)} %get-tuple-element.18, pred[1,256,128]{1,2,0:T(8,128)(4,1)S(1)} %get-tuple-element.17, pred[1,256,128]{1,2,0:T(8,128)(4,1)S(1)} %get-tuple-element.16, ...), kind=kLoop, calls=%fused_computation.247 | loop fusion | flops 262144 | bytes 393248 | tf_op jit(solution)/shard_map/broadcast_in_dim | solution.py:161
  18.6 8.7 %collective-permute-start.1 = (f32[4,1,256,128]{2,3,1,0:T(8,128)S(1)}, f32[4,1,256,128]{2,3,1,0:T(8,128)S(1)}, u32[]{:S(2)}, u32[]{:S(2)}) collective-permute-start(f32[4,1,256,128]{2,3,1,0:T(8,128)S(1)} %pad_maximum_fusion.50), channel_id=1, source_target_pairs={{4,0},{8,4},{12,8},{16,12},{20,16},{24,20},{28,24},{32,28},{36,32}... | collective-permute-start | bytes 1572872 | tf_op jit(solution)/shard_map/ppermute | solution.py:20
  29.5 5.8 %select_bitcast_fusion.3 = f32[256,128]{0,1:T(8,128)} fusion(pred[1,256,128]{1,2,0:T(8,128)(4,1)S(1)} %get-tuple-element.19, pred[1,256,128]{1,2,0:T(8,128)(4,1)S(1)} %get-tuple-element.18, pred[1,256,128]{1,2,0:T(8,128)(4,1)S(1)} %get-tuple-element.17, pred[1,256,128]{1,2,0:T(8,128)(4,1)S(1)} %get-tuple-element.16, ...), kind=kLoop, calls=%fused_computation.246 | loop fusion | flops 262144 | bytes 393248 | tf_op jit(solution)/shard_map/mul | solution.py:164
  35.9 5.9 %select_bitcast_fusion = f32[1,1,256,128]{2,3,1,0:T(8,128)} fusion(pred[1,256,128]{1,2,0:T(8,128)(4,1)S(1)} %get-tuple-element.19, pred[1,256,128]{1,2,0:T(8,128)(4,1)S(1)} %get-tuple-element.18, pred[1,256,128]{1,2,0:T(8,128)(4,1)S(1)} %get-tuple-element.17, pred[1,256,128]{1,2,0:T(8,128)(4,1)S(1)} %get-tuple-element.16, ...), kind=kLoop, calls=%fused_computation.242 | loop fusion | flops 262144 | bytes 393248 | tf_op jit(solution)/shard_map/stack | solution.py:169
  41.8 5.8 %select_bitcast_fusion.1 = f32[1,1,256,128]{2,3,1,0:T(8,128)} fusion(pred[1,256,128]{1,2,0:T(8,128)(4,1)S(1)} %get-tuple-element.19, pred[1,256,128]{1,2,0:T(8,128)(4,1)S(1)} %get-tuple-element.18, pred[1,256,128]{1,2,0:T(8,128)(4,1)S(1)} %get-tuple-element.17, pred[1,256,128]{1,2,0:T(8,128)(4,1)S(1)} %get-tuple-element.16, ...), kind=kLoop, calls=%fused_computation.243 | loop fusion | flops 262144 | bytes 393248 | tf_op jit(solution)/shard_map/stack | solution.py:169
  49.8 4.6 %collective-permute-start.2 = (f32[4,3,1,128]{3,0,2,1:T(4,128)S(1)}, f32[4,3,1,128]{3,0,2,1:T(4,128)}, u32[]{:S(2)}, u32[]{:S(2)}) collective-permute-start(f32[4,3,1,128]{3,0,2,1:T(4,128)S(1)} %copy.171), channel_id=1, source_target_pairs={{0,128},{1,129},{2,130},{3,131},{4,132},{5,133},{6,134},{7,135},{8... | collective-permute-start | bytes 18440 | tf_op jit(solution)/shard_map/ppermute | solution.py:17
  57.1 3.4 %collective-permute-start.5 = (f32[4,3,258,1]{2,0,3,1:T(4,128)}, f32[4,3,258,1]{2,0,3,1:T(4,128)}, u32[]{:S(2)}, u32[]{:S(2)}) collective-permute-start(f32[4,3,258,1]{2,0,3,1:T(4,128)} %copy.176), channel_id=1, source_target_pairs={{1,0},{2,1},{3,2},{5,4},{6,5},{7,6},{9,8},{10,9},{11,10},{13,12},{... | collective-permute-start | bytes 37160 | tf_op jit(solution)/shard_map/ppermute | solution.py:20
  61.1 4.7 %collective-permute-start.4 = (f32[4,3,258,1]{2,0,3,1:T(4,128)}, f32[4,3,258,1]{2,0,3,1:T(4,128)}, u32[]{:S(2)}, u32[]{:S(2)}) collective-permute-start(f32[4,3,258,1]{2,0,3,1:T(4,128)} %copy.175), channel_id=1, source_target_pairs={{0,1},{1,2},{2,3},{4,5},{5,6},{6,7},{8,9},{9,10},{10,11},{12,13},{... | collective-permute-start | bytes 37160 | tf_op jit(solution)/shard_map/ppermute | solution.py:17
  73.4 4.9 %fusion.105 = f32[1,1,256,128]{2,3,1,0:T(8,128)S(1)} fusion(f32[256,128]{0,1:T(8,128)S(1)} %get-tuple-element.9, pred[1,256,128]{1,2,0:T(8,128)(4,1)S(1)} %get-tuple-element.19, pred[1,256,128]{1,2,0:T(8,128)(4,1)S(1)} %get-tuple-element.18, pred[1,256,128]{1,2,0:T(8,128)(4,1)S(1)} %get-tuple-element.17, pred[1,256,128]{1,2,0:T(8,128)(4,1)S(1)} %get-tuple-element.16, ...), kind=kLoop, calls=%fused_computation.235 | loop fusion | flops 294912 | bytes 524320 | tf_op jit(solution)/shard_map/stack | solution.py:169
  79.5 6.7 %all-to-all-start = ((f32[4,1,256,128]{3,1,0,2:T(1,128)}), f32[4,1,256,128]{3,1,0,2:T(1,128)S(1)}, u32[]{:S(2)}, u32[]{:S(2)}) async-start(f32[4,1,256,128]{3,1,0,2:T(1,128)} %copy.183), calls=%async_computation | async-start | bytes 1048576 | tf_op jit(solution)/shard_map/all_to_all | solution.py:122
  90.6 11.7 %all-to-all-done = f32[4,1,256,128]{3,1,0,2:T(1,128)S(1)} async-done(((f32[4,1,256,128]{3,1,0,2:T(1,128)}), f32[4,1,256,128]{3,1,0,2:T(1,128)S(1)}, u32[]{:S(2)}, u32[]{:S(2)}) %all-to-all-start) | async-done | bytes 524320 | tf_op jit(solution)/shard_map/all_to_all | solution.py:122
  104.0 5.6 %collective-permute-start.7 = (f32[4,32,1,128]{3,2,1,0:T(1,128)S(1)}, f32[4,32,1,128]{3,2,1,0:T(1,128)}, u32[]{:S(2)}, u32[]{:S(2)}) collective-permute-start(f32[4,32,1,128]{3,2,1,0:T(1,128)S(1)} %get-tuple-element.104), channel_id=1, source_target_pairs={{0,4},{4,8},{8,12},{12,16},{16,20},{20,24},{24,28},{28,32},{32,36}... | collective-permute-start | bytes 196616 | tf_op jit(solution)/shard_map/ppermute | solution.py:17
  115.3 5.3 %collective-permute-start.9 = (f32[4,32,10,1]{1,0,3,2:T(4,128)S(1)}, f32[4,32,10,1]{1,0,3,2:T(4,128)}, u32[]{:S(2)}, u32[]{:S(2)}) collective-permute-start(f32[4,32,10,1]{1,0,3,2:T(4,128)S(1)} %copy.194), channel_id=1, source_target_pairs={{0,1},{1,2},{2,3},{4,5},{5,6},{6,7},{8,9},{9,10},{10,11},{12,13},{... | collective-permute-start | bytes 15368 | tf_op jit(solution)/shard_map/ppermute | solution.py:17
  125.0 3.3 %fusion.14 = (f32[4,32,10,129]{3,2,1,0:T(8,128)S(1)}, f32[4,32,10,129]{3,2,1,0:T(8,128)S(1)}) fusion(f32[1,32,8,128]{3,2,1,0:T(8,128)S(1)} %bitcast.198, f32[1,32,8,128]{3,2,1,0:T(8,128)S(1)} %bitcast.178, f32[4,32,10,1]{3,2,1,0:T(8,128)S(1)} %copy.193, f32[4,32,1,128]{3,2,1,0:T(1,128)} %collective-permute-done.6, f32[1,32,8,128]{3,2,1,0:T(8,128)} %copy-done.13, ...), kind=kLoop, calls=%fused_computation.56 | loop fusion | flops 1981440 | bytes 1986560 | tf_op jit(solution)/shard_map/concatenate | solution.py:21
  133.2 4.3 %collective-permute-start.11 = (f32[4,32,1,128]{3,2,1,0:T(1,128)S(1)}, f32[4,32,1,128]{3,2,1,0:T(1,128)S(1)}, u32[]{:S(2)}, u32[]{:S(2)}) collective-permute-start(f32[4,32,1,128]{3,2,1,0:T(1,128)S(1)} %get-tuple-element.92), channel_id=1, source_target_pairs={{0,4},{4,8},{8,12},{12,16},{16,20},{20,24},{24,28},{28,32},{32,36}... | collective-permute-start | bytes 196616 | tf_op jit(solution)/shard_map/ppermute | solution.py:17
  142.6 5.1 %collective-permute-start.13 = (f32[4,32,10,1]{1,0,3,2:T(4,128)S(1)}, f32[4,32,10,1]{1,0,3,2:T(4,128)}, u32[]{:S(2)}, u32[]{:S(2)}) collective-permute-start(f32[4,32,10,1]{1,0,3,2:T(4,128)S(1)} %copy.198), channel_id=1, source_target_pairs={{0,1},{1,2},{2,3},{4,5},{5,6},{6,7},{8,9},{9,10},{10,11},{12,13},{... | collective-permute-start | bytes 15368 | tf_op jit(solution)/shard_map/ppermute | solution.py:17
  159.1 4.3 %collective-permute-start.15 = (f32[4,32,1,128]{3,2,1,0:T(1,128)S(1)}, f32[4,32,1,128]{3,2,1,0:T(1,128)S(1)}, u32[]{:S(2)}, u32[]{:S(2)}) collective-permute-start(f32[4,32,1,128]{3,2,1,0:T(1,128)S(1)} %get-tuple-element.88), channel_id=1, source_target_pairs={{0,4},{4,8},{8,12},{12,16},{16,20},{20,24},{24,28},{28,32},{32,36}... | collective-permute-start | bytes 196616 | tf_op jit(solution)/shard_map/ppermute | solution.py:17
  169.2 6.0 %collective-permute-start.17 = (f32[4,32,10,1]{1,0,3,2:T(4,128)S(1)}, f32[4,32,10,1]{1,0,3,2:T(4,128)}, u32[]{:S(2)}, u32[]{:S(2)}) collective-permute-start(f32[4,32,10,1]{1,0,3,2:T(4,128)S(1)} %copy.202), channel_id=1, source_target_pairs={{0,1},{1,2},{2,3},{4,5},{5,6},{6,7},{8,9},{9,10},{10,11},{12,13},{... | collective-permute-start | bytes 15368 | tf_op jit(solution)/shard_map/ppermute | solution.py:17
  187.3 4.6 %collective-permute-start.19 = (f32[4,32,1,128]{3,2,1,0:T(1,128)S(1)}, f32[4,32,1,128]{3,2,1,0:T(1,128)S(1)}, u32[]{:S(2)}, u32[]{:S(2)}) collective-permute-start(f32[4,32,1,128]{3,2,1,0:T(1,128)S(1)} %get-tuple-element.84), channel_id=1, source_target_pairs={{0,4},{4,8},{8,12},{12,16},{16,20},{20,24},{24,28},{28,32},{32,36}... | collective-permute-start | bytes 196616 | tf_op jit(solution)/shard_map/ppermute | solution.py:17
  197.9 5.1 %collective-permute-start.21 = (f32[4,32,10,1]{1,0,3,2:T(4,128)S(1)}, f32[4,32,10,1]{1,0,3,2:T(4,128)}, u32[]{:S(2)}, u32[]{:S(2)}) collective-permute-start(f32[4,32,10,1]{1,0,3,2:T(4,128)S(1)} %copy.206), channel_id=1, source_target_pairs={{0,1},{1,2},{2,3},{4,5},{5,6},{6,7},{8,9},{9,10},{10,11},{12,13},{... | collective-permute-start | bytes 15368 | tf_op jit(solution)/shard_map/ppermute | solution.py:17
  213.8 20.2 %all-to-all-start.1 = ((f32[2,32,8,128]{3,2,0,1:T(8,128)}), f32[2,32,8,128]{3,2,0,1:T(8,128)S(1)}, u32[]{:S(2)}, u32[]{:S(2)}) async-start(f32[2,32,8,128]{3,2,0,1:T(8,128)} %copy.208), calls=%async_computation.1 | async-start | bytes 524288 | tf_op jit(solution)/shard_map/all_to_all | solution.py:183
  237.8 7.4 %all-to-all-done.1 = f32[2,32,8,128]{3,2,0,1:T(8,128)S(1)} async-done(((f32[2,32,8,128]{3,2,0,1:T(8,128)}), f32[2,32,8,128]{3,2,0,1:T(8,128)S(1)}, u32[]{:S(2)}, u32[]{:S(2)}) %all-to-all-start.1) | async-done | bytes 262176 | tf_op jit(solution)/shard_map/all_to_all | solution.py:183
  246.0 4.9 %multiply_bitcast_fusion = f32[256,128]{0,1:T(8,128)S(1)} fusion(f32[1,256,128]{1,2,0:T(8,128)S(1)} %copy.210, pred[1,256,128]{1,2,0:T(8,128)(4,1)S(1)} %copy-done.33, pred[1,256,128]{1,2,0:T(8,128)(4,1)S(1)} %copy-done.31, pred[1,256,128]{1,2,0:T(8,128)(4,1)S(1)} %copy-done.29, pred[1,256,128]{1,2,0:T(8,128)(4,1)S(1)} %copy-done.27, ...), kind=kLoop, calls=%fused_computation.236 | loop fusion | flops 327680 | bytes 524320 | tf_op jit(solution)/shard_map/mul | solution.py:187
  (269 shorter events, 100.4 us)
Async XLA Ops:
  18.6 29.0 %collective-permute-start.1 = (f32[4,1,256,128]{2,3,1,0:T(8,128)S(1)}, f32[4,1,256,128]{2,3,1,0:T(8,128)S(1)}, u32[]{:S(2)}, u32[]{:S(2)}) collective-permute-start(f32[4,1,256,128]{2,3,1,0:T(8,128)S(1)} %pad_maximum_fusion.50), channel_id=1, source_target_pairs={{4,0},{8,4},{12,8},{16,12},{20,16},{24,20},{28,24},{32,28},{36,32}... | collective-permute-start | bytes 1572872 | tf_op jit(solution)/shard_map/ppermute | solution.py:20
  27.2 20.4 %collective-permute-start = (f32[4,1,256,128]{2,3,1,0:T(8,128)S(1)}, f32[4,1,256,128]{2,3,1,0:T(8,128)S(1)}, u32[]{:S(2)}, u32[]{:S(2)}) collective-permute-start(f32[4,1,256,128]{2,3,1,0:T(8,128)S(1)} %pad_maximum_fusion.50), channel_id=1, source_target_pairs={{0,4},{4,8},{8,12},{12,16},{16,20},{20,24},{24,28},{28,32},{32,36}... | collective-permute-start | bytes 1572872 | tf_op jit(solution)/shard_map/ppermute | solution.py:17
  48.3 6.7 %collective-permute-start.3 = (f32[4,3,1,128]{3,0,2,1:T(4,128)S(1)}, f32[4,3,1,128]{3,0,2,1:T(4,128)S(1)}, u32[]{:S(2)}, u32[]{:S(2)}) collective-permute-start(f32[4,3,1,128]{3,0,2,1:T(4,128)S(1)} %copy.172), channel_id=1, source_target_pairs={{128,0},{129,1},{130,2},{131,3},{132,4},{133,5},{134,6},{135,7},{1... | collective-permute-start | bytes 18440 | tf_op jit(solution)/shard_map/ppermute | solution.py:20
  49.8 5.5 %collective-permute-start.2 = (f32[4,3,1,128]{3,0,2,1:T(4,128)S(1)}, f32[4,3,1,128]{3,0,2,1:T(4,128)}, u32[]{:S(2)}, u32[]{:S(2)}) collective-permute-start(f32[4,3,1,128]{3,0,2,1:T(4,128)S(1)} %copy.171), channel_id=1, source_target_pairs={{0,128},{1,129},{2,130},{3,131},{4,132},{5,133},{6,134},{7,135},{8... | collective-permute-start | bytes 18440 | tf_op jit(solution)/shard_map/ppermute | solution.py:17
  57.1 11.3 %collective-permute-start.5 = (f32[4,3,258,1]{2,0,3,1:T(4,128)}, f32[4,3,258,1]{2,0,3,1:T(4,128)}, u32[]{:S(2)}, u32[]{:S(2)}) collective-permute-start(f32[4,3,258,1]{2,0,3,1:T(4,128)} %copy.176), channel_id=1, source_target_pairs={{1,0},{2,1},{3,2},{5,4},{6,5},{7,6},{9,8},{10,9},{11,10},{13,12},{... | collective-permute-start | bytes 37160 | tf_op jit(solution)/shard_map/ppermute | solution.py:20
  61.1 8.1 %collective-permute-start.4 = (f32[4,3,258,1]{2,0,3,1:T(4,128)}, f32[4,3,258,1]{2,0,3,1:T(4,128)}, u32[]{:S(2)}, u32[]{:S(2)}) collective-permute-start(f32[4,3,258,1]{2,0,3,1:T(4,128)} %copy.175), channel_id=1, source_target_pairs={{0,1},{1,2},{2,3},{4,5},{5,6},{6,7},{8,9},{9,10},{10,11},{12,13},{... | collective-permute-start | bytes 37160 | tf_op jit(solution)/shard_map/ppermute | solution.py:17
  79.5 22.7 %all-to-all-start = ((f32[4,1,256,128]{3,1,0,2:T(1,128)}), f32[4,1,256,128]{3,1,0,2:T(1,128)S(1)}, u32[]{:S(2)}, u32[]{:S(2)}) async-start(f32[4,1,256,128]{3,1,0,2:T(1,128)} %copy.183), calls=%async_computation | async-start | bytes 1048576 | tf_op jit(solution)/shard_map/all_to_all | solution.py:122
  102.7 7.7 %collective-permute-start.6 = (f32[4,32,1,128]{3,2,1,0:T(1,128)S(1)}, f32[4,32,1,128]{3,2,1,0:T(1,128)}, u32[]{:S(2)}, u32[]{:S(2)}) collective-permute-start(f32[4,32,1,128]{3,2,1,0:T(1,128)S(1)} %get-tuple-element.105), channel_id=1, source_target_pairs={{4,0},{8,4},{12,8},{16,12},{20,16},{24,20},{28,24},{32,28},{36,32}... | collective-permute-start | bytes 196616 | tf_op jit(solution)/shard_map/ppermute | solution.py:20
  104.0 6.5 %collective-permute-start.7 = (f32[4,32,1,128]{3,2,1,0:T(1,128)S(1)}, f32[4,32,1,128]{3,2,1,0:T(1,128)}, u32[]{:S(2)}, u32[]{:S(2)}) collective-permute-start(f32[4,32,1,128]{3,2,1,0:T(1,128)S(1)} %get-tuple-element.104), channel_id=1, source_target_pairs={{0,4},{4,8},{8,12},{12,16},{16,20},{20,24},{24,28},{28,32},{32,36}... | collective-permute-start | bytes 196616 | tf_op jit(solution)/shard_map/ppermute | solution.py:17
  113.0 10.2 %collective-permute-start.8 = (f32[4,32,10,1]{1,0,3,2:T(4,128)}, f32[4,32,10,1]{1,0,3,2:T(4,128)S(1)}, u32[]{:S(2)}, u32[]{:S(2)}) collective-permute-start(f32[4,32,10,1]{1,0,3,2:T(4,128)} %copy.192), channel_id=1, source_target_pairs={{1,0},{2,1},{3,2},{5,4},{6,5},{7,6},{9,8},{10,9},{11,10},{13,12},{... | collective-permute-start | bytes 15368 | tf_op jit(solution)/shard_map/ppermute | solution.py:20
  115.3 8.4 %collective-permute-start.9 = (f32[4,32,10,1]{1,0,3,2:T(4,128)S(1)}, f32[4,32,10,1]{1,0,3,2:T(4,128)}, u32[]{:S(2)}, u32[]{:S(2)}) collective-permute-start(f32[4,32,10,1]{1,0,3,2:T(4,128)S(1)} %copy.194), channel_id=1, source_target_pairs={{0,1},{1,2},{2,3},{4,5},{5,6},{6,7},{8,9},{9,10},{10,11},{12,13},{... | collective-permute-start | bytes 15368 | tf_op jit(solution)/shard_map/ppermute | solution.py:17
  131.9 5.6 %collective-permute-start.10 = (f32[4,32,1,128]{3,2,1,0:T(1,128)S(1)}, f32[4,32,1,128]{3,2,1,0:T(1,128)S(1)}, u32[]{:S(2)}, u32[]{:S(2)}) collective-permute-start(f32[4,32,1,128]{3,2,1,0:T(1,128)S(1)} %get-tuple-element.93), channel_id=1, source_target_pairs={{4,0},{8,4},{12,8},{16,12},{20,16},{24,20},{28,24},{32,28},{36,32}... | collective-permute-start | bytes 196616 | tf_op jit(solution)/shard_map/ppermute | solution.py:20
  133.2 5.6 %collective-permute-start.11 = (f32[4,32,1,128]{3,2,1,0:T(1,128)S(1)}, f32[4,32,1,128]{3,2,1,0:T(1,128)S(1)}, u32[]{:S(2)}, u32[]{:S(2)}) collective-permute-start(f32[4,32,1,128]{3,2,1,0:T(1,128)S(1)} %get-tuple-element.92), channel_id=1, source_target_pairs={{0,4},{4,8},{8,12},{12,16},{16,20},{20,24},{24,28},{28,32},{32,36}... | collective-permute-start | bytes 196616 | tf_op jit(solution)/shard_map/ppermute | solution.py:17
  140.3 9.0 %collective-permute-start.12 = (f32[4,32,10,1]{1,0,3,2:T(4,128)}, f32[4,32,10,1]{1,0,3,2:T(4,128)S(1)}, u32[]{:S(2)}, u32[]{:S(2)}) collective-permute-start(f32[4,32,10,1]{1,0,3,2:T(4,128)} %copy.196), channel_id=1, source_target_pairs={{1,0},{2,1},{3,2},{5,4},{6,5},{7,6},{9,8},{10,9},{11,10},{13,12},{... | collective-permute-start | bytes 15368 | tf_op jit(solution)/shard_map/ppermute | solution.py:20
  142.6 7.2 %collective-permute-start.13 = (f32[4,32,10,1]{1,0,3,2:T(4,128)S(1)}, f32[4,32,10,1]{1,0,3,2:T(4,128)}, u32[]{:S(2)}, u32[]{:S(2)}) collective-permute-start(f32[4,32,10,1]{1,0,3,2:T(4,128)S(1)} %copy.198), channel_id=1, source_target_pairs={{0,1},{1,2},{2,3},{4,5},{5,6},{6,7},{8,9},{9,10},{10,11},{12,13},{... | collective-permute-start | bytes 15368 | tf_op jit(solution)/shard_map/ppermute | solution.py:17
  157.8 5.6 %collective-permute-start.14 = (f32[4,32,1,128]{3,2,1,0:T(1,128)S(1)}, f32[4,32,1,128]{3,2,1,0:T(1,128)S(1)}, u32[]{:S(2)}, u32[]{:S(2)}) collective-permute-start(f32[4,32,1,128]{3,2,1,0:T(1,128)S(1)} %get-tuple-element.89), channel_id=1, source_target_pairs={{4,0},{8,4},{12,8},{16,12},{20,16},{24,20},{28,24},{32,28},{36,32}... | collective-permute-start | bytes 196616 | tf_op jit(solution)/shard_map/ppermute | solution.py:20
  159.1 5.6 %collective-permute-start.15 = (f32[4,32,1,128]{3,2,1,0:T(1,128)S(1)}, f32[4,32,1,128]{3,2,1,0:T(1,128)S(1)}, u32[]{:S(2)}, u32[]{:S(2)}) collective-permute-start(f32[4,32,1,128]{3,2,1,0:T(1,128)S(1)} %get-tuple-element.88), channel_id=1, source_target_pairs={{0,4},{4,8},{8,12},{12,16},{16,20},{20,24},{24,28},{28,32},{32,36}... | collective-permute-start | bytes 196616 | tf_op jit(solution)/shard_map/ppermute | solution.py:17
  166.9 10.7 %collective-permute-start.16 = (f32[4,32,10,1]{1,0,3,2:T(4,128)}, f32[4,32,10,1]{1,0,3,2:T(4,128)S(1)}, u32[]{:S(2)}, u32[]{:S(2)}) collective-permute-start(f32[4,32,10,1]{1,0,3,2:T(4,128)} %copy.200), channel_id=1, source_target_pairs={{1,0},{2,1},{3,2},{5,4},{6,5},{7,6},{9,8},{10,9},{11,10},{13,12},{... | collective-permute-start | bytes 15368 | tf_op jit(solution)/shard_map/ppermute | solution.py:20
  169.2 9.0 %collective-permute-start.17 = (f32[4,32,10,1]{1,0,3,2:T(4,128)S(1)}, f32[4,32,10,1]{1,0,3,2:T(4,128)}, u32[]{:S(2)}, u32[]{:S(2)}) collective-permute-start(f32[4,32,10,1]{1,0,3,2:T(4,128)S(1)} %copy.202), channel_id=1, source_target_pairs={{0,1},{1,2},{2,3},{4,5},{5,6},{6,7},{8,9},{9,10},{10,11},{12,13},{... | collective-permute-start | bytes 15368 | tf_op jit(solution)/shard_map/ppermute | solution.py:17
  186.0 5.9 %collective-permute-start.18 = (f32[4,32,1,128]{3,2,1,0:T(1,128)S(1)}, f32[4,32,1,128]{3,2,1,0:T(1,128)S(1)}, u32[]{:S(2)}, u32[]{:S(2)}) collective-permute-start(f32[4,32,1,128]{3,2,1,0:T(1,128)S(1)} %get-tuple-element.85), channel_id=1, source_target_pairs={{4,0},{8,4},{12,8},{16,12},{20,16},{24,20},{28,24},{32,28},{36,32}... | collective-permute-start | bytes 196616 | tf_op jit(solution)/shard_map/ppermute | solution.py:20
  187.3 5.9 %collective-permute-start.19 = (f32[4,32,1,128]{3,2,1,0:T(1,128)S(1)}, f32[4,32,1,128]{3,2,1,0:T(1,128)S(1)}, u32[]{:S(2)}, u32[]{:S(2)}) collective-permute-start(f32[4,32,1,128]{3,2,1,0:T(1,128)S(1)} %get-tuple-element.84), channel_id=1, source_target_pairs={{0,4},{4,8},{8,12},{12,16},{16,20},{20,24},{24,28},{28,32},{32,36}... | collective-permute-start | bytes 196616 | tf_op jit(solution)/shard_map/ppermute | solution.py:17
  195.4 10.1 %collective-permute-start.20 = (f32[4,32,10,1]{1,0,3,2:T(4,128)}, f32[4,32,10,1]{1,0,3,2:T(4,128)S(1)}, u32[]{:S(2)}, u32[]{:S(2)}) collective-permute-start(f32[4,32,10,1]{1,0,3,2:T(4,128)} %copy.204), channel_id=1, source_target_pairs={{1,0},{2,1},{3,2},{5,4},{6,5},{7,6},{9,8},{10,9},{11,10},{13,12},{... | collective-permute-start | bytes 15368 | tf_op jit(solution)/shard_map/ppermute | solution.py:20
  197.9 8.1 %collective-permute-start.21 = (f32[4,32,10,1]{1,0,3,2:T(4,128)S(1)}, f32[4,32,10,1]{1,0,3,2:T(4,128)}, u32[]{:S(2)}, u32[]{:S(2)}) collective-permute-start(f32[4,32,10,1]{1,0,3,2:T(4,128)S(1)} %copy.206), channel_id=1, source_target_pairs={{0,1},{1,2},{2,3},{4,5},{5,6},{6,7},{8,9},{9,10},{10,11},{12,13},{... | collective-permute-start | bytes 15368 | tf_op jit(solution)/shard_map/ppermute | solution.py:17
  213.8 31.4 %all-to-all-start.1 = ((f32[2,32,8,128]{3,2,0,1:T(8,128)}), f32[2,32,8,128]{3,2,0,1:T(8,128)S(1)}, u32[]{:S(2)}, u32[]{:S(2)}) async-start(f32[2,32,8,128]{3,2,0,1:T(8,128)} %copy.208), calls=%async_computation.1 | async-start | bytes 524288 | tf_op jit(solution)/shard_map/all_to_all | solution.py:183
  (62 other events, 1022.5 us)
where the time goes:
time: 255 us; the launch traced here: 252 us
  starting transfers between devices  103 us (40%)
  other arithmetic  79.1 us (31%)
  local copies, waits for them, and re-layouts  44.7 us (18%)
  waiting for transfers between devices  23 us (9%)
    ppermute x11, starting transfers between devices, padded_2(): lax.ppermute(lax.slice_in_dim(block, block.shape[dim] - width, None, axis...  49.7 us
    ppermute x11, starting transfers between devices, padded_2(): lax.ppermute(lax.slice_in_dim(block, 0, width, axis=dim), axis, backward)  26.4 us
    concatenate x14, other arithmetic, padded_2(): block = jnp.concatenate([low, block, high], axis=dim)  23.8 us
    another operation x5, other arithmetic, body(): jnp.stack([thermal_rhs, plane_cell, axial_cell, local_thermal_storage])  22.6 us
    all_to_all x1, starting transfers between devices, body(): lax.all_to_all(repeat_relaxation_passes, 'azim', split_axis=1, concat_axi...  20.2 us
    all_to_all x1, waiting for transfers between devices, relay_out(): lax.all_to_all(stacked, 'azim', split_axis=2, concat_axis=1, tiled=True)  11.7 us
    all_to_all x1, waiting for transfers between devices, body(): lax.all_to_all(repeat_relaxation_passes, 'azim', split_axis=1, concat_axi...  7.41 us
    unnamed x129, local copies, waits for them, and re-layouts  7.41 us
  transfers between devices with their start and end apart: 24, of which 5 were waited for; matrix products, arithmetic and copies ran while one was open for 19% of the time, Pallas kernels for 0%

commit v1 on v0

v1 whole, which is shorter than its diff:
```python
import functools
import jax
import jax.numpy as jnp
from jax import lax
from jax.experimental import pallas as pl
from jax.experimental.pallas import tpu as pltpu
from jax.sharding import PartitionSpec as P

NREG = 8
SWEEPS = 4
NA = 32
F32 = jnp.float32
VM = pl.BlockSpec(memory_space=pltpu.VMEM)
SM = pl.BlockSpec(memory_space=pltpu.SMEM)


def params(mib):
    return pltpu.CompilerParams(vmem_limit_bytes=mib * 1024 * 1024)


def sub_low(shape):
    return lax.broadcasted_iota(jnp.int32, shape, len(shape) - 2) % 8 < 4


def pack_down(first, second):
    return jnp.where(sub_low(first.shape), first, pltpu.roll(second, 4, 0))


def pack_up(first, second):
    return jnp.where(sub_low(first.shape), pltpu.roll(first, 4, 0), second)


def unpack_first(from_next, from_prev):
    return jnp.where(sub_low(from_next.shape), from_next, pltpu.roll(from_prev, 4, 0))


def unpack_second(from_next, from_prev):
    return jnp.where(sub_low(from_next.shape), pltpu.roll(from_next, 4, 0), from_prev)


def lookup(region, tables):
    found = [jnp.zeros(region.shape, F32) for _ in tables]
    for k in range(NREG):
        match = region == float(k + 1)
        found = [jnp.where(match, t[k], f) for t, f in zip(tables, found)]
    return found


def send_kernel(pot, fixed, spin, offs, prior, goal, out, region_out, prior_down, prior_up):
    section = lax.axis_index("section")
    azim = lax.axis_index("azim")
    shifted = (azim - offs[...]) & (NA - 1)
    rows = lax.broadcasted_iota(jnp.int32, (NA, 128), 0)
    hot = jnp.where(rows == shifted, 1.0, 0.0).astype(jnp.bfloat16)
    rotor = lax.dot_general(
        spin[...].astype(F32).astype(jnp.bfloat16), hot, (((0,), (0,)), ((), ())), preferred_element_type=F32
    )
    stator = fixed[0].astype(F32)
    inner = jnp.where(section == 0, rotor, stator[:128])
    region_out[:128] = inner + 1.0
    region_out[128:] = stator[128:] + 1.0
    for j in range(NA):
        at = pl.ds(8 * j, 8)
        for f in range(3):
            out[j, pl.ds(8 * f, 8), :] = pot[f, 0, at, :]
        out[j, pl.ds(24, 8), :] = region_out[at, :]
        prior_down[j] = pack_down(prior[j], goal[j])
        prior_up[j] = pack_up(prior[j], goal[j])


def rows_kernel(got, down, up):
    for a in range(NA):
        for p in range(2):
            first = got[a, pl.ds(16 * p, 8), :]
            second = got[a, pl.ds(16 * p + 8, 8), :]
            down[a, pl.ds(8 * p, 8), :] = pack_down(first, second)
            up[a, pl.ds(8 * p, 8), :] = pack_up(first, second)


def window(got, prior, goal, from_next, from_prev, heat_next, heat_prev, a):
    tiles = []
    for p in range(2):
        nxt = from_next[a, pl.ds(8 * p, 8), :]
        prv = from_prev[a, pl.ds(8 * p, 8), :]
        tiles.append((got[a, pl.ds(16 * p, 8), :], unpack_first(nxt, prv)))
        tiles.append((got[a, pl.ds(16 * p + 8, 8), :], unpack_second(nxt, prv)))
    nxt, prv = heat_next[a], heat_prev[a]
    tiles.append((prior[a], unpack_first(nxt, prv)))
    tiles.append((goal[a], unpack_second(nxt, prv)))
    return tiles


def layers_kernel(got, prior, goal, from_next, from_prev, heat_next, heat_prev, edge):
    lane = lax.broadcasted_iota(jnp.int32, (8, 128), 1) // 8

    def step(a, carry):
        tiles = window(got, prior, goal, from_next, from_prev, heat_next, heat_prev, a)
        packed = jnp.zeros((8, 128), F32)
        for f in range(6):
            for t in range(2):
                c = 2 * f + t
                packed = jnp.where(lane == c, pltpu.roll(tiles[f][t], 4 + 8 * c, 1), packed)
        edge[a] = packed
        return carry

    lax.fori_loop(0, NA, step, 0)


def rnext(v):
    return pltpu.roll(v, 15, 0)


def rprev(v):
    return pltpu.roll(v, 1, 0)


def lnext(v):
    return pltpu.roll(v, 255, 1)


def lprev(v):
    return pltpu.roll(v, 1, 1)


def heat_kernel(
    got, prior, goal, from_next, from_prev, heat_next, heat_prev, edge_core, edge_far,
    reluct, loss, plane, axial, storage, out,
    pot, mats, pri, sens, coef, base, flux, hfield, temp, adj,
):
    odd = lax.axis_index("axial") % 2 == 1
    lane = lax.broadcasted_iota(jnp.int32, (8, 128), 1)
    from_right = lane % 8 >= 4
    near = (lane < 4) | (lane >= 124)

    def gather(a, carry):
        tiles = window(got, prior, goal, from_next, from_prev, heat_next, heat_prev, a)
        core, far = edge_core[a], edge_far[a]
        pick_core = from_right != odd
        merged = jnp.where(pick_core, core, far)
        wide = []
        for f in range(6):
            ends = []
            for t in range(2):
                c = 2 * f + t
                ends.append(jnp.where(near, pltpu.roll(merged, 124 - 8 * c, 1), 0.0))
            main = jnp.concatenate([tiles[f][0], tiles[f][1]], axis=0)
            side = jnp.concatenate([ends[0], ends[1]], axis=0)
            wide.append(jnp.concatenate([main, side], axis=1))
        for f in range(3):
            pot[f, a] = wide[f]
        found = lookup(wide[3], (reluct, loss, plane, axial, storage))
        for m in range(5):
            mats[m, a] = found[m]
        pri[a] = wide[4]
        sens[a] = wide[5]
        return carry

    lax.fori_loop(0, NA, gather, 0)

    def prepare(a, carry):
        up = (a + 1) & (NA - 1)
        down = (a - 1) & (NA - 1)
        pa, pr, pz = pot[0, a], pot[1, a], pot[2, a]
        fa = (rnext(pz) - pz) - (lnext(pr) - pr)
        fr = (lnext(pa) - pa) - (pot[2, up] - pz)
        fz = (pot[1, up] - pr) - (rnext(pa) - pa)
        flux[0, a] = fa[:8, :128]
        flux[1, a] = fr[:8, :128]
        flux[2, a] = fz[:8, :128]
        rel, dens, kp, ka, cap = (mats[m, a] for m in range(5))
        hfield[0, a] = rel * fa
        hfield[1, a] = rel * fr
        hfield[2, a] = rel * fz
        source = cap * pri[a] + dens * (fa * fa + fr * fr + fz * fz)
        w = [
            0.5 * (kp + mats[2, up]), 0.5 * (kp + mats[2, down]),
            0.5 * (kp + rnext(kp)), 0.5 * (kp + rprev(kp)),
            0.5 * (ka + lnext(ka)), 0.5 * (ka + lprev(ka)),
        ]
        total = cap + (((((w[0] + w[1]) + w[2]) + w[3]) + w[4]) + w[5])
        inside = cap > 0.0
        inv = jnp.where(inside, 1.0 / jnp.where(inside, total, 1.0), 0.0)
        for n in range(6):
            coef[n, a] = inv * w[n]
        base[0, a] = inv * source
        first = inv * sens[a]
        base[1, a] = first
        adj[0, a] = first
        return carry

    lax.fori_loop(0, NA, prepare, 0)

    def relax(field, slot, a, c, b):
        up = (a + 1) & (NA - 1)
        down = (a - 1) & (NA - 1)
        v = field(a)
        total = b + c[0] * field(up) + c[1] * field(down)
        total = total + c[2] * rnext(v) + c[3] * rprev(v)
        return total + c[4] * lnext(v) + c[5] * lprev(v)

    for sweep in range(SWEEPS):
        now, later = sweep % 2, (sweep + 1) % 2

        def step(a, carry, sweep=sweep, now=now, later=later):
            c = [coef[n, a] for n in range(6)]
            if sweep == 0:
                temp[later, a] = relax(lambda i: pri[i], later, a, c, base[0, a])
            else:
                temp[later, a] = relax(lambda i: temp[now, i], later, a, c, base[0, a])
                adj[now, a] = relax(lambda i: adj[later, i], later, a, c, base[1, a])
            return carry

        lax.fori_loop(0, NA, step, 0)

    last_t = SWEEPS % 2
    last_a = (SWEEPS - 1) % 2

    def finish(a, carry):
        down = (a - 1) & (NA - 1)
        scale = 2.0 * mats[1, a][:8, :128] * adj[last_a, a][:8, :128]
        ha, hr, hz = hfield[0, a], hfield[1, a], hfield[2, a]
        ca = (lprev(hr) - hr) - (rprev(hz) - hz)
        cr = (hfield[2, down] - hz) - (lprev(ha) - ha)
        cz = (rprev(ha) - ha) - (hfield[1, down] - hr)
        out[a, pl.ds(0, 8), :] = ca[:8, :128]
        out[a, pl.ds(8, 8), :] = cr[:8, :128]
        out[a, pl.ds(16, 8), :] = cz[:8, :128]
        for f in range(3):
            out[a, pl.ds(24 + 8 * f, 8), :] = scale * flux[f, a]
        out[a, pl.ds(48, 8), :] = temp[last_t, a][:8, :128]
        return carry

    lax.fori_loop(0, NA, finish, 0)


def finish_kernel(got, region, pot, current, eddy, misfit, dual, state):
    def step(j, carry):
        at = pl.ds(pl.multiple_of(8 * j, 8), 8)
        (sigma,) = lookup(region[at, :], (eddy,))
        for f in range(3):
            curl = got[j, pl.ds(8 * f, 8), :]
            misfit[f, 0, at, :] = curl + sigma * pot[f, 0, at, :] - current[f, 0, at, :]
            dual[f, 0, at, :] = got[j, pl.ds(24 + 8 * f, 8), :]
        state[0, at, :] = got[j, pl.ds(48, 8), :]
        return carry

    lax.fori_loop(0, NA, step, 0)


def struct(*shape):
    return jax.ShapeDtypeStruct(shape, F32)


def body(
    magnetic_vector_field,
    imposed_current_density,
    fixed_material_map,
    spinning_material_map,
    slab_slide_offsets,
    inverse_permeability,
    electric_conductance,
    core_dissipation_coefficient,
    inplane_thermal_conductance,
    through_plane_conductance,
    thermal_storage,
    prior_thermal_state,
    goal_sensitivity,
):
    rows = lax.axis_size("section") * lax.axis_size("azim")
    chain = ("section", "azim")
    onward = [(i, i + 1) for i in range(rows - 1)]
    backward = [(i + 1, i) for i in range(rows - 1)]
    cores = [(0, 1), (1, 0), (2, 3), (3, 2)]
    far = [(1, 2), (2, 1)]

    payload, region, heat_down, heat_up = pl.pallas_call(
        send_kernel,
        out_shape=(struct(NA, 32, 128), struct(256, 128), struct(NA, 8, 128), struct(NA, 8, 128)),
        in_specs=[VM] * 6,
        out_specs=(VM,) * 4,
        compiler_params=params(16),
        name="send",
    )(
        magnetic_vector_field, fixed_material_map, spinning_material_map,
        slab_slide_offsets.reshape(1, 128), prior_thermal_state, goal_sensitivity,
    )
    heat_prev = lax.ppermute(heat_up, chain, onward)
    heat_next = lax.ppermute(heat_down, chain, backward)
    got = lax.all_to_all(payload, "azim", split_axis=0, concat_axis=0, tiled=True)
    down, up = pl.pallas_call(
        rows_kernel,
        out_shape=(struct(NA, 16, 128), struct(NA, 16, 128)),
        in_specs=[VM],
        out_specs=(VM, VM),
        compiler_params=params(8),
        name="pack_rows",
    )(got)
    from_prev = lax.ppermute(up, chain, onward)
    from_next = lax.ppermute(down, chain, backward)
    heat_args = (got, prior_thermal_state, goal_sensitivity, from_next, from_prev, heat_next, heat_prev)
    edge = pl.pallas_call(
        layers_kernel,
        out_shape=struct(NA, 8, 128),
        in_specs=[VM] * 7,
        out_specs=VM,
        compiler_params=params(8),
        name="pack_layers",
    )(*heat_args)
    edge_core = lax.ppermute(edge, "axial", cores)
    edge_far = lax.ppermute(edge, "axial", far)
    wide = (NA, 16, 256)
    result = pl.pallas_call(
        heat_kernel,
        out_shape=struct(NA, 56, 128),
        in_specs=[VM] * 9 + [SM] * 5,
        out_specs=VM,
        scratch_shapes=[
            pltpu.VMEM((3,) + wide, F32),
            pltpu.VMEM((5,) + wide, F32),
            pltpu.VMEM(wide, F32),
            pltpu.VMEM(wide, F32),
            pltpu.VMEM((6,) + wide, F32),
            pltpu.VMEM((2,) + wide, F32),
            pltpu.VMEM((3, NA, 8, 128), F32),
            pltpu.VMEM((3,) + wide, F32),
            pltpu.VMEM((2,) + wide, F32),
            pltpu.VMEM((2,) + wide, F32),
        ],
        compiler_params=params(32),
        name="heat",
    )(
        *heat_args, edge_core, edge_far,
        inverse_permeability, core_dissipation_coefficient, inplane_thermal_conductance,
        through_plane_conductance, thermal_storage,
    )
    back = lax.all_to_all(result, "azim", split_axis=0, concat_axis=0, tiled=True)
    return pl.pallas_call(
        finish_kernel,
        out_shape=(struct(3, 1, 256, 128), struct(3, 1, 256, 128), struct(1, 256, 128)),
        in_specs=[VM] * 4 + [SM],
        out_specs=(VM,) * 3,
        compiler_params=params(16),
        name="finish",
    )(back, region, magnetic_vector_field, imposed_current_density, electric_conductance)


def solution(mesh):
    in_specs = (
        P(None, "azim", "section", "axial"),
        P(None, "azim", "section", "axial"),
        P("azim", "section", "axial"),
        P(),
        P("axial"),
        P(),
        P(),
        P(),
        P(),
        P(),
        P(),
        P(None, ("section", "azim"), "axial"),
        P(None, ("section", "azim"), "axial"),
    )
    out_specs = (
        P(None, "azim", "section", "axial"),
        P(None, "azim", "section", "axial"),
        P("azim", "section", "axial"),
    )
    return jax.shard_map(body, mesh=mesh, in_specs=in_specs, out_specs=out_specs, check_vma=False)
```

time: 255 us -> 121 us (0.47)
  starting transfers between devices: 103 us -> 20.7 us
  other arithmetic: 79.1 us -> 0 us
  blocking collectives: 0 us -> 62.1 us
  local copies, waits for them, and re-layouts: 44.7 us -> 5.78 us
  Pallas kernels: 0 us -> 24.5 us
  waiting for transfers between devices: 23 us -> 6.07 us
    all_to_all x0 -> x2, blocking collectives: none -> 62.1 us  [the longest x1 36.2 us: body(): lax.all_to_all(result, 'azim', split_axis=0, concat_axis=0, tiled=True)]
    ppermute x22 -> x6, starting transfers between devices: 76.1 us -> 20.7 us  [the longest x1 8.41 us: body(): edge_far = lax.ppermute(edge, 'axial', far)]
    another operation x10 -> x0, other arithmetic: 27 us -> none  [the longest x5 22.6 us: body(): jnp.stack([thermal_rhs, plane_cell, axial_cell, local_thermal_storage])]
    all_to_all x2 -> x0, starting transfers between devices: 26.9 us -> none  [the longest x1 20.2 us: body(): lax.all_to_all(repeat_relaxation_passes, 'azim', split_axis=1, concat_axi...]
    pallas_call x0 -> x5, Pallas kernels: none -> 24.5 us  [the longest x1 19.8 us: body(): pl.pallas_call(heat_kernel, out_shape=struct(NA, 56, 128), in_specs=[VM]...]
    slice x48 -> x0, local copies, waits for them, and re-layouts: 24.1 us -> none  [the longest x10 6.24 us: padded_2(): lax.slice_in_dim(block, 0, width, axis=dim)]
    concatenate x19 -> x0, other arithmetic: 24 us -> none  [the longest x14 23.8 us: padded_2(): block = jnp.concatenate([low, block, high], axis=dim)]
    all_to_all x2 -> x0, waiting for transfers between devices: 19.1 us -> none  [the longest x1 11.7 us: relay_out(): lax.all_to_all(stacked, 'azim', split_axis=2, concat_axis=1, tiled=True)]
  transfers between devices with their start and end apart: 24 -> 6, of which waited for: 5 -> 3; matrix products, arithmetic and copies ran while one was open for 19% -> 0% of each run, Pallas kernels for 0% -> 0%
where the time goes in v1:
time: 121 us; the launch traced here: 120 us
  blocking collectives  62.1 us (51%)
  Pallas kernels  24.5 us (20%)
  starting transfers between devices  20.7 us (17%)
  waiting for transfers between devices  6.07 us (5%)
  local copies, waits for them, and re-layouts  5.78 us (5%)
    all_to_all x1, blocking collectives, body(): lax.all_to_all(result, 'azim', split_axis=0, concat_axis=0, tiled=True)  36.2 us
    all_to_all x1, blocking collectives, body(): lax.all_to_all(payload, 'azim', split_axis=0, concat_axis=0, tiled=True)  26 us
    pallas_call x1, Pallas kernels, body(): pl.pallas_call(heat_kernel, out_shape=struct(NA, 56, 128), in_specs=[VM]...  19.8 us
    ppermute x1, starting transfers between devices, body(): edge_far = lax.ppermute(edge, 'axial', far)  8.41 us
    unnamed x32, local copies, waits for them, and re-layouts  5.78 us
    ppermute x1, starting transfers between devices, body(): from_prev = lax.ppermute(up, chain, onward)  5.48 us
    ppermute x1, starting transfers between devices, body(): heat_prev = lax.ppermute(heat_up, chain, onward)  4.13 us
    ppermute x1, waiting for transfers between devices, body(): edge_far = lax.ppermute(edge, 'axial', far)  3.6 us
  transfers between devices with their start and end apart: 6, of which 3 were waited for; matrix products, arithmetic and copies ran while one was open for 0% of the time, Pallas kernels for 0%

profile of v1, /device:TPU:1, one launch (start us, length us, event | category | flops | bytes accessed | tf_op | source)
XLA Modules:
  0.0 120.0 jit_solution(12990276697330632524)
XLA Ops:
  0.6 0.6 copy-done.9
  1.3 1.0 copy-done
  2.3 0.9 copy-done.2
  3.2 0.9 copy-done.4
  4.1 0.9 copy-done.7
  5.0 0.7 copy-done.8
  5.7 0.2 send.1
  5.9 26.0 %all_to_all.10.got = f32[32,32,128]{2,1,0:T(8,128)S(1)} all-to-all(f32[32,32,128]{2,1,0:T(8,128)S(1)} %get-tuple-element.9), channel_id=1, replica_groups=mesh['section'=2,'azim'=32,'axial'=4] {'azim'}, dimensions={0} | all-to-all | bytes 1048576 | tf_op jit(solution)/shard_map/all_to_all | solution.py:289
  31.9 1.3 %collective-permute-start = (f32[32,16,128]{2,1,0:T(8,128)S(1)}, f32[32,16,128]{2,1,0:T(8,128)S(1)}, u32[]{:S(2)}, u32[]{:S(2)}) collective-permute-start(f32[32,16,128]{2,1,0:T(8,128)S(1)} %get-tuple-element.10), channel_id=1, source_target_pairs={{4,0},{8,4},{12,8},{16,12},{20,16},{24,20},{28,24},{32,28},{36,32}... | collective-permute-start | bytes 786440 | tf_op jit(solution)/shard_map/ppermute | solution.py:299
  33.2 5.5 %collective-permute-start.1 = (f32[32,16,128]{2,1,0:T(8,128)S(1)}, f32[32,16,128]{2,1,0:T(8,128)S(1)}, u32[]{:S(2)}, u32[]{:S(2)}) collective-permute-start(f32[32,16,128]{2,1,0:T(8,128)S(1)} %get-tuple-element.11), channel_id=1, source_target_pairs={{0,4},{4,8},{8,12},{12,16},{16,20},{20,24},{24,28},{28,32},{32,36}... | collective-permute-start | bytes 786440 | tf_op jit(solution)/shard_map/ppermute | solution.py:298
  38.7 1.3 %collective-permute-start.2 = (f32[32,8,128]{2,1,0:T(8,128)S(1)}, f32[32,8,128]{2,1,0:T(8,128)S(1)}, u32[]{:S(2)}, u32[]{:S(2)}) collective-permute-start(f32[32,8,128]{2,1,0:T(8,128)S(1)} %get-tuple-element.12), channel_id=1, source_target_pairs={{4,0},{8,4},{12,8},{16,12},{20,16},{24,20},{28,24},{32,28},{36,32}... | collective-permute-start | bytes 393224 | tf_op jit(solution)/shard_map/ppermute | solution.py:288
  40.0 0.0 copy-start.3
  40.1 4.1 %collective-permute-start.3 = (f32[32,8,128]{2,1,0:T(8,128)S(1)}, f32[32,8,128]{2,1,0:T(8,128)S(1)}, u32[]{:S(2)}, u32[]{:S(2)}) collective-permute-start(f32[32,8,128]{2,1,0:T(8,128)S(1)} %get-tuple-element.13), channel_id=1, source_target_pairs={{0,4},{4,8},{8,12},{12,16},{16,20},{20,24},{24,28},{28,32},{32,36}... | collective-permute-start | bytes 393224 | tf_op jit(solution)/shard_map/ppermute | solution.py:287
  44.2 0.7 collective-permute-done.2.heat_next
  44.9 1.8 %collective-permute-done.3.heat_prev = f32[32,8,128]{2,1,0:T(8,128)S(1)} collective-permute-done((f32[32,8,128]{2,1,0:T(8,128)S(1)}, f32[32,8,128]{2,1,0:T(8,128)S(1)}, u32[]{:S(2)}, u32[]{:S(2)}) %collective-permute-start.3) | collective-permute-done | bytes 131104 | tf_op jit(solution)/shard_map/ppermute | solution.py:287
  46.7 2.6 %pack_layers.1 = f32[32,8,128]{2,1,0:T(8,128)S(1)} custom-call(f32[32,32,128]{2,1,0:T(8,128)S(1)} %all_to_all.10.got, f32[32,8,128]{2,1,0:T(8,128)S(1)} %copy-done.2, f32[32,8,128]{2,1,0:T(8,128)S(1)} %copy-done.4, f32[32,16,128]{2,1,0:T(8,128)S(1)} %collective-permute-done.from_next, f32[32,16,128]{2,1,0:T(8,128)S(1)} %collective-permute-done.1.from_prev, ...), custom_call_target="tpu_custom_call" | custom-call | tf_op jit(solution)/shard_map/pack_layers/pallas_call | solution.py:301
  49.3 8.4 %collective-permute-start.5 = (f32[32,8,128]{2,1,0:T(8,128)S(1)}, f32[32,8,128]{2,1,0:T(8,128)S(1)}, u32[]{:S(2)}, u32[]{:S(2)}) collective-permute-start(f32[32,8,128]{2,1,0:T(8,128)S(1)} %pack_layers.1), channel_id=1, source_target_pairs={{1,2},{2,1},{5,6},{6,5},{9,10},{10,9},{13,14},{14,13},{17,18},{18,... | collective-permute-start | bytes 393224 | tf_op jit(solution)/shard_map/ppermute | solution.py:310
  57.7 0.1 collective-permute-start.4
  57.8 3.6 %collective-permute-done.5.edge_far = f32[32,8,128]{2,1,0:T(8,128)S(1)} collective-permute-done((f32[32,8,128]{2,1,0:T(8,128)S(1)}, f32[32,8,128]{2,1,0:T(8,128)S(1)}, u32[]{:S(2)}, u32[]{:S(2)}) %collective-permute-start.5) | collective-permute-done | bytes 131104 | tf_op jit(solution)/shard_map/ppermute | solution.py:310
  61.5 19.8 %heat.1 = f32[32,56,128]{2,1,0:T(8,128)S(1)} custom-call(f32[32,32,128]{2,1,0:T(8,128)S(1)} %all_to_all.10.got, f32[32,8,128]{2,1,0:T(8,128)S(1)} %copy-done.3, f32[32,8,128]{2,1,0:T(8,128)S(1)} %copy-done.5, f32[32,16,128]{2,1,0:T(8,128)S(1)} %collective-permute-done.from_next, f32[32,16,128]{2,1,0:T(8,128)S(1)} %collective-permute-done.1.from_prev, ...), custom_call_target="tpu_custom_call" | custom-call | tf_op jit(solution)/shard_map/heat/pallas_call | solution.py:312
  81.3 0.0 copy-start.6
  81.3 36.2 %all_to_all.11.got = f32[32,56,128]{2,1,0:T(8,128)S(1)} all-to-all(f32[32,56,128]{2,1,0:T(8,128)S(1)} %heat.1), channel_id=1, replica_groups=mesh['section'=2,'azim'=32,'axial'=4] {'azim'}, dimensions={0} | all-to-all | bytes 1835008 | tf_op jit(solution)/shard_map/all_to_all | solution.py:336
  117.5 0.6 copy-done.15
  118.1 1.9 %finish.1 = (f32[3,1,256,128]{3,2,1,0:T(8,128)}, f32[3,1,256,128]{3,2,1,0:T(8,128)}, f32[1,256,128]{2,1,0:T(8,128)}) custom-call(f32[32,56,128]{2,1,0:T(8,128)S(1)} %all_to_all.11.got, f32[256,128]{1,0:T(8,128)S(1)} %get-tuple-element.14.region, f32[3,1,256,128]{3,2,1,0:T(8,128)S(1)} %copy-done.1, f32[3,1,256,128]{3,2,1,0:T(8,128)S(1)} %copy-done.6, ...), custom_call_target="tpu_custom_call" | custom-call | tf_op jit(solution)/shard_map/finish/pallas_call | solution.py:337
  (27 shorter events, 0.1 us)
Async XLA Ops:
  0.6 0.7 copy-start.9
  1.3 1.0 copy-start
  2.3 0.9 copy-start.2
  3.2 0.9 copy-start.4
  4.1 0.9 copy-start.7
  5.0 0.7 copy-start.8
  31.9 14.8 %collective-permute-start = (f32[32,16,128]{2,1,0:T(8,128)S(1)}, f32[32,16,128]{2,1,0:T(8,128)S(1)}, u32[]{:S(2)}, u32[]{:S(2)}) collective-permute-start(f32[32,16,128]{2,1,0:T(8,128)S(1)} %get-tuple-element.10), channel_id=1, source_target_pairs={{4,0},{8,4},{12,8},{16,12},{20,16},{24,20},{28,24},{32,28},{36,32}... | collective-permute-start | bytes 786440 | tf_op jit(solution)/shard_map/ppermute | solution.py:299
  33.2 13.5 %collective-permute-start.1 = (f32[32,16,128]{2,1,0:T(8,128)S(1)}, f32[32,16,128]{2,1,0:T(8,128)S(1)}, u32[]{:S(2)}, u32[]{:S(2)}) collective-permute-start(f32[32,16,128]{2,1,0:T(8,128)S(1)} %get-tuple-element.11), channel_id=1, source_target_pairs={{0,4},{4,8},{8,12},{12,16},{16,20},{20,24},{24,28},{28,32},{32,36}... | collective-permute-start | bytes 786440 | tf_op jit(solution)/shard_map/ppermute | solution.py:298
  38.7 6.2 %collective-permute-start.2 = (f32[32,8,128]{2,1,0:T(8,128)S(1)}, f32[32,8,128]{2,1,0:T(8,128)S(1)}, u32[]{:S(2)}, u32[]{:S(2)}) collective-permute-start(f32[32,8,128]{2,1,0:T(8,128)S(1)} %get-tuple-element.12), channel_id=1, source_target_pairs={{4,0},{8,4},{12,8},{16,12},{20,16},{24,20},{28,24},{32,28},{36,32}... | collective-permute-start | bytes 393224 | tf_op jit(solution)/shard_map/ppermute | solution.py:288
  40.0 21.4 %copy-start.3 = (f32[32,8,128]{2,1,0:T(8,128)S(1)}, f32[32,8,128]{2,1,0:T(8,128)}, u32[]{:S(2)}) copy-start(f32[32,8,128]{2,1,0:T(8,128)} %prior.5) | copy-start | bytes 393220
  40.0 21.4 %copy-start.5 = (f32[32,8,128]{2,1,0:T(8,128)S(1)}, f32[32,8,128]{2,1,0:T(8,128)}, u32[]{:S(2)}) copy-start(f32[32,8,128]{2,1,0:T(8,128)} %goal.5) | copy-start | bytes 393220
  40.0 21.4 %copy-start.10 = (f32[8]{0:T(128)S(1)}, f32[8]{0:T(128)}, u32[]{:S(2)}) copy-start(f32[8]{0:T(128)} %reluct.1) | copy-start | bytes 100
  40.0 21.4 %copy-start.11 = (f32[8]{0:T(128)S(1)}, f32[8]{0:T(128)}, u32[]{:S(2)}) copy-start(f32[8]{0:T(128)} %loss.1) | copy-start | bytes 100
  40.1 21.4 %copy-start.12 = (f32[8]{0:T(128)S(1)}, f32[8]{0:T(128)}, u32[]{:S(2)}) copy-start(f32[8]{0:T(128)} %plane.1) | copy-start | bytes 100
  40.1 21.4 %copy-start.13 = (f32[8]{0:T(128)S(1)}, f32[8]{0:T(128)}, u32[]{:S(2)}) copy-start(f32[8]{0:T(128)} %axial.1) | copy-start | bytes 100
  40.1 21.4 %copy-start.14 = (f32[8]{0:T(128)S(1)}, f32[8]{0:T(128)}, u32[]{:S(2)}) copy-start(f32[8]{0:T(128)} %storage.1) | copy-start | bytes 100
  40.1 6.6 %collective-permute-start.3 = (f32[32,8,128]{2,1,0:T(8,128)S(1)}, f32[32,8,128]{2,1,0:T(8,128)S(1)}, u32[]{:S(2)}, u32[]{:S(2)}) collective-permute-start(f32[32,8,128]{2,1,0:T(8,128)S(1)} %get-tuple-element.13), channel_id=1, source_target_pairs={{0,4},{4,8},{8,12},{12,16},{16,20},{20,24},{24,28},{28,32},{32,36}... | collective-permute-start | bytes 393224 | tf_op jit(solution)/shard_map/ppermute | solution.py:287
  49.3 12.1 %collective-permute-start.5 = (f32[32,8,128]{2,1,0:T(8,128)S(1)}, f32[32,8,128]{2,1,0:T(8,128)S(1)}, u32[]{:S(2)}, u32[]{:S(2)}) collective-permute-start(f32[32,8,128]{2,1,0:T(8,128)S(1)} %pack_layers.1), channel_id=1, source_target_pairs={{1,2},{2,1},{5,6},{6,5},{9,10},{10,9},{13,14},{14,13},{17,18},{18,... | collective-permute-start | bytes 393224 | tf_op jit(solution)/shard_map/ppermute | solution.py:310
  57.7 3.7 %collective-permute-start.4 = (f32[32,8,128]{2,1,0:T(8,128)S(1)}, f32[32,8,128]{2,1,0:T(8,128)S(1)}, u32[]{:S(2)}, u32[]{:S(2)}) collective-permute-start(f32[32,8,128]{2,1,0:T(8,128)S(1)} %pack_layers.1), channel_id=1, source_target_pairs={{0,1},{1,0},{2,3},{3,2},{4,5},{5,4},{6,7},{7,6},{8,9},{9,8},{10,11... | collective-permute-start | bytes 393224 | tf_op jit(solution)/shard_map/ppermute | solution.py:309
  81.3 36.2 %copy-start.1 = (f32[3,1,256,128]{3,2,1,0:T(8,128)S(1)}, f32[3,1,256,128]{3,2,1,0:T(8,128)}, u32[]{:S(2)}) copy-start(f32[3,1,256,128]{3,2,1,0:T(8,128)} %pot.3) | copy-start | bytes 1179652
  81.3 36.2 %copy-start.6 = (f32[3,1,256,128]{3,2,1,0:T(8,128)S(1)}, f32[3,1,256,128]{3,2,1,0:T(8,128)}, u32[]{:S(2)}) copy-start(f32[3,1,256,128]{3,2,1,0:T(8,128)} %current.1) | copy-start | bytes 1179652
  117.5 0.7 copy-start.15

commit v2 on v1

v2 whole, which is shorter than its diff:
```python
import jax
import jax.numpy as jnp
from jax import lax
from jax.experimental import pallas as pl
from jax.experimental.pallas import tpu as pltpu
from jax.sharding import PartitionSpec as P

NREG = 8
SWEEPS = 4
NA = 32
F32 = jnp.float32
VM = pl.BlockSpec(memory_space=pltpu.VMEM)
SM = pl.BlockSpec(memory_space=pltpu.SMEM)
HBM = pl.BlockSpec(memory_space=pl.ANY)


def params(mib):
    return pltpu.CompilerParams(vmem_limit_bytes=mib * 1024 * 1024)


def struct(*shape):
    return jax.ShapeDtypeStruct(shape, F32)


def sub_low():
    return lax.broadcasted_iota(jnp.int32, (8, 128), 0) < 4


def lanes():
    return lax.broadcasted_iota(jnp.int32, (8, 128), 1)


def put(packed, slot, tile):
    return jnp.where(lanes() // 8 == slot, pltpu.roll(tile, 4 + 8 * slot, 1), packed)


def take(packed, slot):
    lane = lanes()
    return jnp.where((lane < 4) | (lane >= 124), pltpu.roll(packed, 124 - 8 * slot, 1), 0.0)


def lookup(region, tables):
    found = [jnp.zeros(region.shape, F32) for _ in tables]
    for k in range(NREG):
        match = region == float(k + 1)
        found = [jnp.where(match, t[k], f) for t, f in zip(tables, found)]
    return found


def send_kernel(
    pot_in, fixed_in, spin_in, offs_in, prior_in, goal_in,
    region, frame, ring, heat_down, heat_up,
    pot, fixed, spin, offs, prior, goal, sems,
):
    pairs = ((pot_in, pot), (fixed_in, fixed), (spin_in, spin), (offs_in, offs), (prior_in, prior), (goal_in, goal))
    copies = [pltpu.make_async_copy(src, dst, sems.at[n]) for n, (src, dst) in enumerate(pairs)]
    for copy in copies:
        copy.start()
    for copy in copies[1:4]:
        copy.wait()
    section = lax.axis_index("section")
    azim = lax.axis_index("azim")
    shifted = (azim - offs[...]) & (NA - 1)
    rows = lax.broadcasted_iota(jnp.int32, (NA, 128), 0)
    hot = jnp.where(rows == shifted, 1.0, 0.0).astype(jnp.bfloat16)
    rotor = lax.dot_general(
        spin[...].astype(F32).astype(jnp.bfloat16), hot, (((0,), (0,)), ((), ())), preferred_element_type=F32
    )
    stator = fixed[0].astype(F32)
    region[:128] = jnp.where(section == 0, rotor, stator[:128]) + 1.0
    region[128:] = stator[128:] + 1.0
    copies[0].wait()
    low = sub_low()

    def tile(f, t):
        at = pl.ds(8 * t, 8)
        return region[at, :] if f == 3 else pot[f, 0, at, :]

    for f in range(4):
        frame[pl.ds(8 * f, 8), :] = jnp.where(low, tile(f, 0), tile(f, 31))
    for g in range(8):
        packed = jnp.zeros((8, 128), F32)
        for u in range(4):
            for f in range(4):
                packed = put(packed, 4 * u + f, tile(f, 4 * g + u))
        frame[pl.ds(32 + 8 * g, 8), :] = packed
    ring[0] = pot[1, 0]
    ring[1] = pot[2, 0]
    copies[4].wait()
    copies[5].wait()
    for a in range(NA):
        heat_down[a] = jnp.where(low, prior[a], pltpu.roll(goal[a], 4, 0))
        heat_up[a] = jnp.where(low, pltpu.roll(prior[a], 4, 0), goal[a])


def beside(gathered, own, step, count, at):
    index = own + step
    valid = (index >= 0) & (index < count)
    safe = jnp.clip(index, 0, count - 1)
    return jnp.where(valid, gathered[at(safe)], 0.0)


def halo_kernel(frames, halo):
    section = lax.axis_index("section")
    axial = lax.axis_index("axial")
    other = 1 - section
    lane = lanes()
    right = lane % 8 >= 4
    valid = sub_low() == (section == 0)
    for g in range(8):
        at = pl.ds(32 + 8 * g, 8)
        after = beside(frames, axial, 1, 4, lambda b: (4 * section + b, at, slice(None)))
        before = beside(frames, axial, -1, 4, lambda b: (4 * section + b, at, slice(None)))
        halo[g] = jnp.where(right, after, before)
    for f in range(4):
        at = pl.ds(8 * f, 8)
        halo[8 + f] = jnp.where(valid, frames[4 * other + axial, at, :], 0.0)
        after = beside(frames, axial, 1, 4, lambda b: (4 * other + b, at, slice(None)))
        before = beside(frames, axial, -1, 4, lambda b: (4 * other + b, at, slice(None)))
        ends = jnp.where(lane < 4, after, jnp.where(lane >= 124, before, 0.0))
        halo[12 + f] = jnp.where(valid, ends, 0.0)


def heat_tiles(prior, goal, from_next, from_prev, a):
    low = sub_low()
    nxt, prv = from_next[a], from_prev[a]
    return (
        (prior[a], jnp.where(low, nxt, pltpu.roll(prv, 4, 0))),
        (goal[a], jnp.where(low, pltpu.roll(nxt, 4, 0), prv)),
    )


def layers_kernel(prior, goal, from_next, from_prev, edge):
    for g in range(NA // 4):
        packed = jnp.zeros((8, 128), F32)
        for u in range(4):
            tiles = heat_tiles(prior, goal, from_next, from_prev, 4 * g + u)
            for f in range(2):
                for t in range(2):
                    packed = put(packed, 4 * u + 2 * f + t, tiles[f][t])
        edge[g] = packed


def rnext(v):
    return pltpu.roll(v, 15, 0)


def rprev(v):
    return pltpu.roll(v, 1, 0)


def lnext(v):
    return pltpu.roll(v, 255, 1)


def lprev(v):
    return pltpu.roll(v, 1, 1)


def magnetic_kernel(
    pot, region, halo, ring, ring_halo, current, reluct, eddy, loss,
    payload, misfit, weight, hring,
    wide, heat, hfield,
):
    low = sub_low()
    mains = [
        lambda at: pot[0, 0, at, :], lambda at: pot[1, 0, at, :], lambda at: pot[2, 0, at, :],
        lambda at: region[at, :], lambda at: ring[0, at, :], lambda at: ring[1, at, :],
    ]
    left, right = pl.ds(0, 128), pl.ds(128, 128)
    for n in range(6):
        source, f = (halo, n) if n < 4 else (ring_halo, n - 3)
        for t in range(32):
            wide[n, pl.ds(8 + 8 * t, 8), left] = mains[n](pl.ds(8 * t, 8))
            wide[n, pl.ds(8 + 8 * t, 8), right] = take(source[t // 4], 4 * (t % 4) + f)
        for side, block in ((left, source[8 + f]), (right, source[12 + f])):
            wide[n, pl.ds(264, 8), side] = jnp.where(low, block, 0.0)
            wide[n, pl.ds(0, 8), side] = jnp.where(low, 0.0, block)
            wide[n, pl.ds(272, 8), side] = jnp.zeros((8, 128), F32)
    for t in range(34):
        here, ahead = pl.ds(8 * t, 8), pl.ds(8 * t + 1, 8)
        pa, pr, pz = wide[0, here, :], wide[1, here, :], wide[2, here, :]
        fa = (wide[2, ahead, :] - pz) - (lnext(pr) - pr)
        fr = (lnext(pa) - pa) - (wide[5, here, :] - pz)
        fz = (wide[4, here, :] - pr) - (wide[0, ahead, :] - pa)
        rel, dens = lookup(wide[3, here, :], (reluct, loss))
        heat[t] = dens * (fa * fa + fr * fr + fz * fz)
        hfield[0, here, :] = rel * fa
        hfield[1, here, :] = rel * fr
        hfield[2, here, :] = rel * fz
        if 1 <= t <= 32:
            rows = pl.ds(8 * t - 8, 8)
            scale = 2.0 * dens
            for n, f in enumerate((fa, fr, fz)):
                weight[n, rows, :] = (scale * f)[:, :128]
            hring[0, rows, :] = (rel * fr)[:, :128]
            hring[1, rows, :] = (rel * fz)[:, :128]
    for t in range(1, 33):
        here, behind, rows = pl.ds(8 * t, 8), pl.ds(8 * t - 1, 8), pl.ds(8 * t - 8, 8)
        ha, hr, hz = hfield[0, here, :], hfield[1, here, :], hfield[2, here, :]
        ca = (lprev(hr) - hr) - (hfield[2, behind, :] - hz)
        cr = -hz - (lprev(ha) - ha)
        cz = (hfield[0, behind, :] - ha) + hr
        (sigma,) = lookup(region[rows, :], (eddy,))
        for n, c in enumerate((ca, cr, cz)):
            misfit[n, rows, :] = c[:, :128] + (sigma * pot[n, 0, rows, :] - current[n, 0, rows, :])
    for j in range(NA):
        t = j + 1
        packed = jnp.zeros((8, 128), F32)
        tiles = []
        for get in (lambda i: heat[i], lambda i: wide[3, pl.ds(8 * i, 8), :]):
            near, after, before = get(t), get(t + 1), get(t - 1)
            beyond = [jnp.where(low, after[:, k:k + 128], before[:, k:k + 128]) for k in (0, 128)]
            tiles.append((near[:, :128], near[:, 128:]))
            tiles.append(tuple(beyond))
        for c, (main, side) in enumerate(tiles):
            payload[j, pl.ds(8 * c, 8), :] = main
            packed = put(packed, c, side)
        payload[j, pl.ds(32, 8), :] = packed


def heat_kernel(
    got, prior, goal, from_next, from_prev, edges,
    plane, axial, storage, out,
    kin, kax, cap, pri, sens, src, coef, base, temp0, temp1, adj0, adj1,
):
    own = lax.axis_index("axial")
    right = lanes() % 8 >= 4

    def join(tiles, ends):
        return jnp.concatenate([jnp.concatenate(tiles, axis=0), jnp.concatenate(ends, axis=0)], axis=1)

    def gather(g, carry):
        after = beside(edges, own, 1, 4, lambda b: (b, g))
        before = beside(edges, own, -1, 4, lambda b: (b, g))
        merged = jnp.where(right, after, before)
        for u in range(4):
            a = 4 * g + u
            side = got[a, pl.ds(32, 8), :]
            tiles = [got[a, pl.ds(8 * c, 8), :] for c in range(4)]
            ends = [take(side, c) for c in range(4)]
            src[a] = join(tiles[:2], ends[:2])
            kin[a], kax[a], cap[a] = lookup(join(tiles[2:], ends[2:]), (plane, axial, storage))
            held = heat_tiles(prior, goal, from_next, from_prev, a)
            pri[a] = join(held[0], [take(merged, 4 * u + t) for t in range(2)])
            sens[a] = join(held[1], [take(merged, 4 * u + 2 + t) for t in range(2)])
        return carry

    lax.fori_loop(0, NA // 4, gather, 0, unroll=2)

    def prepare(a, carry):
        up = (a + 1) & (NA - 1)
        down = (a - 1) & (NA - 1)
        kp, ka, c = kin[a], kax[a], cap[a]
        source = c * pri[a] + src[a]
        w = [
            0.5 * (kp + kin[up]), 0.5 * (kp + kin[down]),
            0.5 * (kp + rnext(kp)), 0.5 * (kp + rprev(kp)),
            0.5 * (ka + lnext(ka)), 0.5 * (ka + lprev(ka)),
        ]
        total = c + (((((w[0] + w[1]) + w[2]) + w[3]) + w[4]) + w[5])
        inside = c > 0.0
        inv = jnp.where(inside, 1.0 / jnp.where(inside, total, 1.0), 0.0)
        for n in range(6):
            coef[n, a] = inv * w[n]
        base[0, a] = inv * source
        first = inv * sens[a]
        base[1, a] = first
        adj0[a] = first
        return carry

    lax.fori_loop(0, NA, prepare, 0, unroll=8)

    def relax(field, a, c, b):
        up = (a + 1) & (NA - 1)
        down = (a - 1) & (NA - 1)
        v = field[a]
        total = b + c[0] * field[up] + c[1] * field[down]
        total = total + c[2] * rnext(v) + c[3] * rprev(v)
        return total + c[4] * lnext(v) + c[5] * lprev(v)

    temps = [pri, temp0, temp1, temp0, temp1]
    adjs = [None, adj0, adj1, adj0, adj1]
    for sweep in range(SWEEPS):

        def step(a, carry, sweep=sweep):
            c = [coef[n, a] for n in range(6)]
            t = relax(temps[sweep], a, c, base[0, a])
            if sweep == SWEEPS - 1:
                out[a, pl.ds(0, 8), :] = t[:8, :128]
            else:
                temps[sweep + 1][a] = t
            if sweep > 0:
                s = relax(adjs[sweep], a, c, base[1, a])
                if sweep == SWEEPS - 1:
                    out[a, pl.ds(8, 8), :] = s[:8, :128]
                else:
                    adjs[sweep + 1][a] = s
            return carry

        lax.fori_loop(0, NA, step, 0, unroll=8)


def finish_kernel(got, part, weight, hring, misfit, dual, state):
    misfit[0, 0] = part[0]
    misfit[1, 0] = part[1] + hring[1]
    misfit[2, 0] = part[2] - hring[0]

    def step(j, carry):
        at = pl.ds(pl.multiple_of(8 * j, 8), 8)
        state[0, at, :] = got[j, pl.ds(0, 8), :]
        adjoint = got[j, pl.ds(8, 8), :]
        for f in range(3):
            dual[f, 0, at, :] = weight[f, at, :] * adjoint
        return carry

    lax.fori_loop(0, NA, step, 0, unroll=8)


def body(
    magnetic_vector_field,
    imposed_current_density,
    fixed_material_map,
    spinning_material_map,
    slab_slide_offsets,
    inverse_permeability,
    electric_conductance,
    core_dissipation_coefficient,
    inplane_thermal_conductance,
    through_plane_conductance,
    thermal_storage,
    prior_thermal_state,
    goal_sensitivity,
):
    rows = lax.axis_size("section") * lax.axis_size("azim")
    chain = ("section", "azim")
    onward = [(i, i + 1) for i in range(rows - 1)]
    backward = [(i + 1, i) for i in range(rows - 1)]
    from_after = [((i + 1) % NA, i) for i in range(NA)]
    from_before = [(i, (i + 1) % NA) for i in range(NA)]

    region, frame, ring, heat_down, heat_up = pl.pallas_call(
        send_kernel,
        out_shape=(
            struct(256, 128), struct(96, 128), struct(2, 256, 128), struct(NA, 8, 128), struct(NA, 8, 128),
        ),
        in_specs=[HBM] * 6,
        out_specs=(VM,) * 5,
        scratch_shapes=[
            pltpu.VMEM((3, 1, 256, 128), F32),
            pltpu.VMEM((1, 256, 128), jnp.int32),
            pltpu.VMEM((NA, 128), jnp.int32),
            pltpu.VMEM((1, 128), jnp.int32),
            pltpu.VMEM((NA, 8, 128), F32),
            pltpu.VMEM((NA, 8, 128), F32),
            pltpu.SemaphoreType.DMA((6,)),
        ],
        compiler_params=params(62),
        name="send",
    )(
        magnetic_vector_field, fixed_material_map, spinning_material_map,
        slab_slide_offsets.reshape(1, 128), prior_thermal_state, goal_sensitivity,
    )
    frames = lax.all_gather(frame, ("section", "axial"))
    ring_main = lax.ppermute(ring, "azim", from_after)
    heat_prev = lax.ppermute(heat_up, chain, onward)
    heat_next = lax.ppermute(heat_down, chain, backward)
    halo = pl.pallas_call(
        halo_kernel, out_shape=struct(16, 8, 128), in_specs=[VM], out_specs=VM,
        compiler_params=params(8), name="halo",
    )(frames)
    ring_halo = lax.ppermute(halo, "azim", from_after)
    heat_args = (prior_thermal_state, goal_sensitivity, heat_next, heat_prev)
    edge = pl.pallas_call(
        layers_kernel, out_shape=struct(8, 8, 128), in_specs=[VM] * 4, out_specs=VM,
        compiler_params=params(8), name="layers",
    )(*heat_args)
    edges = lax.all_gather(edge, "axial")
    payload, part, weight, hring = pl.pallas_call(
        magnetic_kernel,
        out_shape=(struct(NA, 40, 128), struct(3, 256, 128), struct(3, 256, 128), struct(2, 256, 128)),
        in_specs=[VM] * 6 + [SM] * 3,
        out_specs=(VM,) * 4,
        scratch_shapes=[
            pltpu.VMEM((6, 280, 256), F32),
            pltpu.VMEM((34, 8, 256), F32),
            pltpu.VMEM((3, 272, 256), F32),
        ],
        compiler_params=params(24),
        name="magnetic",
    )(
        magnetic_vector_field, region, halo, ring_main, ring_halo, imposed_current_density,
        inverse_permeability, electric_conductance, core_dissipation_coefficient,
    )
    got = lax.all_to_all(payload, "azim", split_axis=0, concat_axis=0, tiled=True)
    hring = lax.ppermute(hring, "azim", from_before)
    wide = pltpu.VMEM((NA, 16, 256), F32)
    result = pl.pallas_call(
        heat_kernel,
        out_shape=struct(NA, 16, 128),
        in_specs=[VM] * 6 + [SM] * 3,
        out_specs=VM,
        scratch_shapes=[
            wide, wide, wide, wide, wide, wide,
            pltpu.VMEM((6, NA, 16, 256), F32),
            pltpu.VMEM((2, NA, 16, 256), F32),
            wide, wide, wide, wide,
        ],
        compiler_params=params(32),
        name="heat",
    )(
        got, *heat_args, edges,
        inplane_thermal_conductance, through_plane_conductance, thermal_storage,
    )
    back = lax.all_to_all(result, "azim", split_axis=0, concat_axis=0, tiled=True)
    return pl.pallas_call(
        finish_kernel,
        out_shape=(struct(3, 1, 256, 128), struct(3, 1, 256, 128), struct(1, 256, 128)),
        in_specs=[VM] * 4,
        out_specs=(VM,) * 3,
        compiler_params=params(16),
        name="finish",
    )(back, part, weight, hring)


def solution(mesh):
    in_specs = (
        P(None, "azim", "section", "axial"),
        P(None, "azim", "section", "axial"),
        P("azim", "section", "axial"),
        P(),
        P("axial"),
        P(),
        P(),
        P(),
        P(),
        P(),
        P(),
        P(None, ("section", "azim"), "axial"),
        P(None, ("section", "azim"), "axial"),
    )
    out_specs = (
        P(None, "azim", "section", "axial"),
        P(None, "azim", "section", "axial"),
        P("azim", "section", "axial"),
    )
    return jax.shard_map(body, mesh=mesh, in_specs=in_specs, out_specs=out_specs, check_vma=False)
```

time: 121 us -> 99.5 us (0.82)
  blocking collectives: 62.1 us -> 24.3 us
  waiting for transfers between devices: 6.07 us -> 30.5 us
  Pallas kernels: 24.5 us -> 11.7 us
  starting transfers between devices: 20.7 us -> 30.2 us
  local copies, waits for them, and re-layouts: 5.78 us -> 1.62 us
    all_to_all x2 -> x0, blocking collectives: 62.1 us -> none  [the longest x1 36.2 us: body(): lax.all_to_all(result, 'azim', split_axis=0, concat_axis=0, tiled=True)]
    all_gather x0 -> x2, blocking collectives: none -> 24.3 us  [the longest x1 15.7 us: body(): frames = lax.all_gather(frame, ('section', 'axial'))]
    ppermute x4 -> x3, waiting for transfers between devices: 3.6 us -> 17.8 us  [the longest x1 15 us: body(): hring = lax.ppermute(hring, 'azim', from_before)]
    all_to_all x0 -> x2, starting transfers between devices: none -> 14.1 us  [the longest x1 8.23 us: body(): lax.all_to_all(result, 'azim', split_axis=0, concat_axis=0, tiled=True)]
    ppermute x1, waiting for transfers between devices: 0.71 us -> 12.7 us  [body(): heat_next = lax.ppermute(heat_down, chain, backward)]
    pallas_call x4 -> x5, Pallas kernels: 22.6 us -> 10.7 us  [the longest x1 5.61 us: body(): pl.pallas_call(heat_kernel, out_shape=struct(NA, 16, 128), in_specs=[VM]...]
    ppermute x4 -> x3, starting transfers between devices: 15.3 us -> 10.8 us  [the longest x1 8.68 us: body(): ring_main = lax.ppermute(ring, 'azim', from_after)]
    unnamed x32 -> x26, local copies, waits for them, and re-layouts: 5.78 us -> 1.62 us
  transfers between devices with their start and end apart: 6 -> 7, of which waited for: 3 -> 3; matrix products, arithmetic and copies ran while one was open for 0% -> 0% of each run, Pallas kernels for 0% -> 0%
where the time goes in v2:
time: 99.5 us; the launch traced here: 99.1 us
  waiting for transfers between devices  30.5 us (31%)
  starting transfers between devices  30.2 us (30%)
  blocking collectives  24.3 us (24%)
  Pallas kernels  11.7 us (12%)
  local copies, waits for them, and re-layouts  1.62 us (2%)
    all_gather x1, blocking collectives, body(): frames = lax.all_gather(frame, ('section', 'axial'))  15.7 us
    ppermute x1, waiting for transfers between devices, body(): hring = lax.ppermute(hring, 'azim', from_before)  15 us
    ppermute x1, waiting for transfers between devices, body(): heat_next = lax.ppermute(heat_down, chain, backward)  12.7 us
    ppermute x1, starting transfers between devices, body(): ring_main = lax.ppermute(ring, 'azim', from_after)  8.68 us
    all_gather x1, blocking collectives, body(): edges = lax.all_gather(edge, 'axial')  8.65 us
    all_to_all x1, starting transfers between devices, body(): lax.all_to_all(result, 'azim', split_axis=0, concat_axis=0, tiled=True)  8.23 us
    all_to_all x1, starting transfers between devices, body(): lax.all_to_all(payload, 'azim', split_axis=0, concat_axis=0, tiled=True)  5.86 us
    pallas_call x1, Pallas kernels, body(): pl.pallas_call(heat_kernel, out_shape=struct(NA, 16, 128), in_specs=[VM]...  5.61 us
  transfers between devices with their start and end apart: 7, of which 3 were waited for; matrix products, arithmetic and copies ran while one was open for 0% of the time, Pallas kernels for 0%

profile of v2, /device:TPU:1, one launch (start us, length us, event | category | flops | bytes accessed | tf_op | source)
XLA Modules:
  0.0 99.1 jit_solution(7621659057659569276)
XLA Ops:
  0.6 2.3 %send.1 = (f32[256,128]{1,0:T(8,128)}, f32[96,128]{1,0:T(8,128)}, f32[2,256,128]{2,1,0:T(8,128)}, f32[32,8,128]{2,1,0:T(8,128)}, f32[32,8,128]{2,1,0:T(8,128)}) custom-call(f32[3,1,256,128]{3,2,1,0:T(8,128)} %pot.1, s32[1,256,128]{2,1,0:T(8,128)} %fixed_in.1, s32[32,128]{1,0:T(8,128)} %spin_in.1, s32[1,128]{1,0:T(1,128)} %bitcast.5, f32[32,8,128]{2,1,0:T(8,128)} %prior.3, ...), custom_call_target="tpu_custom_call" | custom-call | tf_op jit(solution)/shard_map/send/pallas_call | solution.py:342
  3.0 8.7 %collective-permute-start = (f32[2,256,128]{2,1,0:T(8,128)}, f32[2,256,128]{2,1,0:T(8,128)S(1)}, u32[]{:S(2)}, u32[]{:S(2)}) collective-permute-start(f32[2,256,128]{2,1,0:T(8,128)} %get-tuple-element.14), channel_id=1, source_target_pairs={{4,0},{8,4},{12,8},{16,12},{20,16},{24,20},{28,24},{32,28},{36,32}... | collective-permute-start | bytes 786440 | tf_op jit(solution)/shard_map/ppermute | solution.py:365
  11.6 15.7 %all-gather = f32[768,128]{1,0:T(8,128)S(1)} all-gather(f32[96,128]{1,0:T(8,128)} %get-tuple-element.13), channel_id=2, replica_groups=mesh['section'=2,'azim'=32,'axial'=4] {'section','axial'}, dimensions={0}, use_global_device_ids=true | all-gather | bytes 442368 | tf_op jit(solution)/shard_map/all_gather | solution.py:364
  27.3 0.0 copy-start.8
  27.3 0.0 copy-start.9
  27.4 0.8 collective-permute-start.1
  28.2 2.8 %collective-permute-done.1.ring_halo = f32[16,8,128]{2,1,0:T(8,128)S(1)} collective-permute-done((f32[16,8,128]{2,1,0:T(8,128)S(1)}, f32[16,8,128]{2,1,0:T(8,128)S(1)}, u32[]{:S(2)}, u32[]{:S(2)}) %collective-permute-start.1) | collective-permute-done | bytes 65568 | tf_op jit(solution)/shard_map/ppermute | solution.py:372
  31.0 0.0 copy-start.4
  31.0 0.9 copy-done.4
  31.9 2.6 %magnetic.1 = (f32[32,40,128]{2,1,0:T(8,128)}, f32[3,256,128]{2,1,0:T(8,128)S(1)}, f32[3,256,128]{2,1,0:T(8,128)S(1)}, f32[2,256,128]{2,1,0:T(8,128)S(1)}) custom-call(f32[3,1,256,128]{3,2,1,0:T(8,128)S(1)} %copy-done, f32[256,128]{1,0:T(8,128)S(1)} %copy-done.4, f32[16,8,128]{2,1,0:T(8,128)S(1)} %halo.1, f32[2,256,128]{2,1,0:T(8,128)S(1)} %collective-permute-done.ring, ...), custom_call_target="tpu_custom_call" | custom-call | tf_op jit(solution)/shard_map/magnetic/pallas_call | solution.py:379
  34.5 5.9 %all-to-all-start = ((f32[32,40,128]{2,1,0:T(8,128)}), f32[32,40,128]{2,1,0:T(8,128)S(1)}, u32[]{:S(2)}, u32[]{:S(2)}) async-start(f32[32,40,128]{2,1,0:T(8,128)} %get-tuple-element.15), calls=%async_computation | async-start | bytes 1310720 | tf_op jit(solution)/shard_map/all_to_all | solution.py:395
  40.4 1.3 %collective-permute-start.2 = (f32[32,8,128]{2,1,0:T(8,128)S(1)}, f32[32,8,128]{2,1,0:T(8,128)S(1)}, u32[]{:S(2)}, u32[]{:S(2)}) collective-permute-start(f32[32,8,128]{2,1,0:T(8,128)S(1)} %copy-done.12), channel_id=1, source_target_pairs={{4,0},{8,4},{12,8},{16,12},{20,16},{24,20},{28,24},{32,28},{36,32}... | collective-permute-start | bytes 393224 | tf_op jit(solution)/shard_map/ppermute | solution.py:367
  41.7 4.0 %collective-permute-start.3 = (f32[32,8,128]{2,1,0:T(8,128)S(1)}, f32[32,8,128]{2,1,0:T(8,128)S(1)}, u32[]{:S(2)}, u32[]{:S(2)}) collective-permute-start(f32[32,8,128]{2,1,0:T(8,128)S(1)} %copy-done.11), channel_id=1, source_target_pairs={{0,4},{4,8},{8,12},{12,16},{16,20},{20,24},{24,28},{28,32},{32,36}... | collective-permute-start | bytes 393224 | tf_op jit(solution)/shard_map/ppermute | solution.py:366
  45.7 12.7 %collective-permute-done.2.from_next = f32[32,8,128]{2,1,0:T(8,128)S(1)} collective-permute-done((f32[32,8,128]{2,1,0:T(8,128)S(1)}, f32[32,8,128]{2,1,0:T(8,128)S(1)}, u32[]{:S(2)}, u32[]{:S(2)}) %collective-permute-start.2) | collective-permute-done | bytes 131104 | tf_op jit(solution)/shard_map/ppermute | solution.py:367
  58.4 0.2 layers.1
  58.6 8.7 %all-gather.1 = f32[32,8,128]{2,1,0:T(8,128)S(1)} all-gather(f32[8,8,128]{2,1,0:T(8,128)S(1)} %layers.1), channel_id=3, replica_groups=mesh['section'=2,'azim'=32,'axial'=4] {'axial'}, dimensions={0}, use_global_device_ids=true | all-gather | bytes 163840 | tf_op jit(solution)/shard_map/all_gather | solution.py:378
  67.3 0.6 copy-done.5
  67.9 0.0 copy-done.6
  67.9 0.0 copy-done.7
  67.9 5.6 %heat.1 = f32[32,16,128]{2,1,0:T(8,128)} custom-call(f32[32,40,128]{2,1,0:T(8,128)S(1)} %all-to-all-done.got, f32[32,8,128]{2,1,0:T(8,128)S(1)} %copy-done.1, f32[32,8,128]{2,1,0:T(8,128)S(1)} %copy-done.2, f32[32,8,128]{2,1,0:T(8,128)S(1)} %collective-permute-done.2.from_next, f32[32,8,128]{2,1,0:T(8,128)S(1)} %collective-permute-done.3.from_prev, ...), custom_call_target="tpu_custom_call" | custom-call | tf_op jit(solution)/shard_map/heat/pallas_call | solution.py:398
  73.5 8.2 %all-to-all-start.1 = ((f32[32,16,128]{2,1,0:T(8,128)}), f32[32,16,128]{2,1,0:T(8,128)S(1)}, u32[]{:S(2)}, u32[]{:S(2)}) async-start(f32[32,16,128]{2,1,0:T(8,128)} %heat.1), calls=%async_computation.1 | async-start | bytes 524288 | tf_op jit(solution)/shard_map/all_to_all | solution.py:415
  81.8 1.3 %collective-permute-start.4 = (f32[2,256,128]{2,1,0:T(8,128)S(1)}, f32[2,256,128]{2,1,0:T(8,128)S(1)}, u32[]{:S(2)}, u32[]{:S(2)}) collective-permute-start(f32[2,256,128]{2,1,0:T(8,128)S(1)} %get-tuple-element.20), channel_id=1, source_target_pairs={{0,4},{4,8},{8,12},{12,16},{16,20},{20,24},{24,28},{28,32},{32,36}... | collective-permute-start | bytes 786440 | tf_op jit(solution)/shard_map/ppermute | solution.py:396
  83.1 15.0 %collective-permute-done.4.hring = f32[2,256,128]{2,1,0:T(8,128)S(1)} collective-permute-done((f32[2,256,128]{2,1,0:T(8,128)S(1)}, f32[2,256,128]{2,1,0:T(8,128)S(1)}, u32[]{:S(2)}, u32[]{:S(2)}) %collective-permute-start.4) | collective-permute-done | bytes 262176 | tf_op jit(solution)/shard_map/ppermute | solution.py:396
  98.1 1.0 %finish.1 = (f32[3,1,256,128]{3,2,1,0:T(8,128)}, f32[3,1,256,128]{3,2,1,0:T(8,128)}, f32[1,256,128]{2,1,0:T(8,128)}) custom-call(f32[32,16,128]{2,1,0:T(8,128)S(1)} %all-to-all-done.1.got, f32[3,256,128]{2,1,0:T(8,128)S(1)} %get-tuple-element.18.part, f32[3,256,128]{2,1,0:T(8,128)S(1)} %get-tuple-element.19.weight, ...), custom_call_target="tpu_custom_call" | custom-call | tf_op jit(solution)/shard_map/finish/pallas_call | solution.py:416
  (24 shorter events, 0.1 us)
Async XLA Ops:
  3.0 28.0 %collective-permute-start = (f32[2,256,128]{2,1,0:T(8,128)}, f32[2,256,128]{2,1,0:T(8,128)S(1)}, u32[]{:S(2)}, u32[]{:S(2)}) collective-permute-start(f32[2,256,128]{2,1,0:T(8,128)} %get-tuple-element.14), channel_id=1, source_target_pairs={{4,0},{8,4},{12,8},{16,12},{20,16},{24,20},{28,24},{32,28},{36,32}... | collective-permute-start | bytes 786440 | tf_op jit(solution)/shard_map/ppermute | solution.py:365
  11.6 19.3 %copy-start = (f32[3,1,256,128]{3,2,1,0:T(8,128)S(1)}, f32[3,1,256,128]{3,2,1,0:T(8,128)}, u32[]{:S(2)}) copy-start(f32[3,1,256,128]{3,2,1,0:T(8,128)} %pot.1) | copy-start | bytes 1179652
  11.6 19.3 %copy-start.3 = (f32[3,1,256,128]{3,2,1,0:T(8,128)S(1)}, f32[3,1,256,128]{3,2,1,0:T(8,128)}, u32[]{:S(2)}) copy-start(f32[3,1,256,128]{3,2,1,0:T(8,128)} %current.1) | copy-start | bytes 1179652
  27.3 3.7 %copy-start.8 = (f32[8]{0:T(128)S(1)}, f32[8]{0:T(128)}, u32[]{:S(2)}) copy-start(f32[8]{0:T(128)} %reluct.1) | copy-start | bytes 100
  27.3 3.7 %copy-start.9 = (f32[8]{0:T(128)S(1)}, f32[8]{0:T(128)}, u32[]{:S(2)}) copy-start(f32[8]{0:T(128)} %eddy.1) | copy-start | bytes 100
  27.3 3.7 %copy-start.10 = (f32[8]{0:T(128)S(1)}, f32[8]{0:T(128)}, u32[]{:S(2)}) copy-start(f32[8]{0:T(128)} %loss.1) | copy-start | bytes 100
  27.4 3.6 %collective-permute-start.1 = (f32[16,8,128]{2,1,0:T(8,128)S(1)}, f32[16,8,128]{2,1,0:T(8,128)S(1)}, u32[]{:S(2)}, u32[]{:S(2)}) collective-permute-start(f32[16,8,128]{2,1,0:T(8,128)S(1)} %halo.1), channel_id=1, source_target_pairs={{4,0},{8,4},{12,8},{16,12},{20,16},{24,20},{28,24},{32,28},{36,32}... | collective-permute-start | bytes 196616 | tf_op jit(solution)/shard_map/ppermute | solution.py:372
  31.0 0.9 copy-start.4
  34.5 5.9 %copy-start.12 = (f32[32,8,128]{2,1,0:T(8,128)S(1)}, f32[32,8,128]{2,1,0:T(8,128)}, u32[]{:S(2)}) copy-start(f32[32,8,128]{2,1,0:T(8,128)} %get-tuple-element.16) | copy-start | bytes 393220
  34.5 7.2 %copy-start.11 = (f32[32,8,128]{2,1,0:T(8,128)S(1)}, f32[32,8,128]{2,1,0:T(8,128)}, u32[]{:S(2)}) copy-start(f32[32,8,128]{2,1,0:T(8,128)} %get-tuple-element.17) | copy-start | bytes 393220
  34.5 23.9 %copy-start.1 = (f32[32,8,128]{2,1,0:T(8,128)S(1)}, f32[32,8,128]{2,1,0:T(8,128)}, u32[]{:S(2)}) copy-start(f32[32,8,128]{2,1,0:T(8,128)} %prior.3) | copy-start | bytes 393220
  34.5 23.9 %copy-start.2 = (f32[32,8,128]{2,1,0:T(8,128)S(1)}, f32[32,8,128]{2,1,0:T(8,128)}, u32[]{:S(2)}) copy-start(f32[32,8,128]{2,1,0:T(8,128)} %goal.3) | copy-start | bytes 393220
  34.5 32.7 %all-to-all-start = ((f32[32,40,128]{2,1,0:T(8,128)}), f32[32,40,128]{2,1,0:T(8,128)S(1)}, u32[]{:S(2)}, u32[]{:S(2)}) async-start(f32[32,40,128]{2,1,0:T(8,128)} %get-tuple-element.15), calls=%async_computation | async-start | bytes 1310720 | tf_op jit(solution)/shard_map/all_to_all | solution.py:395
  40.4 18.0 %collective-permute-start.2 = (f32[32,8,128]{2,1,0:T(8,128)S(1)}, f32[32,8,128]{2,1,0:T(8,128)S(1)}, u32[]{:S(2)}, u32[]{:S(2)}) collective-permute-start(f32[32,8,128]{2,1,0:T(8,128)S(1)} %copy-done.12), channel_id=1, source_target_pairs={{4,0},{8,4},{12,8},{16,12},{20,16},{24,20},{28,24},{32,28},{36,32}... | collective-permute-start | bytes 393224 | tf_op jit(solution)/shard_map/ppermute | solution.py:367
  41.7 16.7 %collective-permute-start.3 = (f32[32,8,128]{2,1,0:T(8,128)S(1)}, f32[32,8,128]{2,1,0:T(8,128)S(1)}, u32[]{:S(2)}, u32[]{:S(2)}) collective-permute-start(f32[32,8,128]{2,1,0:T(8,128)S(1)} %copy-done.11), channel_id=1, source_target_pairs={{0,4},{4,8},{8,12},{12,16},{16,20},{20,24},{24,28},{28,32},{32,36}... | collective-permute-start | bytes 393224 | tf_op jit(solution)/shard_map/ppermute | solution.py:366
  67.2 0.7 copy-start.5
  67.2 0.7 copy-start.6
  67.2 0.7 copy-start.7
  73.5 24.6 %all-to-all-start.1 = ((f32[32,16,128]{2,1,0:T(8,128)}), f32[32,16,128]{2,1,0:T(8,128)S(1)}, u32[]{:S(2)}, u32[]{:S(2)}) async-start(f32[32,16,128]{2,1,0:T(8,128)} %heat.1), calls=%async_computation.1 | async-start | bytes 524288 | tf_op jit(solution)/shard_map/all_to_all | solution.py:415
  81.8 16.3 %collective-permute-start.4 = (f32[2,256,128]{2,1,0:T(8,128)S(1)}, f32[2,256,128]{2,1,0:T(8,128)S(1)}, u32[]{:S(2)}, u32[]{:S(2)}) collective-permute-start(f32[2,256,128]{2,1,0:T(8,128)S(1)} %get-tuple-element.20), channel_id=1, source_target_pairs={{0,4},{4,8},{8,12},{12,16},{16,20},{20,24},{24,28},{28,32},{32,36}... | collective-permute-start | bytes 786440 | tf_op jit(solution)/shard_map/ppermute | solution.py:396

commit v3 on v2

--- a/solution.py
+++ b/solution.py
@@ -47,10 +47,24 @@
     return found
 
 
+def find_region(fixed, spin, offs, region):
+    section = lax.axis_index("section")
+    azim = lax.axis_index("azim")
+    shifted = (azim - offs[...]) & (NA - 1)
+    rows = lax.broadcasted_iota(jnp.int32, (NA, 128), 0)
+    hot = jnp.where(rows == shifted, 1.0, 0.0).astype(jnp.bfloat16)
+    rotor = lax.dot_general(
+        spin[...].astype(F32).astype(jnp.bfloat16), hot, (((0,), (0,)), ((), ())), preferred_element_type=F32
+    )
+    stator = fixed[0].astype(F32)
+    region[:128] = jnp.where(section == 0, rotor, stator[:128]) + 1.0
+    region[128:] = stator[128:] + 1.0
+
+
 def send_kernel(
     pot_in, fixed_in, spin_in, offs_in, prior_in, goal_in,
-    region, frame, ring, heat_down, heat_up,
-    pot, fixed, spin, offs, prior, goal, sems,
+    row_edge, frame, ring,
+    pot, fixed, spin, offs, prior, goal, region, sems,
 ):
     pairs = ((pot_in, pot), (fixed_in, fixed), (spin_in, spin), (offs_in, offs), (prior_in, prior), (goal_in, goal))
     copies = [pltpu.make_async_copy(src, dst, sems.at[n]) for n, (src, dst) in enumerate(pairs)]
@@ -58,17 +72,7 @@
         copy.start()
     for copy in copies[1:4]:
         copy.wait()
-    section = lax.axis_index("section")
-    azim = lax.axis_index("azim")
-    shifted = (azim - offs[...]) & (NA - 1)
-    rows = lax.broadcasted_iota(jnp.int32, (NA, 128), 0)
-    hot = jnp.where(rows == shifted, 1.0, 0.0).astype(jnp.bfloat16)
-    rotor = lax.dot_general(
-        spin[...].astype(F32).astype(jnp.bfloat16), hot, (((0,), (0,)), ((), ())), preferred_element_type=F32
-    )
-    stator = fixed[0].astype(F32)
-    region[:128] = jnp.where(section == 0, rotor, stator[:128]) + 1.0
-    region[128:] = stator[128:] + 1.0
+    find_region(fixed, spin, offs, region)
     copies[0].wait()
     low = sub_low()
 
@@ -77,48 +81,53 @@
         return region[at, :] if f == 3 else pot[f, 0, at, :]
 
     for f in range(4):
-        frame[pl.ds(8 * f, 8), :] = jnp.where(low, tile(f, 0), tile(f, 31))
+        row_edge[f] = jnp.where(low, tile(f, 0), tile(f, 31))
     for g in range(8):
         packed = jnp.zeros((8, 128), F32)
         for u in range(4):
             for f in range(4):
                 packed = put(packed, 4 * u + f, tile(f, 4 * g + u))
-        frame[pl.ds(32 + 8 * g, 8), :] = packed
+        frame[g] = packed
     ring[0] = pot[1, 0]
     ring[1] = pot[2, 0]
     copies[4].wait()
     copies[5].wait()
+    for g in range(4):
+        packed = jnp.zeros((8, 128), F32)
+        for u in range(8):
+            packed = put(packed, 2 * u, prior[8 * g + u])
+            packed = put(packed, 2 * u + 1, goal[8 * g + u])
+        frame[8 + g] = packed
+
+
+def frame_kernel(frame, across, out):
+    valid = sub_low() == (lax.axis_index("section") == 0)
+    for g in range(12):
+        out[g] = frame[g]
+    for f in range(4):
+        out[12 + f] = jnp.where(valid, across[f], 0.0)
+
+
+def halo_kernel(own, core, far, prior, goal, halo, heat_down, heat_up):
+    odd = lax.axis_index("axial") % 2 == 1
+    lane = lanes()
+    low = sub_low()
+    right = lane % 8 >= 4
+    for g in range(16):
+        after = jnp.where(odd, far[g], core[g])
+        before = jnp.where(odd, core[g], far[g])
+        if g < 8:
+            halo[g] = jnp.where(right, after, before)
+        elif g < 12:
+            merged = jnp.where(right, after, before)
+            heat_down[24 + g] = merged
+            heat_up[24 + g] = merged
+        else:
+            halo[g - 4] = own[g]
+            halo[g] = jnp.where(lane < 4, after, jnp.where(lane >= 124, before, 0.0))
     for a in range(NA):
         heat_down[a] = jnp.where(low, prior[a], pltpu.roll(goal[a], 4, 0))
         heat_up[a] = jnp.where(low, pltpu.roll(prior[a], 4, 0), goal[a])
-
-
-def beside(gathered, own, step, count, at):
-    index = own + step
-    valid = (index >= 0) & (index < count)
-    safe = jnp.clip(index, 0, count - 1)
-    return jnp.where(valid, gathered[at(safe)], 0.0)
-
-
-def halo_kernel(frames, halo):
-    section = lax.axis_index("section")
-    axial = lax.axis_index("axial")
-    other = 1 - section
-    lane = lanes()
-    right = lane % 8 >= 4
-    valid = sub_low() == (section == 0)
-    for g in range(8):
-        at = pl.ds(32 + 8 * g, 8)
-        after = beside(frames, axial, 1, 4, lambda b: (4 * section + b, at, slice(None)))
-        before = beside(frames, axial, -1, 4, lambda b: (4 * section + b, at, slice(None)))
-        halo[g] = jnp.where(right, after, before)
-    for f in range(4):
-        at = pl.ds(8 * f, 8)
-        halo[8 + f] = jnp.where(valid, frames[4 * other + axial, at, :], 0.0)
-        after = beside(frames, axial, 1, 4, lambda b: (4 * other + b, at, slice(None)))
-        before = beside(frames, axial, -1, 4, lambda b: (4 * other + b, at, slice(None)))
-        ends = jnp.where(lane < 4, after, jnp.where(lane >= 124, before, 0.0))
-        halo[12 + f] = jnp.where(valid, ends, 0.0)
 
 
 def heat_tiles(prior, goal, from_next, from_prev, a):
@@ -130,17 +139,6 @@
     )
 
 
-def layers_kernel(prior, goal, from_next, from_prev, edge):
-    for g in range(NA // 4):
-        packed = jnp.zeros((8, 128), F32)
-        for u in range(4):
-            tiles = heat_tiles(prior, goal, from_next, from_prev, 4 * g + u)
-            for f in range(2):
-                for t in range(2):
-                    packed = put(packed, 4 * u + 2 * f + t, tiles[f][t])
-        edge[g] = packed
-
-
 def rnext(v):
     return pltpu.roll(v, 15, 0)
 
@@ -158,10 +156,11 @@
 
 
 def magnetic_kernel(
-    pot, region, halo, ring, ring_halo, current, reluct, eddy, loss,
+    pot, fixed, spin, offs, halo, ring, ring_halo, current, reluct, eddy, loss,
     payload, misfit, weight, hring,
-    wide, heat, hfield,
+    wide, heat, hfield, region,
 ):
+    find_region(fixed, spin, offs, region)
     low = sub_low()
     mains = [
         lambda at: pot[0, 0, at, :], lambda at: pot[1, 0, at, :], lambda at: pot[2, 0, at, :],
@@ -220,33 +219,31 @@
 
 
 def heat_kernel(
-    got, prior, goal, from_next, from_prev, edges,
+    got, prior, goal, from_next, from_prev, sides,
     plane, axial, storage, out,
     kin, kax, cap, pri, sens, src, coef, base, temp0, temp1, adj0, adj1,
 ):
-    own = lax.axis_index("axial")
-    right = lanes() % 8 >= 4
+    low = sub_low()
 
     def join(tiles, ends):
         return jnp.concatenate([jnp.concatenate(tiles, axis=0), jnp.concatenate(ends, axis=0)], axis=1)
 
     def gather(g, carry):
-        after = beside(edges, own, 1, 4, lambda b: (b, g))
-        before = beside(edges, own, -1, 4, lambda b: (b, g))
-        merged = jnp.where(right, after, before)
-        for u in range(4):
-            a = 4 * g + u
+        inner = sides[NA + g]
+        outer = jnp.where(low, from_next[NA + g], from_prev[NA + g])
+        for u in range(8):
+            a = 8 * g + u
             side = got[a, pl.ds(32, 8), :]
             tiles = [got[a, pl.ds(8 * c, 8), :] for c in range(4)]
             ends = [take(side, c) for c in range(4)]
             src[a] = join(tiles[:2], ends[:2])
             kin[a], kax[a], cap[a] = lookup(join(tiles[2:], ends[2:]), (plane, axial, storage))
             held = heat_tiles(prior, goal, from_next, from_prev, a)
-            pri[a] = join(held[0], [take(merged, 4 * u + t) for t in range(2)])
-            sens[a] = join(held[1], [take(merged, 4 * u + 2 + t) for t in range(2)])
+            pri[a] = join(held[0], [take(inner, 2 * u), take(outer, 2 * u)])
+            sens[a] = join(held[1], [take(inner, 2 * u + 1), take(outer, 2 * u + 1)])
         return carry
 
-    lax.fori_loop(0, NA // 4, gather, 0, unroll=2)
+    lax.fori_loop(0, NA // 8, gather, 0)
 
     def prepare(a, carry):
         up = (a + 1) & (NA - 1)
@@ -269,7 +266,7 @@
         adj0[a] = first
         return carry
 
-    lax.fori_loop(0, NA, prepare, 0, unroll=8)
+    lax.fori_loop(0, NA, prepare, 0, unroll=16)
 
     def relax(field, a, c, b):
         up = (a + 1) & (NA - 1)
@@ -298,7 +295,7 @@
                     adjs[sweep + 1][a] = s
             return carry
 
-        lax.fori_loop(0, NA, step, 0, unroll=8)
+        lax.fori_loop(0, NA, step, 0, unroll=32)
 
 
 def finish_kernel(got, part, weight, hring, misfit, dual, state):
@@ -339,13 +336,13 @@
     from_after = [((i + 1) % NA, i) for i in range(NA)]
     from_before = [(i, (i + 1) % NA) for i in range(NA)]
 
-    region, frame, ring, heat_down, heat_up = pl.pallas_call(
+    offsets = slab_slide_offsets.reshape(1, 128)
+    maps = (fixed_material_map, spinning_material_map, offsets)
+    row_edge, frame, ring = pl.pallas_call(
         send_kernel,
-        out_shape=(
-            struct(256, 128), struct(96, 128), struct(2, 256, 128), struct(NA, 8, 128), struct(NA, 8, 128),
-        ),
+        out_shape=(pltpu.VMEM((4, 8, 128), F32), pltpu.VMEM((12, 8, 128), F32), pltpu.VMEM((2, 256, 128), F32)),
         in_specs=[HBM] * 6,
-        out_specs=(VM,) * 5,
+        out_specs=(VM,) * 3,
         scratch_shapes=[
             pltpu.VMEM((3, 1, 256, 128), F32),
             pltpu.VMEM((1, 256, 128), jnp.int32),
@@ -353,51 +350,54 @@
             pltpu.VMEM((1, 128), jnp.int32),
             pltpu.VMEM((NA, 8, 128), F32),
             pltpu.VMEM((NA, 8, 128), F32),
+            pltpu.VMEM((256, 128), F32),
             pltpu.SemaphoreType.DMA((6,)),
         ],
-        compiler_params=params(62),
+        compiler_params=params(56),
         name="send",
-    )(
-        magnetic_vector_field, fixed_material_map, spinning_material_map,
-        slab_slide_offsets.reshape(1, 128), prior_thermal_state, goal_sensitivity,
-    )
-    frames = lax.all_gather(frame, ("section", "axial"))
+    )(magnetic_vector_field, *maps, prior_thermal_state, goal_sensitivity)
+    across = lax.ppermute(row_edge, "section", [(0, 1), (1, 0)])
     ring_main = lax.ppermute(ring, "azim", from_after)
-    heat_prev = lax.ppermute(heat_up, chain, onward)
-    heat_next = lax.ppermute(heat_down, chain, backward)
-    halo = pl.pallas_call(
-        halo_kernel, out_shape=struct(16, 8, 128), in_specs=[VM], out_specs=VM,
-        compiler_params=params(8), name="halo",
-    )(frames)
+    frame = pl.pallas_call(
+        frame_kernel, out_shape=struct(16, 8, 128), in_specs=[VM] * 2, out_specs=VM,
+        compiler_params=params(8), name="frame",
+    )(frame, across)
+    core = lax.ppermute(frame, "axial", [(0, 1), (1, 0), (2, 3), (3, 2)])
+    far = lax.ppermute(frame, "axial", [(1, 2), (2, 1)])
+    halo, heat_down, heat_up = pl.pallas_call(
+        halo_kernel,
+        out_shape=(struct(16, 8, 128), struct(NA + 4, 8, 128), struct(NA + 4, 8, 128)),
+        in_specs=[VM] * 5,
+        out_specs=(VM,) * 3,
+        compiler_params=params(8),
+        name="halo",
+    )(frame, core, far, prior_thermal_state, goal_sensitivity)
     ring_halo = lax.ppermute(halo, "azim", from_after)
-    heat_args = (prior_thermal_state, goal_sensitivity, heat_next, heat_prev)
-    edge = pl.pallas_call(
-        layers_kernel, out_shape=struct(8, 8, 128), in_specs=[VM] * 4, out_specs=VM,
-        compiler_params=params(8), name="layers",
-    )(*heat_args)
-    edges = lax.all_gather(edge, "axial")
     payload, part, weight, hring = pl.pallas_call(
         magnetic_kernel,
-        out_shape=(struct(NA, 40, 128), struct(3, 256, 128), struct(3, 256, 128), struct(2, 256, 128)),
-        in_specs=[VM] * 6 + [SM] * 3,
+        out_shape=(pltpu.VMEM((NA, 40, 128), F32), struct(3, 256, 128), struct(3, 256, 128), struct(2, 256, 128)),
+        in_specs=[VM] * 8 + [SM] * 3,
         out_specs=(VM,) * 4,
         scratch_shapes=[
             pltpu.VMEM((6, 280, 256), F32),
             pltpu.VMEM((34, 8, 256), F32),
             pltpu.VMEM((3, 272, 256), F32),
+            pltpu.VMEM((256, 128), F32),
         ],
         compiler_params=params(24),
         name="magnetic",
     )(
-        magnetic_vector_field, region, halo, ring_main, ring_halo, imposed_current_density,
+        magnetic_vector_field, *maps, halo, ring_main, ring_halo, imposed_current_density,
         inverse_permeability, electric_conductance, core_dissipation_coefficient,
     )
+    heat_prev = lax.ppermute(heat_up, chain, onward)
+    heat_next = lax.ppermute(heat_down, chain, backward)
+    hring = lax.ppermute(hring, "azim", from_before)
     got = lax.all_to_all(payload, "azim", split_axis=0, concat_axis=0, tiled=True)
-    hring = lax.ppermute(hring, "azim", from_before)
     wide = pltpu.VMEM((NA, 16, 256), F32)
     result = pl.pallas_call(
         heat_kernel,
-        out_shape=struct(NA, 16, 128),
+        out_shape=pltpu.VMEM((NA, 16, 128), F32),
         in_specs=[VM] * 6 + [SM] * 3,
         out_specs=VM,
         scratch_shapes=[
@@ -407,11 +407,13 @@
             wide, wide, wide, wide,
         ],
         compiler_params=params(32),
+        cost_estimate=pl.CostEstimate(flops=20_000_000, bytes_accessed=20_000_000, transcendentals=0),
         name="heat",
     )(
-        got, *heat_args, edges,
+        got, prior_thermal_state, goal_sensitivity, heat_next, heat_prev, heat_down,
         inplane_thermal_conductance, through_plane_conductance, thermal_storage,
     )
+    result, hring = lax.optimization_barrier((result, hring))
     back = lax.all_to_all(result, "azim", split_axis=0, concat_axis=0, tiled=True)
     return pl.pallas_call(
         finish_kernel,

time: 99.5 us -> 80.7 us (0.81)
  waiting for transfers between devices: 30.5 us -> 18.4 us
  blocking collectives: 24.3 us -> 21.8 us
  Pallas kernels: 11.7 us -> 9.23 us
  local copies, waits for them, and re-layouts: 1.62 us -> 0.07 us
    all_gather x2 -> x0, blocking collectives: 24.3 us -> none  [the longest x1 15.7 us: body(): frames = lax.all_gather(frame, ('section', 'axial'))]
    all_to_all x0 -> x1, blocking collectives: none -> 21.8 us  [body(): lax.all_to_all(result, 'azim', split_axis=0, concat_axis=0, tiled=True)]
    ppermute x1, waiting for transfers between devices: 15 us -> 0.01 us  [body(): hring = lax.ppermute(hring, 'azim', from_before)]
    all_to_all x1 -> x0, starting transfers between devices: 8.23 us -> none  [body(): lax.all_to_all(result, 'azim', split_axis=0, concat_axis=0, tiled=True)]
    ppermute x0 -> x3, starting transfers between devices: none -> 8.21 us  [the longest x1 4.72 us: body(): far = lax.ppermute(frame, 'axial', [(1, 2), (2, 1)])]
    ppermute x0 -> x3, waiting for transfers between devices: none -> 3.63 us  [the longest x1 2.34 us: body(): far = lax.ppermute(frame, 'axial', [(1, 2), (2, 1)])]
    ppermute x1, waiting for transfers between devices: 12.7 us -> 9.17 us  [body(): heat_next = lax.ppermute(heat_down, chain, backward)]
    ppermute x1, waiting for transfers between devices: 0.01 us -> 3.2 us  [body(): heat_prev = lax.ppermute(heat_up, chain, onward)]
  transfers between devices with their start and end apart: 7 -> 9, of which waited for: 3 -> 5; matrix products, arithmetic and copies ran while one was open for 0% -> 0% of each run, Pallas kernels for 0% -> 5%
where the time goes in v3:
time: 80.7 us; the launch traced here: 80.4 us
  starting transfers between devices  30.1 us (37%)
  blocking collectives  21.8 us (27%)
  waiting for transfers between devices  18.4 us (23%)
  Pallas kernels  9.23 us (11%)
  between operations  0.84 us (1%)
    all_to_all x1, blocking collectives, body(): lax.all_to_all(result, 'azim', split_axis=0, concat_axis=0, tiled=True)  21.8 us
    ppermute x1, waiting for transfers between devices, body(): heat_next = lax.ppermute(heat_down, chain, backward)  9.17 us
    ppermute x1, starting transfers between devices, body(): ring_main = lax.ppermute(ring, 'azim', from_after)  8.68 us
    all_to_all x1, starting transfers between devices, body(): lax.all_to_all(payload, 'azim', split_axis=0, concat_axis=0, tiled=True)  5.71 us
    ppermute x1, starting transfers between devices, body(): far = lax.ppermute(frame, 'axial', [(1, 2), (2, 1)])  4.72 us
    ppermute x1, starting transfers between devices, body(): heat_prev = lax.ppermute(heat_up, chain, onward)  3.99 us
    pallas_call x1, Pallas kernels, body(): pl.pallas_call(heat_kernel, out_shape=pltpu.VMEM((NA, 16, 128), F32), in_...  3.89 us
    ppermute x1, waiting for transfers between devices, body(): heat_prev = lax.ppermute(heat_up, chain, onward)  3.2 us
  transfers between devices with their start and end apart: 9, of which 5 were waited for; matrix products, arithmetic and copies ran while one was open for 0% of the time, Pallas kernels for 5%

profile of v3, /device:TPU:1, one launch (start us, length us, event | category | flops | bytes accessed | tf_op | source)
XLA Modules:
  0.0 80.4 jit_solution(16506803909833045995)
XLA Ops:
  0.7 1.7 %send.1 = (f32[4,8,128]{2,1,0:T(8,128)S(1)}, f32[12,8,128]{2,1,0:T(8,128)S(1)}, f32[2,256,128]{2,1,0:T(8,128)S(1)}) custom-call(f32[3,1,256,128]{3,2,1,0:T(8,128)} %pot.1, s32[1,256,128]{2,1,0:T(8,128)} %fixed.1, s32[32,128]{1,0:T(8,128)} %spin.1, s32[1,128]{1,0:T(1,128)} %bitcast.1, f32[32,8,128]{2,1,0:T(8,128)} %prior.3, f32[32,8,128]{2,1,0:T(8,128)} %goal.3), custom_call_target="tpu_custom_call" | custom-call | tf_op jit(solution)/shard_map/send/pallas_call | solution.py:341
  2.4 0.0 copy-start
  2.4 8.7 %collective-permute-start.3 = (f32[2,256,128]{2,1,0:T(8,128)S(1)}, f32[2,256,128]{2,1,0:T(8,128)S(1)}, u32[]{:S(2)}, u32[]{:S(2)}) collective-permute-start(f32[2,256,128]{2,1,0:T(8,128)S(1)} %get-tuple-element.18), channel_id=1, source_target_pairs={{4,0},{8,4},{12,8},{16,12},{20,16},{24,20},{28,24},{32,28},{36,32}... | collective-permute-start | bytes 786440 | tf_op jit(solution)/shard_map/ppermute | solution.py:360
  11.0 1.3 %collective-permute-start = (f32[4,8,128]{2,1,0:T(8,128)S(1)}, f32[4,8,128]{2,1,0:T(8,128)S(1)}, u32[]{:S(2)}, u32[]{:S(2)}) collective-permute-start(f32[4,8,128]{2,1,0:T(8,128)S(1)} %get-tuple-element.16), channel_id=1, source_target_pairs={{0,128},{128,0},{1,129},{129,1},{2,130},{130,2},{3,131},{131,3},{4... | collective-permute-start | bytes 49160 | tf_op jit(solution)/shard_map/ppermute | solution.py:359
  12.3 1.3 %collective-permute-done.across = f32[4,8,128]{2,1,0:T(8,128)S(1)} collective-permute-done((f32[4,8,128]{2,1,0:T(8,128)S(1)}, f32[4,8,128]{2,1,0:T(8,128)S(1)}, u32[]{:S(2)}, u32[]{:S(2)}) %collective-permute-start) | collective-permute-done | bytes 16416 | tf_op jit(solution)/shard_map/ppermute | solution.py:359
  13.7 0.0 copy-start.3
  13.7 0.0 copy-start.5
  13.7 2.2 %collective-permute-start.1 = (f32[16,8,128]{2,1,0:T(8,128)S(1)}, f32[16,8,128]{2,1,0:T(8,128)S(1)}, u32[]{:S(2)}, u32[]{:S(2)}) collective-permute-start(f32[16,8,128]{2,1,0:T(8,128)S(1)} %frame.1.own), channel_id=1, source_target_pairs={{0,1},{1,0},{2,3},{3,2},{4,5},{5,4},{6,7},{7,6},{8,9},{9,8},{10,11... | collective-permute-start | bytes 196616 | tf_op jit(solution)/shard_map/ppermute | solution.py:365
  15.9 4.7 %collective-permute-start.2 = (f32[16,8,128]{2,1,0:T(8,128)S(1)}, f32[16,8,128]{2,1,0:T(8,128)S(1)}, u32[]{:S(2)}, u32[]{:S(2)}) collective-permute-start(f32[16,8,128]{2,1,0:T(8,128)S(1)} %frame.1.own), channel_id=1, source_target_pairs={{1,2},{2,1},{5,6},{6,5},{9,10},{10,9},{13,14},{14,13},{17,18},{18,... | collective-permute-start | bytes 196616 | tf_op jit(solution)/shard_map/ppermute | solution.py:366
  20.6 2.3 %collective-permute-done.2.far = f32[16,8,128]{2,1,0:T(8,128)S(1)} collective-permute-done((f32[16,8,128]{2,1,0:T(8,128)S(1)}, f32[16,8,128]{2,1,0:T(8,128)S(1)}, u32[]{:S(2)}, u32[]{:S(2)}) %collective-permute-start.2) | collective-permute-done | bytes 65568 | tf_op jit(solution)/shard_map/ppermute | solution.py:366
  23.0 0.0 copy-start.6
  23.0 0.0 copy-start.8
  23.0 0.8 collective-permute-start.4
  23.8 2.4 %collective-permute-done.4.ring_halo = f32[16,8,128]{2,1,0:T(8,128)S(1)} collective-permute-done((f32[16,8,128]{2,1,0:T(8,128)S(1)}, f32[16,8,128]{2,1,0:T(8,128)S(1)}, u32[]{:S(2)}, u32[]{:S(2)}) %collective-permute-start.4) | collective-permute-done | bytes 65568 | tf_op jit(solution)/shard_map/ppermute | solution.py:375
  26.3 2.6 %magnetic.1 = (f32[32,40,128]{2,1,0:T(8,128)}, f32[3,256,128]{2,1,0:T(8,128)S(1)}, f32[3,256,128]{2,1,0:T(8,128)S(1)}, f32[2,256,128]{2,1,0:T(8,128)S(1)}) custom-call(f32[3,1,256,128]{3,2,1,0:T(8,128)S(1)} %copy-done, s32[1,256,128]{2,1,0:T(8,128)S(1)} %copy-done.3, s32[32,128]{1,0:T(8,128)S(1)} %copy-done.5, s32[1,128]{1,0:T(1,128)S(1)} %bitcast.2, ...), custom_call_target="tpu_custom_call" | custom-call | tf_op jit(solution)/shard_map/magnetic/pallas_call | solution.py:376
  28.9 5.7 %all-to-all-start = ((f32[32,40,128]{2,1,0:T(8,128)}), f32[32,40,128]{2,1,0:T(8,128)S(1)}, u32[]{:S(2)}, u32[]{:S(2)}) async-start(f32[32,40,128]{2,1,0:T(8,128)} %get-tuple-element.19), calls=%async_computation | async-start | bytes 1310720 | tf_op jit(solution)/shard_map/all_to_all | solution.py:396
  34.6 1.3 %collective-permute-start.7 = (f32[2,256,128]{2,1,0:T(8,128)S(1)}, f32[2,256,128]{2,1,0:T(8,128)S(1)}, u32[]{:S(2)}, u32[]{:S(2)}) collective-permute-start(f32[2,256,128]{2,1,0:T(8,128)S(1)} %get-tuple-element.22), channel_id=1, source_target_pairs={{0,4},{4,8},{8,12},{12,16},{16,20},{20,24},{24,28},{28,32},{32,36}... | collective-permute-start | bytes 786440 | tf_op jit(solution)/shard_map/ppermute | solution.py:395
  35.9 1.4 %collective-permute-start.5 = (f32[36,8,128]{2,1,0:T(8,128)S(1)}, f32[36,8,128]{2,1,0:T(8,128)S(1)}, u32[]{:S(2)}, u32[]{:S(2)}) collective-permute-start(f32[36,8,128]{2,1,0:T(8,128)S(1)} %get-tuple-element.20.sides), channel_id=1, source_target_pairs={{4,0},{8,4},{12,8},{16,12},{20,16},{24,20},{28,24},{32,28},{36,32}... | collective-permute-start | bytes 442376 | tf_op jit(solution)/shard_map/ppermute | solution.py:394
  37.4 4.0 %collective-permute-start.6 = (f32[36,8,128]{2,1,0:T(8,128)S(1)}, f32[36,8,128]{2,1,0:T(8,128)S(1)}, u32[]{:S(2)}, u32[]{:S(2)}) collective-permute-start(f32[36,8,128]{2,1,0:T(8,128)S(1)} %get-tuple-element.21), channel_id=1, source_target_pairs={{0,4},{4,8},{8,12},{12,16},{16,20},{20,24},{24,28},{28,32},{32,36}... | collective-permute-start | bytes 442376 | tf_op jit(solution)/shard_map/ppermute | solution.py:393
  41.4 9.2 %collective-permute-done.5.from_next = f32[36,8,128]{2,1,0:T(8,128)S(1)} collective-permute-done((f32[36,8,128]{2,1,0:T(8,128)S(1)}, f32[36,8,128]{2,1,0:T(8,128)S(1)}, u32[]{:S(2)}, u32[]{:S(2)}) %collective-permute-start.5) | collective-permute-done | bytes 147488 | tf_op jit(solution)/shard_map/ppermute | solution.py:394
  50.5 3.2 %collective-permute-done.6.from_prev = f32[36,8,128]{2,1,0:T(8,128)S(1)} collective-permute-done((f32[36,8,128]{2,1,0:T(8,128)S(1)}, f32[36,8,128]{2,1,0:T(8,128)S(1)}, u32[]{:S(2)}, u32[]{:S(2)}) %collective-permute-start.6) | collective-permute-done | bytes 147488 | tf_op jit(solution)/shard_map/ppermute | solution.py:393
  53.7 3.9 %heat.1 = f32[32,16,128]{2,1,0:T(8,128)S(1)} custom-call(f32[32,40,128]{2,1,0:T(8,128)S(1)} %all-to-all-done.got, f32[32,8,128]{2,1,0:T(8,128)S(1)} %copy-done.1, f32[32,8,128]{2,1,0:T(8,128)S(1)} %copy-done.2, f32[36,8,128]{2,1,0:T(8,128)S(1)} %collective-permute-done.5.from_next, f32[36,8,128]{2,1,0:T(8,128)S(1)} %collective-permute-done.6.from_prev, ...), custom_call_target="tpu_custom_call" | custom-call | flops 20000000 | bytes 20000000 | tf_op jit(solution)/shard_map/heat/pallas_call | solution.py:398
  57.7 21.8 %all_to_all.10.got = f32[32,16,128]{2,1,0:T(8,128)S(1)} all-to-all(f32[32,16,128]{2,1,0:T(8,128)S(1)} %heat.1), channel_id=1, replica_groups=mesh['section'=2,'azim'=32,'axial'=4] {'azim'}, dimensions={0} | all-to-all | bytes 524288 | tf_op jit(solution)/shard_map/all_to_all | solution.py:417
  79.4 1.0 %finish.1 = (f32[3,1,256,128]{3,2,1,0:T(8,128)}, f32[3,1,256,128]{3,2,1,0:T(8,128)}, f32[1,256,128]{2,1,0:T(8,128)}) custom-call(f32[32,16,128]{2,1,0:T(8,128)S(1)} %all_to_all.10.got, f32[3,256,128]{2,1,0:T(8,128)S(1)} %get-tuple-element.24.part, f32[3,256,128]{2,1,0:T(8,128)S(1)} %get-tuple-element.25.weight, f32[2,256,128]{2,1,0:T(8,128)S(1)} %collective-permute-done.7.hring), custom_call_target="tpu_custom_call" | custom-call | tf_op jit(solution)/shard_map/finish/pallas_call | solution.py:418
  (27 shorter events, 0.1 us)
Async XLA Ops:
  0.6 22.3 %copy-start.1 = (f32[32,8,128]{2,1,0:T(8,128)S(1)}, f32[32,8,128]{2,1,0:T(8,128)}, u32[]{:S(2)}) copy-start(f32[32,8,128]{2,1,0:T(8,128)} %prior.3) | copy-start | bytes 393220
  0.6 22.3 %copy-start.2 = (f32[32,8,128]{2,1,0:T(8,128)S(1)}, f32[32,8,128]{2,1,0:T(8,128)}, u32[]{:S(2)}) copy-start(f32[32,8,128]{2,1,0:T(8,128)} %goal.3) | copy-start | bytes 393220
  0.7 25.6 %copy-start.4 = (f32[3,1,256,128]{3,2,1,0:T(8,128)S(1)}, f32[3,1,256,128]{3,2,1,0:T(8,128)}, u32[]{:S(2)}) copy-start(f32[3,1,256,128]{3,2,1,0:T(8,128)} %current.1) | copy-start | bytes 1179652
  2.4 23.9 %copy-start = (f32[3,1,256,128]{3,2,1,0:T(8,128)S(1)}, f32[3,1,256,128]{3,2,1,0:T(8,128)}, u32[]{:S(2)}) copy-start(f32[3,1,256,128]{3,2,1,0:T(8,128)} %pot.1) | copy-start | bytes 1179652
  2.4 23.9 %collective-permute-start.3 = (f32[2,256,128]{2,1,0:T(8,128)S(1)}, f32[2,256,128]{2,1,0:T(8,128)S(1)}, u32[]{:S(2)}, u32[]{:S(2)}) collective-permute-start(f32[2,256,128]{2,1,0:T(8,128)S(1)} %get-tuple-element.18), channel_id=1, source_target_pairs={{4,0},{8,4},{12,8},{16,12},{20,16},{24,20},{28,24},{32,28},{36,32}... | collective-permute-start | bytes 786440 | tf_op jit(solution)/shard_map/ppermute | solution.py:360
  11.0 2.6 %collective-permute-start = (f32[4,8,128]{2,1,0:T(8,128)S(1)}, f32[4,8,128]{2,1,0:T(8,128)S(1)}, u32[]{:S(2)}, u32[]{:S(2)}) collective-permute-start(f32[4,8,128]{2,1,0:T(8,128)S(1)} %get-tuple-element.16), channel_id=1, source_target_pairs={{0,128},{128,0},{1,129},{129,1},{2,130},{130,2},{3,131},{131,3},{4... | collective-permute-start | bytes 49160 | tf_op jit(solution)/shard_map/ppermute | solution.py:359
  13.7 12.6 %copy-start.3 = (s32[1,256,128]{2,1,0:T(8,128)S(1)}, s32[1,256,128]{2,1,0:T(8,128)}, u32[]{:S(2)}) copy-start(s32[1,256,128]{2,1,0:T(8,128)} %fixed.1) | copy-start | bytes 393220
  13.7 12.6 %copy-start.5 = (s32[32,128]{1,0:T(8,128)S(1)}, s32[32,128]{1,0:T(8,128)}, u32[]{:S(2)}) copy-start(s32[32,128]{1,0:T(8,128)} %spin.1) | copy-start | bytes 49156
  13.7 6.9 %collective-permute-start.1 = (f32[16,8,128]{2,1,0:T(8,128)S(1)}, f32[16,8,128]{2,1,0:T(8,128)S(1)}, u32[]{:S(2)}, u32[]{:S(2)}) collective-permute-start(f32[16,8,128]{2,1,0:T(8,128)S(1)} %frame.1.own), channel_id=1, source_target_pairs={{0,1},{1,0},{2,3},{3,2},{4,5},{5,4},{6,7},{7,6},{8,9},{9,8},{10,11... | collective-permute-start | bytes 196616 | tf_op jit(solution)/shard_map/ppermute | solution.py:365
  15.9 7.1 %collective-permute-start.2 = (f32[16,8,128]{2,1,0:T(8,128)S(1)}, f32[16,8,128]{2,1,0:T(8,128)S(1)}, u32[]{:S(2)}, u32[]{:S(2)}) collective-permute-start(f32[16,8,128]{2,1,0:T(8,128)S(1)} %frame.1.own), channel_id=1, source_target_pairs={{1,2},{2,1},{5,6},{6,5},{9,10},{10,9},{13,14},{14,13},{17,18},{18,... | collective-permute-start | bytes 196616 | tf_op jit(solution)/shard_map/ppermute | solution.py:366
  23.0 3.3 %copy-start.9 = (f32[8]{0:T(128)S(1)}, f32[8]{0:T(128)}, u32[]{:S(2)}) copy-start(f32[8]{0:T(128)} %loss.1) | copy-start | bytes 100
  23.0 3.3 %copy-start.6 = (s32[128]{0:T(128)S(1)}, s32[128]{0:T(128)}, u32[]{:S(2)}) copy-start(s32[128]{0:T(128)} %param.17) | copy-start | bytes 1540
  23.0 3.3 %copy-start.7 = (f32[8]{0:T(128)S(1)}, f32[8]{0:T(128)}, u32[]{:S(2)}) copy-start(f32[8]{0:T(128)} %reluct.1) | copy-start | bytes 100
  23.0 3.3 %copy-start.8 = (f32[8]{0:T(128)S(1)}, f32[8]{0:T(128)}, u32[]{:S(2)}) copy-start(f32[8]{0:T(128)} %eddy.1) | copy-start | bytes 100
  23.0 3.2 %collective-permute-start.4 = (f32[16,8,128]{2,1,0:T(8,128)S(1)}, f32[16,8,128]{2,1,0:T(8,128)S(1)}, u32[]{:S(2)}, u32[]{:S(2)}) collective-permute-start(f32[16,8,128]{2,1,0:T(8,128)S(1)} %get-tuple-element.17.halo), channel_id=1, source_target_pairs={{4,0},{8,4},{12,8},{16,12},{20,16},{24,20},{28,24},{32,28},{36,32}... | collective-permute-start | bytes 196616 | tf_op jit(solution)/shard_map/ppermute | solution.py:375
  28.9 24.8 %all-to-all-start = ((f32[32,40,128]{2,1,0:T(8,128)}), f32[32,40,128]{2,1,0:T(8,128)S(1)}, u32[]{:S(2)}, u32[]{:S(2)}) async-start(f32[32,40,128]{2,1,0:T(8,128)} %get-tuple-element.19), calls=%async_computation | async-start | bytes 1310720 | tf_op jit(solution)/shard_map/all_to_all | solution.py:396
  34.6 23.0 %collective-permute-start.7 = (f32[2,256,128]{2,1,0:T(8,128)S(1)}, f32[2,256,128]{2,1,0:T(8,128)S(1)}, u32[]{:S(2)}, u32[]{:S(2)}) collective-permute-start(f32[2,256,128]{2,1,0:T(8,128)S(1)} %get-tuple-element.22), channel_id=1, source_target_pairs={{0,4},{4,8},{8,12},{12,16},{16,20},{20,24},{24,28},{28,32},{32,36}... | collective-permute-start | bytes 786440 | tf_op jit(solution)/shard_map/ppermute | solution.py:395
  35.9 17.8 %copy-start.10 = (f32[8]{0:T(128)S(1)}, f32[8]{0:T(128)}, u32[]{:S(2)}) copy-start(f32[8]{0:T(128)} %plane.1) | copy-start | bytes 100
  35.9 17.8 %copy-start.11 = (f32[8]{0:T(128)S(1)}, f32[8]{0:T(128)}, u32[]{:S(2)}) copy-start(f32[8]{0:T(128)} %axial.1) | copy-start | bytes 100
  35.9 17.8 %copy-start.12 = (f32[8]{0:T(128)S(1)}, f32[8]{0:T(128)}, u32[]{:S(2)}) copy-start(f32[8]{0:T(128)} %storage.1) | copy-start | bytes 100
  35.9 14.6 %collective-permute-start.5 = (f32[36,8,128]{2,1,0:T(8,128)S(1)}, f32[36,8,128]{2,1,0:T(8,128)S(1)}, u32[]{:S(2)}, u32[]{:S(2)}) collective-permute-start(f32[36,8,128]{2,1,0:T(8,128)S(1)} %get-tuple-element.20.sides), channel_id=1, source_target_pairs={{4,0},{8,4},{12,8},{16,12},{20,16},{24,20},{28,24},{32,28},{36,32}... | collective-permute-start | bytes 442376 | tf_op jit(solution)/shard_map/ppermute | solution.py:394
  37.4 16.4 %collective-permute-start.6 = (f32[36,8,128]{2,1,0:T(8,128)S(1)}, f32[36,8,128]{2,1,0:T(8,128)S(1)}, u32[]{:S(2)}, u32[]{:S(2)}) collective-permute-start(f32[36,8,128]{2,1,0:T(8,128)S(1)} %get-tuple-element.21), channel_id=1, source_target_pairs={{0,4},{4,8},{8,12},{12,16},{16,20},{20,24},{24,28},{28,32},{32,36}... | collective-permute-start | bytes 442376 | tf_op jit(solution)/shard_map/ppermute | solution.py:393

commit v4 on v3

--- a/solution.py
+++ b/solution.py
@@ -11,7 +11,7 @@
 F32 = jnp.float32
 VM = pl.BlockSpec(memory_space=pltpu.VMEM)
 SM = pl.BlockSpec(memory_space=pltpu.SMEM)
-HBM = pl.BlockSpec(memory_space=pl.ANY)
+HBM = pl.BlockSpec(memory_space=pltpu.HBM)
 
 
 def params(mib):
@@ -63,7 +63,7 @@
 
 def send_kernel(
     pot_in, fixed_in, spin_in, offs_in, prior_in, goal_in,
-    row_edge, frame, ring,
+    row_edge, edge, ring, planes,
     pot, fixed, spin, offs, prior, goal, region, sems,
 ):
     pairs = ((pot_in, pot), (fixed_in, fixed), (spin_in, spin), (offs_in, offs), (prior_in, prior), (goal_in, goal))
@@ -87,9 +87,12 @@
         for u in range(4):
             for f in range(4):
                 packed = put(packed, 4 * u + f, tile(f, 4 * g + u))
-        frame[g] = packed
+        edge[g] = packed
     ring[0] = pot[1, 0]
     ring[1] = pot[2, 0]
+    for f in range(3):
+        planes[f] = pot[f, 0]
+    planes[3] = region[...]
     copies[4].wait()
     copies[5].wait()
     for g in range(4):
@@ -97,13 +100,13 @@
         for u in range(8):
             packed = put(packed, 2 * u, prior[8 * g + u])
             packed = put(packed, 2 * u + 1, goal[8 * g + u])
-        frame[8 + g] = packed
-
-
-def frame_kernel(frame, across, out):
+        edge[8 + g] = packed
+
+
+def frame_kernel(edge, across, out):
     valid = sub_low() == (lax.axis_index("section") == 0)
     for g in range(12):
-        out[g] = frame[g]
+        out[g] = edge[g]
     for f in range(4):
         out[12 + f] = jnp.where(valid, across[f], 0.0)
 
@@ -155,67 +158,94 @@
     return pltpu.roll(v, 1, 1)
 
 
+def widen(wide, n, main, halo, f):
+    low = sub_low()
+    left, right = pl.ds(0, 128), pl.ds(128, 128)
+    for t in range(32):
+        wide[n, pl.ds(8 + 8 * t, 8), left] = main(pl.ds(8 * t, 8))
+        wide[n, pl.ds(8 + 8 * t, 8), right] = take(halo[t // 4], 4 * (t % 4) + f)
+    for side, block in ((left, halo[8 + f]), (right, halo[12 + f])):
+        wide[n, pl.ds(264, 8), side] = jnp.where(low, block, 0.0)
+        wide[n, pl.ds(0, 8), side] = jnp.where(low, 0.0, block)
+        wide[n, pl.ds(272, 8), side] = jnp.zeros((8, 128), F32)
+
+
+def fluxes(wide, t):
+    here, ahead = pl.ds(8 * t, 8), pl.ds(8 * t + 1, 8)
+    pa, pr, pz = wide[0, here, :], wide[1, here, :], wide[2, here, :]
+    fa = (wide[2, ahead, :] - pz) - (lnext(pr) - pr)
+    fr = (lnext(pa) - pa) - (wide[5, here, :] - pz)
+    fz = (wide[4, here, :] - pr) - (wide[0, ahead, :] - pa)
+    return fa, fr, fz
+
+
+def widen_all(wide, pot, region, halo, ring, halo_after):
+    for f in range(3):
+        widen(wide, f, lambda at, f=f: pot[f, 0, at, :], halo, f)
+    widen(wide, 3, lambda at: region[at, :], halo, 3)
+    for n in range(2):
+        widen(wide, 4 + n, lambda at, n=n: ring[n, at, :], halo_after, 1 + n)
+
+
 def magnetic_kernel(
-    pot, fixed, spin, offs, halo, ring, ring_halo, current, reluct, eddy, loss,
-    payload, misfit, weight, hring,
-    wide, heat, hfield, region,
+    pot, fixed, spin, offs, halo, ring, halo_after, loss,
+    payload,
+    wide, heat, region,
 ):
     find_region(fixed, spin, offs, region)
-    low = sub_low()
-    mains = [
-        lambda at: pot[0, 0, at, :], lambda at: pot[1, 0, at, :], lambda at: pot[2, 0, at, :],
-        lambda at: region[at, :], lambda at: ring[0, at, :], lambda at: ring[1, at, :],
-    ]
-    left, right = pl.ds(0, 128), pl.ds(128, 128)
-    for n in range(6):
-        source, f = (halo, n) if n < 4 else (ring_halo, n - 3)
-        for t in range(32):
-            wide[n, pl.ds(8 + 8 * t, 8), left] = mains[n](pl.ds(8 * t, 8))
-            wide[n, pl.ds(8 + 8 * t, 8), right] = take(source[t // 4], 4 * (t % 4) + f)
-        for side, block in ((left, source[8 + f]), (right, source[12 + f])):
-            wide[n, pl.ds(264, 8), side] = jnp.where(low, block, 0.0)
-            wide[n, pl.ds(0, 8), side] = jnp.where(low, 0.0, block)
-            wide[n, pl.ds(272, 8), side] = jnp.zeros((8, 128), F32)
+    widen_all(wide, pot, region, halo, ring, halo_after)
+    low = sub_low()
     for t in range(34):
-        here, ahead = pl.ds(8 * t, 8), pl.ds(8 * t + 1, 8)
-        pa, pr, pz = wide[0, here, :], wide[1, here, :], wide[2, here, :]
-        fa = (wide[2, ahead, :] - pz) - (lnext(pr) - pr)
-        fr = (lnext(pa) - pa) - (wide[5, here, :] - pz)
-        fz = (wide[4, here, :] - pr) - (wide[0, ahead, :] - pa)
-        rel, dens = lookup(wide[3, here, :], (reluct, loss))
+        fa, fr, fz = fluxes(wide, t)
+        (dens,) = lookup(wide[3, pl.ds(8 * t, 8), :], (loss,))
         heat[t] = dens * (fa * fa + fr * fr + fz * fz)
-        hfield[0, here, :] = rel * fa
-        hfield[1, here, :] = rel * fr
-        hfield[2, here, :] = rel * fz
-        if 1 <= t <= 32:
-            rows = pl.ds(8 * t - 8, 8)
-            scale = 2.0 * dens
-            for n, f in enumerate((fa, fr, fz)):
-                weight[n, rows, :] = (scale * f)[:, :128]
-            hring[0, rows, :] = (rel * fr)[:, :128]
-            hring[1, rows, :] = (rel * fz)[:, :128]
-    for t in range(1, 33):
-        here, behind, rows = pl.ds(8 * t, 8), pl.ds(8 * t - 1, 8), pl.ds(8 * t - 8, 8)
-        ha, hr, hz = hfield[0, here, :], hfield[1, here, :], hfield[2, here, :]
-        ca = (lprev(hr) - hr) - (hfield[2, behind, :] - hz)
-        cr = -hz - (lprev(ha) - ha)
-        cz = (hfield[0, behind, :] - ha) + hr
-        (sigma,) = lookup(region[rows, :], (eddy,))
-        for n, c in enumerate((ca, cr, cz)):
-            misfit[n, rows, :] = c[:, :128] + (sigma * pot[n, 0, rows, :] - current[n, 0, rows, :])
     for j in range(NA):
         t = j + 1
-        packed = jnp.zeros((8, 128), F32)
         tiles = []
         for get in (lambda i: heat[i], lambda i: wide[3, pl.ds(8 * i, 8), :]):
             near, after, before = get(t), get(t + 1), get(t - 1)
             beyond = [jnp.where(low, after[:, k:k + 128], before[:, k:k + 128]) for k in (0, 128)]
             tiles.append((near[:, :128], near[:, 128:]))
             tiles.append(tuple(beyond))
-        for c, (main, side) in enumerate(tiles):
-            payload[j, pl.ds(8 * c, 8), :] = main
-            packed = put(packed, c, side)
+        packed = jnp.zeros((8, 128), F32)
+        for c in range(4):
+            payload[j, pl.ds(8 * c, 8), :] = tiles[c][0]
+            packed = put(packed, c, tiles[c][1])
         payload[j, pl.ds(32, 8), :] = packed
+
+
+def curl_kernel(
+    pot, fixed, spin, offs, halo, ring, halo_after, planes, halo_before, current, reluct, eddy, loss,
+    misfit, weight,
+    wide, hfield, region,
+):
+    find_region(fixed, spin, offs, region)
+    widen_all(wide, pot, region, halo, ring, halo_after)
+    widen(wide, 6, lambda at: planes[0, at, :], halo_before, 0)
+    for t in range(34):
+        here, rows = pl.ds(8 * t, 8), pl.ds(8 * t - 8, 8)
+        fa, fr, fz = fluxes(wide, t)
+        rel, dens = lookup(wide[3, here, :], (reluct, loss))
+        hfield[0, here, :] = rel * fa
+        hfield[1, here, :] = rel * fr
+        hfield[2, here, :] = rel * fz
+        if 1 <= t <= 32:
+            scale = 2.0 * dens
+            for n, f in enumerate((fa, fr, fz)):
+                weight[n, rows, :] = (scale * f)[:, :128]
+    for t in range(1, 33):
+        here, ahead, behind, rows = pl.ds(8 * t, 8), pl.ds(8 * t + 1, 8), pl.ds(8 * t - 1, 8), pl.ds(8 * t - 8, 8)
+        ha, hr, hz = hfield[0, here, :], hfield[1, here, :], hfield[2, here, :]
+        before = wide[6, here, :]
+        (rel,) = lookup(planes[3, rows, :], (reluct,))
+        hr_before = rel * ((lnext(before) - before)[:, :128] - (pot[2, 0, rows, :] - planes[2, rows, :]))
+        hz_before = rel * ((pot[1, 0, rows, :] - planes[1, rows, :]) - (wide[6, ahead, :] - before)[:, :128])
+        ca = ((lprev(hr) - hr) - (hfield[2, behind, :] - hz))[:, :128]
+        cr = (hz_before - hz[:, :128]) - (lprev(ha) - ha)[:, :128]
+        cz = (hfield[0, behind, :] - ha)[:, :128] - (hr_before - hr[:, :128])
+        (sigma,) = lookup(region[rows, :], (eddy,))
+        for n, c in enumerate((ca, cr, cz)):
+            misfit[n, 0, rows, :] = c + sigma * pot[n, 0, rows, :] - current[n, 0, rows, :]
 
 
 def heat_kernel(
@@ -233,8 +263,8 @@
         outer = jnp.where(low, from_next[NA + g], from_prev[NA + g])
         for u in range(8):
             a = 8 * g + u
+            tiles = [got[a, pl.ds(8 * c, 8), :] for c in range(4)]
             side = got[a, pl.ds(32, 8), :]
-            tiles = [got[a, pl.ds(8 * c, 8), :] for c in range(4)]
             ends = [take(side, c) for c in range(4)]
             src[a] = join(tiles[:2], ends[:2])
             kin[a], kax[a], cap[a] = lookup(join(tiles[2:], ends[2:]), (plane, axial, storage))
@@ -298,11 +328,7 @@
         lax.fori_loop(0, NA, step, 0, unroll=32)
 
 
-def finish_kernel(got, part, weight, hring, misfit, dual, state):
-    misfit[0, 0] = part[0]
-    misfit[1, 0] = part[1] + hring[1]
-    misfit[2, 0] = part[2] - hring[0]
-
+def finish_kernel(got, weight, dual, state):
     def step(j, carry):
         at = pl.ds(pl.multiple_of(8 * j, 8), 8)
         state[0, at, :] = got[j, pl.ds(0, 8), :]
@@ -338,11 +364,11 @@
 
     offsets = slab_slide_offsets.reshape(1, 128)
     maps = (fixed_material_map, spinning_material_map, offsets)
-    row_edge, frame, ring = pl.pallas_call(
+    row_edge, edge, ring, planes = pl.pallas_call(
         send_kernel,
-        out_shape=(pltpu.VMEM((4, 8, 128), F32), pltpu.VMEM((12, 8, 128), F32), pltpu.VMEM((2, 256, 128), F32)),
+        out_shape=tuple(pltpu.VMEM(d, F32) for d in ((4, 8, 128), (12, 8, 128), (2, 256, 128), (4, 256, 128))),
         in_specs=[HBM] * 6,
-        out_specs=(VM,) * 3,
+        out_specs=(VM,) * 4,
         scratch_shapes=[
             pltpu.VMEM((3, 1, 256, 128), F32),
             pltpu.VMEM((1, 256, 128), jnp.int32),
@@ -357,11 +383,13 @@
         name="send",
     )(magnetic_vector_field, *maps, prior_thermal_state, goal_sensitivity)
     across = lax.ppermute(row_edge, "section", [(0, 1), (1, 0)])
-    ring_main = lax.ppermute(ring, "azim", from_after)
     frame = pl.pallas_call(
         frame_kernel, out_shape=struct(16, 8, 128), in_specs=[VM] * 2, out_specs=VM,
         compiler_params=params(8), name="frame",
-    )(frame, across)
+    )(edge, across)
+    frame, ring, planes = lax.optimization_barrier((frame, ring, planes))
+    ring = lax.ppermute(ring, "azim", from_after)
+    planes = lax.ppermute(planes, "azim", from_before)
     core = lax.ppermute(frame, "axial", [(0, 1), (1, 0), (2, 3), (3, 2)])
     far = lax.ppermute(frame, "axial", [(1, 2), (2, 1)])
     halo, heat_down, heat_up = pl.pallas_call(
@@ -372,28 +400,43 @@
         compiler_params=params(8),
         name="halo",
     )(frame, core, far, prior_thermal_state, goal_sensitivity)
-    ring_halo = lax.ppermute(halo, "azim", from_after)
-    payload, part, weight, hring = pl.pallas_call(
+    halo_after = lax.ppermute(halo, "azim", from_after)
+    block = (magnetic_vector_field, *maps, halo, ring, halo_after)
+    payload = pl.pallas_call(
         magnetic_kernel,
-        out_shape=(pltpu.VMEM((NA, 40, 128), F32), struct(3, 256, 128), struct(3, 256, 128), struct(2, 256, 128)),
-        in_specs=[VM] * 8 + [SM] * 3,
-        out_specs=(VM,) * 4,
+        out_shape=pltpu.VMEM((NA, 40, 128), F32),
+        in_specs=[VM] * 7 + [SM],
+        out_specs=VM,
         scratch_shapes=[
             pltpu.VMEM((6, 280, 256), F32),
             pltpu.VMEM((34, 8, 256), F32),
+            pltpu.VMEM((256, 128), F32),
+        ],
+        compiler_params=params(24),
+        name="magnetic",
+    )(*block, core_dissipation_coefficient)
+    halo_before = lax.ppermute(halo, "azim", from_before)
+    payload, planes, halo_before = lax.optimization_barrier((payload, planes, halo_before))
+    got = lax.all_to_all(payload, "azim", split_axis=0, concat_axis=0, tiled=True)
+    heat_prev = lax.ppermute(heat_up, chain, onward)
+    heat_next = lax.ppermute(heat_down, chain, backward)
+    misfit, weight = pl.pallas_call(
+        curl_kernel,
+        out_shape=(struct(3, 1, 256, 128), struct(3, 256, 128)),
+        in_specs=[VM] * 10 + [SM] * 3,
+        out_specs=(VM, VM),
+        scratch_shapes=[
+            pltpu.VMEM((7, 280, 256), F32),
             pltpu.VMEM((3, 272, 256), F32),
             pltpu.VMEM((256, 128), F32),
         ],
         compiler_params=params(24),
-        name="magnetic",
+        cost_estimate=pl.CostEstimate(flops=10_000_000, bytes_accessed=10_000_000, transcendentals=0),
+        name="curl",
     )(
-        magnetic_vector_field, *maps, halo, ring_main, ring_halo, imposed_current_density,
+        *block, planes, halo_before, imposed_current_density,
         inverse_permeability, electric_conductance, core_dissipation_coefficient,
     )
-    heat_prev = lax.ppermute(heat_up, chain, onward)
-    heat_next = lax.ppermute(heat_down, chain, backward)
-    hring = lax.ppermute(hring, "azim", from_before)
-    got = lax.all_to_all(payload, "azim", split_axis=0, concat_axis=0, tiled=True)
     wide = pltpu.VMEM((NA, 16, 256), F32)
     result = pl.pallas_call(
         heat_kernel,
@@ -413,16 +456,16 @@
         got, prior_thermal_state, goal_sensitivity, heat_next, heat_prev, heat_down,
         inplane_thermal_conductance, through_plane_conductance, thermal_storage,
     )
-    result, hring = lax.optimization_barrier((result, hring))
     back = lax.all_to_all(result, "azim", split_axis=0, concat_axis=0, tiled=True)
-    return pl.pallas_call(
+    dual, state = pl.pallas_call(
         finish_kernel,
-        out_shape=(struct(3, 1, 256, 128), struct(3, 1, 256, 128), struct(1, 256, 128)),
-        in_specs=[VM] * 4,
-        out_specs=(VM,) * 3,
+        out_shape=(struct(3, 1, 256, 128), struct(1, 256, 128)),
+        in_specs=[VM] * 2,
+        out_specs=(VM,) * 2,
         compiler_params=params(16),
         name="finish",
-    )(back, part, weight, hring)
+    )(back, weight)
+    return misfit, dual, state
 
 
 def solution(mesh):

time: 80.7 us -> 79.6 us (0.986)
  the two profiles are of different devices: /device:TPU:1 before, /device:TPU:8 now
where the time goes in v4:
time: 79.6 us; the launch traced here: 79.3 us
  starting transfers between devices  33.9 us (43%)
  waiting for transfers between devices  32.8 us (41%)
  Pallas kernels  11.7 us (15%)
  between operations  0.85 us (1%)
    ppermute x1, waiting for transfers between devices, body(): heat_next = lax.ppermute(heat_down, chain, backward)  10.5 us
    all_to_all x1, waiting for transfers between devices, body(): lax.all_to_all(result, 'azim', split_axis=0, concat_axis=0, tiled=True)  10.4 us
    ppermute x1, starting transfers between devices, body(): heat_next = lax.ppermute(heat_down, chain, backward)  7.13 us
    ppermute x1, starting transfers between devices, body(): ring = lax.ppermute(ring, 'azim', from_after)  6.22 us
    all_to_all x1, starting transfers between devices, body(): lax.all_to_all(payload, 'azim', split_axis=0, concat_axis=0, tiled=True)  6.22 us
    all_to_all x1, starting transfers between devices, body(): lax.all_to_all(result, 'azim', split_axis=0, concat_axis=0, tiled=True)  5.58 us
    pallas_call x1, Pallas kernels, body(): pl.pallas_call(heat_kernel, out_shape=pltpu.VMEM((NA, 16, 128), F32), in_...  4.6 us
    ppermute x1, waiting for transfers between devices, body(): heat_prev = lax.ppermute(heat_up, chain, onward)  3.85 us
  transfers between devices with their start and end apart: 11, of which 7 were waited for; matrix products, arithmetic and copies ran while one was open for 0% of the time, Pallas kernels for 6%

profile of v4, /device:TPU:8, one launch (start us, length us, event | category | flops | bytes accessed | tf_op | source)
XLA Modules:
  0.0 79.3 jit_solution(8737492510128859358)
XLA Ops:
  0.7 1.7 %send.1 = (f32[4,8,128]{2,1,0:T(8,128)S(1)}, f32[12,8,128]{2,1,0:T(8,128)S(1)}, f32[2,256,128]{2,1,0:T(8,128)S(1)}, f32[4,256,128]{2,1,0:T(8,128)S(1)}) custom-call(f32[3,1,256,128]{3,2,1,0:T(8,128)} %pot.3, s32[1,256,128]{2,1,0:T(8,128)} %fixed.3, s32[32,128]{1,0:T(8,128)} %spin.3, s32[1,128]{1,0:T(1,128)} %bitcast.1, f32[32,8,128]{2,1,0:T(8,128)} %prior.3, ...), custom_call_target="tpu_custom_call" | custom-call | tf_op jit(solution)/shard_map/send/pallas_call | solution.py:367
  2.4 0.0 copy-start
  2.4 2.3 %collective-permute-start = (f32[4,8,128]{2,1,0:T(8,128)S(1)}, f32[4,8,128]{2,1,0:T(8,128)S(1)}, u32[]{:S(2)}, u32[]{:S(2)}) collective-permute-start(f32[4,8,128]{2,1,0:T(8,128)S(1)} %get-tuple-element.21), channel_id=1, source_target_pairs={{0,128},{128,0},{1,129},{129,1},{2,130},{130,2},{3,131},{131,3},{4... | collective-permute-start | bytes 49160 | tf_op jit(solution)/shard_map/ppermute | solution.py:385
  4.6 1.7 %collective-permute-done.across = f32[4,8,128]{2,1,0:T(8,128)S(1)} collective-permute-done((f32[4,8,128]{2,1,0:T(8,128)S(1)}, f32[4,8,128]{2,1,0:T(8,128)S(1)}, u32[]{:S(2)}, u32[]{:S(2)}) %collective-permute-start) | collective-permute-done | bytes 16416 | tf_op jit(solution)/shard_map/ppermute | solution.py:385
  6.4 0.0 copy-start.5
  6.4 1.8 %collective-permute-start.5 = (f32[4,256,128]{2,1,0:T(8,128)S(1)}, f32[4,256,128]{2,1,0:T(8,128)S(1)}, u32[]{:S(2)}, u32[]{:S(2)}) collective-permute-start(f32[4,256,128]{2,1,0:T(8,128)S(1)} %get-tuple-element.27), channel_id=1, source_target_pairs={{0,4},{4,8},{8,12},{12,16},{16,20},{20,24},{24,28},{28,32},{32,36}... | collective-permute-start | bytes 1572872 | tf_op jit(solution)/shard_map/ppermute | solution.py:392
  8.2 6.2 %collective-permute-start.3 = (f32[2,256,128]{2,1,0:T(8,128)S(1)}, f32[2,256,128]{2,1,0:T(8,128)S(1)}, u32[]{:S(2)}, u32[]{:S(2)}) collective-permute-start(f32[2,256,128]{2,1,0:T(8,128)S(1)} %get-tuple-element.26), channel_id=1, source_target_pairs={{4,0},{8,4},{12,8},{16,12},{20,16},{24,20},{28,24},{32,28},{36,32}... | collective-permute-start | bytes 786440 | tf_op jit(solution)/shard_map/ppermute | solution.py:391
  14.4 0.7 collective-permute-start.2
  15.1 0.6 collective-permute-done.1.core
  15.8 2.0 %collective-permute-start.4 = (f32[16,8,128]{2,1,0:T(8,128)S(1)}, f32[16,8,128]{2,1,0:T(8,128)S(1)}, u32[]{:S(2)}, u32[]{:S(2)}) collective-permute-start(f32[16,8,128]{2,1,0:T(8,128)S(1)} %get-tuple-element.25.halo), channel_id=1, source_target_pairs={{4,0},{8,4},{12,8},{16,12},{20,16},{24,20},{28,24},{32,28},{36,32}... | collective-permute-start | bytes 196616 | tf_op jit(solution)/shard_map/ppermute | solution.py:403
  17.8 0.1 collective-permute-start.6
  17.9 2.2 %collective-permute-done.4.halo_after = f32[16,8,128]{2,1,0:T(8,128)S(1)} collective-permute-done((f32[16,8,128]{2,1,0:T(8,128)S(1)}, f32[16,8,128]{2,1,0:T(8,128)S(1)}, u32[]{:S(2)}, u32[]{:S(2)}) %collective-permute-start.4) | collective-permute-done | bytes 65568 | tf_op jit(solution)/shard_map/ppermute | solution.py:403
  20.2 2.2 %magnetic.1 = f32[32,40,128]{2,1,0:T(8,128)} custom-call(f32[3,1,256,128]{3,2,1,0:T(8,128)S(1)} %copy-done, s32[1,256,128]{2,1,0:T(8,128)S(1)} %copy-done.3, s32[32,128]{1,0:T(8,128)S(1)} %copy-done.5, s32[1,128]{1,0:T(1,128)S(1)} %bitcast.2, f32[16,8,128]{2,1,0:T(8,128)S(1)} %get-tuple-element.25.halo, f32[2,256,128]{2,1,0:T(8,128)S(1)} %collective-permute-done.3.ring, ...), custom_call_target="tpu_custom_call" | custom-call | tf_op jit(solution)/shard_map/magnetic/pallas_call | solution.py:405
  22.4 3.5 %collective-permute-done.6.halo_before = f32[16,8,128]{2,1,0:T(8,128)S(1)} collective-permute-done((f32[16,8,128]{2,1,0:T(8,128)S(1)}, f32[16,8,128]{2,1,0:T(8,128)S(1)}, u32[]{:S(2)}, u32[]{:S(2)}) %collective-permute-start.6) | collective-permute-done | bytes 65568 | tf_op jit(solution)/shard_map/ppermute | solution.py:418
  25.8 6.2 %all-to-all-start = ((f32[32,40,128]{2,1,0:T(8,128)}), f32[32,40,128]{2,1,0:T(8,128)S(1)}, u32[]{:S(2)}, u32[]{:S(2)}) async-start(f32[32,40,128]{2,1,0:T(8,128)} %magnetic.1), calls=%async_computation | async-start | bytes 1310720 | tf_op jit(solution)/shard_map/all_to_all | solution.py:420
  32.1 7.1 %collective-permute-start.7 = (f32[36,8,128]{2,1,0:T(8,128)S(1)}, f32[36,8,128]{2,1,0:T(8,128)S(1)}, u32[]{:S(2)}, u32[]{:S(2)}) collective-permute-start(f32[36,8,128]{2,1,0:T(8,128)S(1)} %get-tuple-element.32.sides), channel_id=1, source_target_pairs={{4,0},{8,4},{12,8},{16,12},{20,16},{24,20},{28,24},{32,28},{36,32}... | collective-permute-start | bytes 442376 | tf_op jit(solution)/shard_map/ppermute | solution.py:422
  39.2 1.9 %collective-permute-start.8 = (f32[36,8,128]{2,1,0:T(8,128)S(1)}, f32[36,8,128]{2,1,0:T(8,128)S(1)}, u32[]{:S(2)}, u32[]{:S(2)}) collective-permute-start(f32[36,8,128]{2,1,0:T(8,128)S(1)} %get-tuple-element.33), channel_id=1, source_target_pairs={{0,4},{4,8},{8,12},{12,16},{16,20},{20,24},{24,28},{28,32},{32,36}... | collective-permute-start | bytes 442376 | tf_op jit(solution)/shard_map/ppermute | solution.py:421
  41.2 10.5 %collective-permute-done.7.from_next = f32[36,8,128]{2,1,0:T(8,128)S(1)} collective-permute-done((f32[36,8,128]{2,1,0:T(8,128)S(1)}, f32[36,8,128]{2,1,0:T(8,128)S(1)}, u32[]{:S(2)}, u32[]{:S(2)}) %collective-permute-start.7) | collective-permute-done | bytes 147488 | tf_op jit(solution)/shard_map/ppermute | solution.py:422
  51.7 3.9 %collective-permute-done.8.from_prev = f32[36,8,128]{2,1,0:T(8,128)S(1)} collective-permute-done((f32[36,8,128]{2,1,0:T(8,128)S(1)}, f32[36,8,128]{2,1,0:T(8,128)S(1)}, u32[]{:S(2)}, u32[]{:S(2)}) %collective-permute-start.8) | collective-permute-done | bytes 147488 | tf_op jit(solution)/shard_map/ppermute | solution.py:421
  55.5 4.6 %heat.1 = f32[32,16,128]{2,1,0:T(8,128)} custom-call(f32[32,40,128]{2,1,0:T(8,128)S(1)} %all-to-all-done.got, f32[32,8,128]{2,1,0:T(8,128)S(1)} %copy-done.1, f32[32,8,128]{2,1,0:T(8,128)S(1)} %copy-done.2, f32[36,8,128]{2,1,0:T(8,128)S(1)} %collective-permute-done.7.from_next, f32[36,8,128]{2,1,0:T(8,128)S(1)} %collective-permute-done.8.from_prev, ...), custom_call_target="tpu_custom_call" | custom-call | flops 20000000 | bytes 20000000 | tf_op jit(solution)/shard_map/heat/pallas_call | solution.py:441
  60.1 5.6 %all-to-all-start.1 = ((f32[32,16,128]{2,1,0:T(8,128)}), f32[32,16,128]{2,1,0:T(8,128)S(1)}, u32[]{:S(2)}, u32[]{:S(2)}) async-start(f32[32,16,128]{2,1,0:T(8,128)} %heat.1), calls=%async_computation.1 | async-start | bytes 524288 | tf_op jit(solution)/shard_map/all_to_all | solution.py:459
  65.8 2.3 %curl.1 = (f32[3,1,256,128]{3,2,1,0:T(8,128)}, f32[3,256,128]{2,1,0:T(8,128)S(1)}) custom-call(f32[3,1,256,128]{3,2,1,0:T(8,128)S(1)} %copy-done, s32[1,256,128]{2,1,0:T(8,128)S(1)} %copy-done.3, s32[32,128]{1,0:T(8,128)S(1)} %copy-done.5, s32[1,128]{1,0:T(1,128)S(1)} %bitcast.3, f32[16,8,128]{2,1,0:T(8,128)S(1)} %get-tuple-element.25.halo, ...), custom_call_target="tpu_custom_call" | custom-call | flops 10000000 | bytes 10000000 | tf_op jit(solution)/shard_map/curl/pallas_call | solution.py:423
  68.0 10.4 %all-to-all-done.1.got = f32[32,16,128]{2,1,0:T(8,128)S(1)} async-done(((f32[32,16,128]{2,1,0:T(8,128)}), f32[32,16,128]{2,1,0:T(8,128)S(1)}, u32[]{:S(2)}, u32[]{:S(2)}) %all-to-all-start.1) | async-done | bytes 262176 | tf_op jit(solution)/shard_map/all_to_all | solution.py:459
  78.4 0.8 %finish.1 = (f32[3,1,256,128]{3,2,1,0:T(8,128)}, f32[1,256,128]{2,1,0:T(8,128)}) custom-call(f32[32,16,128]{2,1,0:T(8,128)S(1)} %all-to-all-done.1.got, f32[3,256,128]{2,1,0:T(8,128)S(1)} %get-tuple-element.34.weight), custom_call_target="tpu_custom_call" | custom-call | tf_op jit(solution)/shard_map/finish/pallas_call | solution.py:460
  (31 shorter events, 0.1 us)
Async XLA Ops:
  0.6 15.1 %copy-start.1 = (f32[32,8,128]{2,1,0:T(8,128)S(1)}, f32[32,8,128]{2,1,0:T(8,128)}, u32[]{:S(2)}) copy-start(f32[32,8,128]{2,1,0:T(8,128)} %prior.3) | copy-start | bytes 393220
  0.6 15.1 %copy-start.2 = (f32[32,8,128]{2,1,0:T(8,128)S(1)}, f32[32,8,128]{2,1,0:T(8,128)}, u32[]{:S(2)}) copy-start(f32[32,8,128]{2,1,0:T(8,128)} %goal.3) | copy-start | bytes 393220
  2.4 17.8 %copy-start = (f32[3,1,256,128]{3,2,1,0:T(8,128)S(1)}, f32[3,1,256,128]{3,2,1,0:T(8,128)}, u32[]{:S(2)}) copy-start(f32[3,1,256,128]{3,2,1,0:T(8,128)} %pot.3) | copy-start | bytes 1179652
  2.4 4.0 %collective-permute-start = (f32[4,8,128]{2,1,0:T(8,128)S(1)}, f32[4,8,128]{2,1,0:T(8,128)S(1)}, u32[]{:S(2)}, u32[]{:S(2)}) collective-permute-start(f32[4,8,128]{2,1,0:T(8,128)S(1)} %get-tuple-element.21), channel_id=1, source_target_pairs={{0,128},{128,0},{1,129},{129,1},{2,130},{130,2},{3,131},{131,3},{4... | collective-permute-start | bytes 49160 | tf_op jit(solution)/shard_map/ppermute | solution.py:385
  6.4 13.8 %copy-start.3 = (s32[1,256,128]{2,1,0:T(8,128)S(1)}, s32[1,256,128]{2,1,0:T(8,128)}, u32[]{:S(2)}) copy-start(s32[1,256,128]{2,1,0:T(8,128)} %fixed.3) | copy-start | bytes 393220
  6.4 13.8 %copy-start.5 = (s32[32,128]{1,0:T(8,128)S(1)}, s32[32,128]{1,0:T(8,128)}, u32[]{:S(2)}) copy-start(s32[32,128]{1,0:T(8,128)} %spin.3) | copy-start | bytes 49156
  6.4 19.4 %collective-permute-start.5 = (f32[4,256,128]{2,1,0:T(8,128)S(1)}, f32[4,256,128]{2,1,0:T(8,128)S(1)}, u32[]{:S(2)}, u32[]{:S(2)}) collective-permute-start(f32[4,256,128]{2,1,0:T(8,128)S(1)} %get-tuple-element.27), channel_id=1, source_target_pairs={{0,4},{4,8},{8,12},{12,16},{16,20},{20,24},{24,28},{28,32},{32,36}... | collective-permute-start | bytes 1572872 | tf_op jit(solution)/shard_map/ppermute | solution.py:392
  8.2 11.9 %collective-permute-start.3 = (f32[2,256,128]{2,1,0:T(8,128)S(1)}, f32[2,256,128]{2,1,0:T(8,128)S(1)}, u32[]{:S(2)}, u32[]{:S(2)}) collective-permute-start(f32[2,256,128]{2,1,0:T(8,128)S(1)} %get-tuple-element.26), channel_id=1, source_target_pairs={{4,0},{8,4},{12,8},{16,12},{20,16},{24,20},{28,24},{32,28},{36,32}... | collective-permute-start | bytes 786440 | tf_op jit(solution)/shard_map/ppermute | solution.py:391
  14.4 1.3 %collective-permute-start.1 = (f32[16,8,128]{2,1,0:T(8,128)S(1)}, f32[16,8,128]{2,1,0:T(8,128)S(1)}, u32[]{:S(2)}, u32[]{:S(2)}) collective-permute-start(f32[16,8,128]{2,1,0:T(8,128)S(1)} %frame.1.own), channel_id=1, source_target_pairs={{0,1},{1,0},{2,3},{3,2},{4,5},{5,4},{6,7},{7,6},{8,9},{9,8},{10,11... | collective-permute-start | bytes 196616 | tf_op jit(solution)/shard_map/ppermute | solution.py:393
  14.4 1.3 %collective-permute-start.2 = (f32[16,8,128]{2,1,0:T(8,128)S(1)}, f32[16,8,128]{2,1,0:T(8,128)S(1)}, u32[]{:S(2)}, u32[]{:S(2)}) collective-permute-start(f32[16,8,128]{2,1,0:T(8,128)S(1)} %frame.1.own), channel_id=1, source_target_pairs={{1,2},{2,1},{5,6},{6,5},{9,10},{10,9},{13,14},{14,13},{17,18},{18,... | collective-permute-start | bytes 196616 | tf_op jit(solution)/shard_map/ppermute | solution.py:394
  15.8 4.4 %copy-start.6 = (s32[128]{0:T(128)S(1)}, s32[128]{0:T(128)}, u32[]{:S(2)}) copy-start(s32[128]{0:T(128)} %param.17) | copy-start | bytes 1540
  15.8 4.4 %copy-start.7 = (f32[8]{0:T(128)S(1)}, f32[8]{0:T(128)}, u32[]{:S(2)}) copy-start(f32[8]{0:T(128)} %loss.3) | copy-start | bytes 100
  15.8 4.3 %collective-permute-start.4 = (f32[16,8,128]{2,1,0:T(8,128)S(1)}, f32[16,8,128]{2,1,0:T(8,128)S(1)}, u32[]{:S(2)}, u32[]{:S(2)}) collective-permute-start(f32[16,8,128]{2,1,0:T(8,128)S(1)} %get-tuple-element.25.halo), channel_id=1, source_target_pairs={{4,0},{8,4},{12,8},{16,12},{20,16},{24,20},{28,24},{32,28},{36,32}... | collective-permute-start | bytes 196616 | tf_op jit(solution)/shard_map/ppermute | solution.py:403
  17.8 8.0 %collective-permute-start.6 = (f32[16,8,128]{2,1,0:T(8,128)S(1)}, f32[16,8,128]{2,1,0:T(8,128)S(1)}, u32[]{:S(2)}, u32[]{:S(2)}) collective-permute-start(f32[16,8,128]{2,1,0:T(8,128)S(1)} %get-tuple-element.25.halo), channel_id=1, source_target_pairs={{0,4},{4,8},{8,12},{12,16},{16,20},{20,24},{24,28},{28,32},{32,36}... | collective-permute-start | bytes 196616 | tf_op jit(solution)/shard_map/ppermute | solution.py:418
  25.8 29.7 %all-to-all-start = ((f32[32,40,128]{2,1,0:T(8,128)}), f32[32,40,128]{2,1,0:T(8,128)S(1)}, u32[]{:S(2)}, u32[]{:S(2)}) async-start(f32[32,40,128]{2,1,0:T(8,128)} %magnetic.1), calls=%async_computation | async-start | bytes 1310720 | tf_op jit(solution)/shard_map/all_to_all | solution.py:420
  32.1 23.5 %copy-start.8 = (f32[8]{0:T(128)S(1)}, f32[8]{0:T(128)}, u32[]{:S(2)}) copy-start(f32[8]{0:T(128)} %plane.1) | copy-start | bytes 100
  32.1 23.4 %copy-start.9 = (f32[8]{0:T(128)S(1)}, f32[8]{0:T(128)}, u32[]{:S(2)}) copy-start(f32[8]{0:T(128)} %axial.1) | copy-start | bytes 100
  32.1 23.4 %copy-start.10 = (f32[8]{0:T(128)S(1)}, f32[8]{0:T(128)}, u32[]{:S(2)}) copy-start(f32[8]{0:T(128)} %storage.1) | copy-start | bytes 100
  32.1 19.6 %collective-permute-start.7 = (f32[36,8,128]{2,1,0:T(8,128)S(1)}, f32[36,8,128]{2,1,0:T(8,128)S(1)}, u32[]{:S(2)}, u32[]{:S(2)}) collective-permute-start(f32[36,8,128]{2,1,0:T(8,128)S(1)} %get-tuple-element.32.sides), channel_id=1, source_target_pairs={{4,0},{8,4},{12,8},{16,12},{20,16},{24,20},{28,24},{32,28},{36,32}... | collective-permute-start | bytes 442376 | tf_op jit(solution)/shard_map/ppermute | solution.py:422
  39.2 16.3 %collective-permute-start.8 = (f32[36,8,128]{2,1,0:T(8,128)S(1)}, f32[36,8,128]{2,1,0:T(8,128)S(1)}, u32[]{:S(2)}, u32[]{:S(2)}) collective-permute-start(f32[36,8,128]{2,1,0:T(8,128)S(1)} %get-tuple-element.33), channel_id=1, source_target_pairs={{0,4},{4,8},{8,12},{12,16},{16,20},{20,24},{24,28},{28,32},{32,36}... | collective-permute-start | bytes 442376 | tf_op jit(solution)/shard_map/ppermute | solution.py:421
  60.1 5.6 %copy-start.4 = (f32[3,1,256,128]{3,2,1,0:T(8,128)S(1)}, f32[3,1,256,128]{3,2,1,0:T(8,128)}, u32[]{:S(2)}) copy-start(f32[3,1,256,128]{3,2,1,0:T(8,128)} %current.1) | copy-start | bytes 1179652
  60.1 5.6 %copy-start.11 = (f32[8]{0:T(128)S(1)}, f32[8]{0:T(128)}, u32[]{:S(2)}) copy-start(f32[8]{0:T(128)} %reluct.1) | copy-start | bytes 100
  60.1 5.6 %copy-start.12 = (f32[8]{0:T(128)S(1)}, f32[8]{0:T(128)}, u32[]{:S(2)}) copy-start(f32[8]{0:T(128)} %eddy.1) | copy-start | bytes 100
  60.1 18.3 %all-to-all-start.1 = ((f32[32,16,128]{2,1,0:T(8,128)}), f32[32,16,128]{2,1,0:T(8,128)S(1)}, u32[]{:S(2)}, u32[]{:S(2)}) async-start(f32[32,16,128]{2,1,0:T(8,128)} %heat.1), calls=%async_computation.1 | async-start | bytes 524288 | tf_op jit(solution)/shard_map/all_to_all | solution.py:459

commit v5 on v4

--- a/solution.py
+++ b/solution.py
@@ -437,6 +437,7 @@
         *block, planes, halo_before, imposed_current_density,
         inverse_permeability, electric_conductance, core_dissipation_coefficient,
     )
+    got, misfit, weight = lax.optimization_barrier((got, misfit, weight))
     wide = pltpu.VMEM((NA, 16, 256), F32)
     result = pl.pallas_call(
         heat_kernel,

time: 79.6 us -> 78.7 us (0.989)
  the two profiles are of different devices: /device:TPU:8 before, /device:TPU:1 now
where the time goes in v5:
time: 78.7 us; the launch traced here: 77.1 us
  starting transfers between devices  28.8 us (37%)
  waiting for transfers between devices  19.4 us (25%)
  blocking collectives  15.5 us (20%)
  Pallas kernels  12 us (15%)
  between operations  0.79 us (1%)
    all_to_all x1, blocking collectives, body(): lax.all_to_all(result, 'azim', split_axis=0, concat_axis=0, tiled=True)  15.5 us
    all_to_all x1, waiting for transfers between devices, body(): lax.all_to_all(payload, 'azim', split_axis=0, concat_axis=0, tiled=True)  11.4 us
    ppermute x1, starting transfers between devices, body(): ring = lax.ppermute(ring, 'azim', from_after)  6.22 us
    ppermute x1, starting transfers between devices, body(): far = lax.ppermute(frame, 'axial', [(1, 2), (2, 1)])  4.7 us
    ppermute x1, starting transfers between devices, body(): heat_prev = lax.ppermute(heat_up, chain, onward)  4.66 us
    pallas_call x1, Pallas kernels, body(): pl.pallas_call(heat_kernel, out_shape=pltpu.VMEM((NA, 16, 128), F32), in_...  4.25 us
    all_to_all x1, starting transfers between devices, body(): lax.all_to_all(payload, 'azim', split_axis=0, concat_axis=0, tiled=True)  4.07 us
    ppermute x1, waiting for transfers between devices, body(): halo_before = lax.ppermute(halo, 'azim', from_before)  2.72 us
  transfers between devices with their start and end apart: 10, of which 5 were waited for; matrix products, arithmetic and copies ran while one was open for 0% of the time, Pallas kernels for 7%

profile of v5, /device:TPU:1, one launch (start us, length us, event | category | flops | bytes accessed | tf_op | source)
XLA Modules:
  0.0 77.1 jit_solution(15607293904828179671)
XLA Ops:
  0.7 1.7 %send.1 = (f32[4,8,128]{2,1,0:T(8,128)S(1)}, f32[12,8,128]{2,1,0:T(8,128)S(1)}, f32[2,256,128]{2,1,0:T(8,128)S(1)}, f32[4,256,128]{2,1,0:T(8,128)S(1)}) custom-call(f32[3,1,256,128]{3,2,1,0:T(8,128)} %pot.3, s32[1,256,128]{2,1,0:T(8,128)} %fixed.3, s32[32,128]{1,0:T(8,128)} %spin.3, s32[1,128]{1,0:T(1,128)} %bitcast.1, f32[32,8,128]{2,1,0:T(8,128)} %prior.3, ...), custom_call_target="tpu_custom_call" | custom-call | tf_op jit(solution)/shard_map/send/pallas_call | solution.py:367
  2.4 2.2 %collective-permute-start = (f32[4,8,128]{2,1,0:T(8,128)S(1)}, f32[4,8,128]{2,1,0:T(8,128)S(1)}, u32[]{:S(2)}, u32[]{:S(2)}) collective-permute-start(f32[4,8,128]{2,1,0:T(8,128)S(1)} %get-tuple-element.24), channel_id=1, source_target_pairs={{0,128},{128,0},{1,129},{129,1},{2,130},{130,2},{3,131},{131,3},{4... | collective-permute-start | bytes 49160 | tf_op jit(solution)/shard_map/ppermute | solution.py:385
  4.6 1.1 %collective-permute-done.across = f32[4,8,128]{2,1,0:T(8,128)S(1)} collective-permute-done((f32[4,8,128]{2,1,0:T(8,128)S(1)}, f32[4,8,128]{2,1,0:T(8,128)S(1)}, u32[]{:S(2)}, u32[]{:S(2)}) %collective-permute-start) | collective-permute-done | bytes 16416 | tf_op jit(solution)/shard_map/ppermute | solution.py:385
  5.7 1.9 %collective-permute-start.5 = (f32[4,256,128]{2,1,0:T(8,128)S(1)}, f32[4,256,128]{2,1,0:T(8,128)S(1)}, u32[]{:S(2)}, u32[]{:S(2)}) collective-permute-start(f32[4,256,128]{2,1,0:T(8,128)S(1)} %get-tuple-element.30), channel_id=1, source_target_pairs={{0,4},{4,8},{8,12},{12,16},{16,20},{20,24},{24,28},{28,32},{32,36}... | collective-permute-start | bytes 1572872 | tf_op jit(solution)/shard_map/ppermute | solution.py:392
  7.6 6.2 %collective-permute-start.3 = (f32[2,256,128]{2,1,0:T(8,128)S(1)}, f32[2,256,128]{2,1,0:T(8,128)S(1)}, u32[]{:S(2)}, u32[]{:S(2)}) collective-permute-start(f32[2,256,128]{2,1,0:T(8,128)S(1)} %get-tuple-element.29), channel_id=1, source_target_pairs={{4,0},{8,4},{12,8},{16,12},{20,16},{24,20},{28,24},{32,28},{36,32}... | collective-permute-start | bytes 786440 | tf_op jit(solution)/shard_map/ppermute | solution.py:391
  13.8 2.1 %collective-permute-start.1 = (f32[16,8,128]{2,1,0:T(8,128)S(1)}, f32[16,8,128]{2,1,0:T(8,128)S(1)}, u32[]{:S(2)}, u32[]{:S(2)}) collective-permute-start(f32[16,8,128]{2,1,0:T(8,128)S(1)} %frame.1.own), channel_id=1, source_target_pairs={{0,1},{1,0},{2,3},{3,2},{4,5},{5,4},{6,7},{7,6},{8,9},{9,8},{10,11... | collective-permute-start | bytes 196616 | tf_op jit(solution)/shard_map/ppermute | solution.py:393
  15.9 4.7 %collective-permute-start.2 = (f32[16,8,128]{2,1,0:T(8,128)S(1)}, f32[16,8,128]{2,1,0:T(8,128)S(1)}, u32[]{:S(2)}, u32[]{:S(2)}) collective-permute-start(f32[16,8,128]{2,1,0:T(8,128)S(1)} %frame.1.own), channel_id=1, source_target_pairs={{1,2},{2,1},{5,6},{6,5},{9,10},{10,9},{13,14},{14,13},{17,18},{18,... | collective-permute-start | bytes 196616 | tf_op jit(solution)/shard_map/ppermute | solution.py:394
  20.7 2.7 %collective-permute-done.2.far = f32[16,8,128]{2,1,0:T(8,128)S(1)} collective-permute-done((f32[16,8,128]{2,1,0:T(8,128)S(1)}, f32[16,8,128]{2,1,0:T(8,128)S(1)}, u32[]{:S(2)}, u32[]{:S(2)}) %collective-permute-start.2) | collective-permute-done | bytes 65568 | tf_op jit(solution)/shard_map/ppermute | solution.py:394
  23.3 0.7 halo.1
  24.0 1.7 %collective-permute-start.4 = (f32[16,8,128]{2,1,0:T(8,128)S(1)}, f32[16,8,128]{2,1,0:T(8,128)S(1)}, u32[]{:S(2)}, u32[]{:S(2)}) collective-permute-start(f32[16,8,128]{2,1,0:T(8,128)S(1)} %get-tuple-element.28.halo), channel_id=1, source_target_pairs={{4,0},{8,4},{12,8},{16,12},{20,16},{24,20},{28,24},{32,28},{36,32}... | collective-permute-start | bytes 196616 | tf_op jit(solution)/shard_map/ppermute | solution.py:403
  25.7 1.5 %collective-permute-done.4.halo_after = f32[16,8,128]{2,1,0:T(8,128)S(1)} collective-permute-done((f32[16,8,128]{2,1,0:T(8,128)S(1)}, f32[16,8,128]{2,1,0:T(8,128)S(1)}, u32[]{:S(2)}, u32[]{:S(2)}) %collective-permute-start.4) | collective-permute-done | bytes 65568 | tf_op jit(solution)/shard_map/ppermute | solution.py:403
  27.2 2.2 %magnetic.1 = f32[32,40,128]{2,1,0:T(8,128)} custom-call(f32[3,1,256,128]{3,2,1,0:T(8,128)S(1)} %copy-done, s32[1,256,128]{2,1,0:T(8,128)S(1)} %copy-done.1, s32[32,128]{1,0:T(8,128)S(1)} %copy-done.5, s32[1,128]{1,0:T(1,128)S(1)} %bitcast.2, f32[16,8,128]{2,1,0:T(8,128)S(1)} %get-tuple-element.28.halo, f32[2,256,128]{2,1,0:T(8,128)S(1)} %collective-permute-done.3.ring, ...), custom_call_target="tpu_custom_call" | custom-call | tf_op jit(solution)/shard_map/magnetic/pallas_call | solution.py:405
  29.4 2.7 %collective-permute-done.6.halo_before = f32[16,8,128]{2,1,0:T(8,128)S(1)} collective-permute-done((f32[16,8,128]{2,1,0:T(8,128)S(1)}, f32[16,8,128]{2,1,0:T(8,128)S(1)}, u32[]{:S(2)}, u32[]{:S(2)}) %collective-permute-start.6) | collective-permute-done | bytes 65568 | tf_op jit(solution)/shard_map/ppermute | solution.py:418
  32.1 4.1 %all-to-all-start = ((f32[32,40,128]{2,1,0:T(8,128)}), f32[32,40,128]{2,1,0:T(8,128)S(1)}, u32[]{:S(2)}, u32[]{:S(2)}) async-start(f32[32,40,128]{2,1,0:T(8,128)} %magnetic.1), calls=%async_computation | async-start | bytes 1310720 | tf_op jit(solution)/shard_map/all_to_all | solution.py:420
  36.2 1.3 %collective-permute-start.7 = (f32[36,8,128]{2,1,0:T(8,128)S(1)}, f32[36,8,128]{2,1,0:T(8,128)S(1)}, u32[]{:S(2)}, u32[]{:S(2)}) collective-permute-start(f32[36,8,128]{2,1,0:T(8,128)S(1)} %get-tuple-element.38.sides), channel_id=1, source_target_pairs={{4,0},{8,4},{12,8},{16,12},{20,16},{24,20},{28,24},{32,28},{36,32}... | collective-permute-start | bytes 442376 | tf_op jit(solution)/shard_map/ppermute | solution.py:422
  37.5 4.7 %collective-permute-start.8 = (f32[36,8,128]{2,1,0:T(8,128)}, f32[36,8,128]{2,1,0:T(8,128)}, u32[]{:S(2)}, u32[]{:S(2)}) collective-permute-start(f32[36,8,128]{2,1,0:T(8,128)} %get-tuple-element.39), channel_id=1, source_target_pairs={{0,4},{4,8},{8,12},{12,16},{16,20},{20,24},{24,28},{28,32},{32,36}... | collective-permute-start | bytes 442376 | tf_op jit(solution)/shard_map/ppermute | solution.py:421
  42.2 2.3 %curl.1 = (f32[3,1,256,128]{3,2,1,0:T(8,128)}, f32[3,256,128]{2,1,0:T(8,128)S(1)}) custom-call(f32[3,1,256,128]{3,2,1,0:T(8,128)S(1)} %copy-done, s32[1,256,128]{2,1,0:T(8,128)S(1)} %copy-done.1, s32[32,128]{1,0:T(8,128)S(1)} %copy-done.5, s32[1,128]{1,0:T(1,128)S(1)} %bitcast.3, f32[16,8,128]{2,1,0:T(8,128)S(1)} %get-tuple-element.28.halo, ...), custom_call_target="tpu_custom_call" | custom-call | flops 10000000 | bytes 10000000 | tf_op jit(solution)/shard_map/curl/pallas_call | solution.py:423
  44.5 11.4 %all-to-all-done.got = f32[32,40,128]{2,1,0:T(8,128)S(1)} async-done(((f32[32,40,128]{2,1,0:T(8,128)}), f32[32,40,128]{2,1,0:T(8,128)S(1)}, u32[]{:S(2)}, u32[]{:S(2)}) %all-to-all-start) | async-done | bytes 655392 | tf_op jit(solution)/shard_map/all_to_all | solution.py:420
  55.9 0.6 copy-done.10
  56.6 0.0 copy-done.11
  56.6 0.0 copy-done.12
  56.6 4.3 %heat.1 = f32[32,16,128]{2,1,0:T(8,128)S(1)} custom-call(f32[32,40,128]{2,1,0:T(8,128)S(1)} %all-to-all-done.got, f32[32,8,128]{2,1,0:T(8,128)S(1)} %copy-done.2, f32[32,8,128]{2,1,0:T(8,128)S(1)} %copy-done.3, f32[36,8,128]{2,1,0:T(8,128)S(1)} %collective-permute-done.7.from_next, f32[36,8,128]{2,1,0:T(8,128)} %collective-permute-done.8.from_prev, ...), custom_call_target="tpu_custom_call" | custom-call | flops 20000000 | bytes 20000000 | tf_op jit(solution)/shard_map/heat/pallas_call | solution.py:442
  60.9 15.5 %all_to_all.10.got = f32[32,16,128]{2,1,0:T(8,128)S(1)} all-to-all(f32[32,16,128]{2,1,0:T(8,128)S(1)} %heat.1), channel_id=1, replica_groups=mesh['section'=2,'azim'=32,'axial'=4] {'azim'}, dimensions={0} | all-to-all | bytes 524288 | tf_op jit(solution)/shard_map/all_to_all | solution.py:460
  76.3 0.8 %finish.1 = (f32[3,1,256,128]{3,2,1,0:T(8,128)}, f32[1,256,128]{2,1,0:T(8,128)}) custom-call(f32[32,16,128]{2,1,0:T(8,128)S(1)} %all_to_all.10.got, f32[3,256,128]{2,1,0:T(8,128)S(1)} %get-tuple-element.40.weight), custom_call_target="tpu_custom_call" | custom-call | tf_op jit(solution)/shard_map/finish/pallas_call | solution.py:461
  (30 shorter events, 0.1 us)
Async XLA Ops:
  0.6 22.7 %copy-start.2 = (f32[32,8,128]{2,1,0:T(8,128)S(1)}, f32[32,8,128]{2,1,0:T(8,128)}, u32[]{:S(2)}) copy-start(f32[32,8,128]{2,1,0:T(8,128)} %prior.3) | copy-start | bytes 393220
  0.6 22.7 %copy-start.3 = (f32[32,8,128]{2,1,0:T(8,128)S(1)}, f32[32,8,128]{2,1,0:T(8,128)}, u32[]{:S(2)}) copy-start(f32[32,8,128]{2,1,0:T(8,128)} %goal.3) | copy-start | bytes 393220
  2.4 24.8 %copy-start = (f32[3,1,256,128]{3,2,1,0:T(8,128)S(1)}, f32[3,1,256,128]{3,2,1,0:T(8,128)}, u32[]{:S(2)}) copy-start(f32[3,1,256,128]{3,2,1,0:T(8,128)} %pot.3) | copy-start | bytes 1179652
  2.4 3.3 %collective-permute-start = (f32[4,8,128]{2,1,0:T(8,128)S(1)}, f32[4,8,128]{2,1,0:T(8,128)S(1)}, u32[]{:S(2)}, u32[]{:S(2)}) collective-permute-start(f32[4,8,128]{2,1,0:T(8,128)S(1)} %get-tuple-element.24), channel_id=1, source_target_pairs={{0,128},{128,0},{1,129},{129,1},{2,130},{130,2},{3,131},{131,3},{4... | collective-permute-start | bytes 49160 | tf_op jit(solution)/shard_map/ppermute | solution.py:385
  5.7 21.4 %copy-start.1 = (s32[1,256,128]{2,1,0:T(8,128)S(1)}, s32[1,256,128]{2,1,0:T(8,128)}, u32[]{:S(2)}) copy-start(s32[1,256,128]{2,1,0:T(8,128)} %fixed.3) | copy-start | bytes 393220
  5.7 21.4 %copy-start.5 = (s32[32,128]{1,0:T(8,128)S(1)}, s32[32,128]{1,0:T(8,128)}, u32[]{:S(2)}) copy-start(s32[32,128]{1,0:T(8,128)} %spin.3) | copy-start | bytes 49156
  5.7 26.4 %collective-permute-start.5 = (f32[4,256,128]{2,1,0:T(8,128)S(1)}, f32[4,256,128]{2,1,0:T(8,128)S(1)}, u32[]{:S(2)}, u32[]{:S(2)}) collective-permute-start(f32[4,256,128]{2,1,0:T(8,128)S(1)} %get-tuple-element.30), channel_id=1, source_target_pairs={{0,4},{4,8},{8,12},{12,16},{16,20},{20,24},{24,28},{28,32},{32,36}... | collective-permute-start | bytes 1572872 | tf_op jit(solution)/shard_map/ppermute | solution.py:392
  7.6 19.5 %collective-permute-start.3 = (f32[2,256,128]{2,1,0:T(8,128)S(1)}, f32[2,256,128]{2,1,0:T(8,128)S(1)}, u32[]{:S(2)}, u32[]{:S(2)}) collective-permute-start(f32[2,256,128]{2,1,0:T(8,128)S(1)} %get-tuple-element.29), channel_id=1, source_target_pairs={{4,0},{8,4},{12,8},{16,12},{20,16},{24,20},{28,24},{32,28},{36,32}... | collective-permute-start | bytes 786440 | tf_op jit(solution)/shard_map/ppermute | solution.py:391
  13.8 6.8 %collective-permute-start.1 = (f32[16,8,128]{2,1,0:T(8,128)S(1)}, f32[16,8,128]{2,1,0:T(8,128)S(1)}, u32[]{:S(2)}, u32[]{:S(2)}) collective-permute-start(f32[16,8,128]{2,1,0:T(8,128)S(1)} %frame.1.own), channel_id=1, source_target_pairs={{0,1},{1,0},{2,3},{3,2},{4,5},{5,4},{6,7},{7,6},{8,9},{9,8},{10,11... | collective-permute-start | bytes 196616 | tf_op jit(solution)/shard_map/ppermute | solution.py:393
  15.9 7.4 %collective-permute-start.2 = (f32[16,8,128]{2,1,0:T(8,128)S(1)}, f32[16,8,128]{2,1,0:T(8,128)S(1)}, u32[]{:S(2)}, u32[]{:S(2)}) collective-permute-start(f32[16,8,128]{2,1,0:T(8,128)S(1)} %frame.1.own), channel_id=1, source_target_pairs={{1,2},{2,1},{5,6},{6,5},{9,10},{10,9},{13,14},{14,13},{17,18},{18,... | collective-permute-start | bytes 196616 | tf_op jit(solution)/shard_map/ppermute | solution.py:394
  24.0 3.1 %copy-start.6 = (s32[128]{0:T(128)S(1)}, s32[128]{0:T(128)}, u32[]{:S(2)}) copy-start(s32[128]{0:T(128)} %param.17) | copy-start | bytes 1540
  24.0 3.2 %copy-start.7 = (f32[8]{0:T(128)S(1)}, f32[8]{0:T(128)}, u32[]{:S(2)}) copy-start(f32[8]{0:T(128)} %loss.3) | copy-start | bytes 100
  24.0 3.1 %collective-permute-start.4 = (f32[16,8,128]{2,1,0:T(8,128)S(1)}, f32[16,8,128]{2,1,0:T(8,128)S(1)}, u32[]{:S(2)}, u32[]{:S(2)}) collective-permute-start(f32[16,8,128]{2,1,0:T(8,128)S(1)} %get-tuple-element.28.halo), channel_id=1, source_target_pairs={{4,0},{8,4},{12,8},{16,12},{20,16},{24,20},{28,24},{32,28},{36,32}... | collective-permute-start | bytes 196616 | tf_op jit(solution)/shard_map/ppermute | solution.py:403
  25.7 6.4 %collective-permute-start.6 = (f32[16,8,128]{2,1,0:T(8,128)S(1)}, f32[16,8,128]{2,1,0:T(8,128)S(1)}, u32[]{:S(2)}, u32[]{:S(2)}) collective-permute-start(f32[16,8,128]{2,1,0:T(8,128)S(1)} %get-tuple-element.28.halo), channel_id=1, source_target_pairs={{0,4},{4,8},{8,12},{12,16},{16,20},{20,24},{24,28},{28,32},{32,36}... | collective-permute-start | bytes 196616 | tf_op jit(solution)/shard_map/ppermute | solution.py:418
  29.4 12.8 %copy-start.4 = (f32[3,1,256,128]{3,2,1,0:T(8,128)S(1)}, f32[3,1,256,128]{3,2,1,0:T(8,128)}, u32[]{:S(2)}) copy-start(f32[3,1,256,128]{3,2,1,0:T(8,128)} %current.1) | copy-start | bytes 1179652
  32.1 23.8 %all-to-all-start = ((f32[32,40,128]{2,1,0:T(8,128)}), f32[32,40,128]{2,1,0:T(8,128)S(1)}, u32[]{:S(2)}, u32[]{:S(2)}) async-start(f32[32,40,128]{2,1,0:T(8,128)} %magnetic.1), calls=%async_computation | async-start | bytes 1310720 | tf_op jit(solution)/shard_map/all_to_all | solution.py:420
  36.2 6.0 %copy-start.8 = (f32[8]{0:T(128)S(1)}, f32[8]{0:T(128)}, u32[]{:S(2)}) copy-start(f32[8]{0:T(128)} %reluct.1) | copy-start | bytes 100
  36.2 6.0 %copy-start.9 = (f32[8]{0:T(128)S(1)}, f32[8]{0:T(128)}, u32[]{:S(2)}) copy-start(f32[8]{0:T(128)} %eddy.1) | copy-start | bytes 100
  36.2 19.7 %collective-permute-start.7 = (f32[36,8,128]{2,1,0:T(8,128)S(1)}, f32[36,8,128]{2,1,0:T(8,128)S(1)}, u32[]{:S(2)}, u32[]{:S(2)}) collective-permute-start(f32[36,8,128]{2,1,0:T(8,128)S(1)} %get-tuple-element.38.sides), channel_id=1, source_target_pairs={{4,0},{8,4},{12,8},{16,12},{20,16},{24,20},{28,24},{32,28},{36,32}... | collective-permute-start | bytes 442376 | tf_op jit(solution)/shard_map/ppermute | solution.py:422
  37.5 18.4 %collective-permute-start.8 = (f32[36,8,128]{2,1,0:T(8,128)}, f32[36,8,128]{2,1,0:T(8,128)}, u32[]{:S(2)}, u32[]{:S(2)}) collective-permute-start(f32[36,8,128]{2,1,0:T(8,128)} %get-tuple-element.39), channel_id=1, source_target_pairs={{0,4},{4,8},{8,12},{12,16},{16,20},{20,24},{24,28},{28,32},{32,36}... | collective-permute-start | bytes 442376 | tf_op jit(solution)/shard_map/ppermute | solution.py:421
  55.9 0.7 copy-start.10
  55.9 0.7 copy-start.11
  55.9 0.7 copy-start.12
